TPU v7x, 256 devices: a whole 4x4x8 slice. The times are simulated.
256 devices in a mesh: ta: 4 (over x), ha: 32 (over z, y_lo, core), ga: 2 (over y_hi).
Axes of the slice: x: 4, y: 4 (y_hi: 2, y_lo: 2; y = y_hi * 2 + y_lo), z: 8, core: 2. Of those that a mesh axis runs over, the one named last changes fastest.
Arguments:
- query_in: bfloat16 [12, 32, 8, 8, 512], P('ta', 'ha', None, None, 'ga'), may hold values from -6 to 6
- key_in: bfloat16 [12, 32, 8, 8, 512], P('ta', 'ha', None, None, 'ga'), may hold values from -6.0625 to 6.0625
- value_in: bfloat16 [12, 32, 8, 8, 512], P('ta', 'ha', None, None, 'ga'), may hold values from -6 to 6
- saved_out: bfloat16 [12, 32, 8, 8, 512], P('ta', 'ha', None, None, 'ga'), may hold values from -6 to 6
- out_grad: bfloat16 [12, 32, 8, 8, 512], P('ta', 'ha', None, None, 'ga'), may hold values from -6 to 6
- window_mask: int32 [2, 4, 8, 27], replicated, may hold values from 0 to 1, as said below
Outputs:
- query_grad: bfloat16 [12, 32, 8, 8, 512], P('ta', 'ha', None, None, 'ga')
- key_grad: bfloat16 [12, 32, 8, 8, 512], P('ta', 'ha', None, None, 'ga')
- value_grad: bfloat16 [12, 32, 8, 8, 512], P('ta', 'ha', None, None, 'ga')
Inputs may be any that keep to these rules, and one draw needn't show every extreme that they name: `window_mask`: entry 13 (the tile itself) is 1 for every tile.
All inputs are finite; a program needn't handle non-finite values.
Results may differ from a plain program's by a relative error of at most 0.0058.
Values may be sent and summed in bfloat16 or wider, within the bound.
No kernel may reach another device: no remote copies, remote signals or barrier semaphores. Data moves between devices by JAX's collectives and lax.ppermute only.
A program may use at most 128 MiB of HBM per device.

v0:
```python
import jax
import jax.numpy as jnp
from jax import lax
from jax.sharding import PartitionSpec as P

HEAD_DIM = 128
TILE_T = 6


def passed_along(block, axis, distance):
    devices = range(lax.axis_size(axis))
    route = [(i - distance, i) for i in devices if i - distance in devices]
    return lax.ppermute(block, axis, route)


def attend(query_rows, key_rows, value_rows, saved_rows, grad_rows, key_bias, score_scale):
    f32 = jnp.float32
    scores = (
        jnp.einsum("qhd,khd->hqk", query_rows, key_rows, preferred_element_type=f32) * score_scale
        + key_bias[None, None, :]
    )
    row_max = jnp.max(scores, axis=-1, keepdims=True)
    raised = jnp.exp(scores - row_max)
    weights = raised / jnp.sum(raised, axis=-1, keepdims=True)
    weights_low = weights.astype(jnp.bfloat16)
    value_part = jnp.einsum(
        "hqk,qhd->khd", weights_low, grad_rows, preferred_element_type=f32
    ).astype(jnp.bfloat16)
    weight_grad = jnp.einsum("qhd,khd->hqk", grad_rows, value_rows, preferred_element_type=f32)
    row_dot = jnp.einsum("qhd,qhd->hq", grad_rows, saved_rows, preferred_element_type=f32)
    score_grad = (weights * (weight_grad - row_dot[:, :, None]) * score_scale).astype(jnp.bfloat16)
    query_part = jnp.einsum(
        "hqk,khd->qhd", score_grad, key_rows, preferred_element_type=f32
    ).astype(jnp.bfloat16)
    key_part = jnp.einsum(
        "hqk,qhd->khd", score_grad, query_rows, preferred_element_type=f32
    ).astype(jnp.bfloat16)
    return (query_part, key_part, value_part)


def local(query_in, key_in, value_in, saved_out, out_grad, window_mask):
    f32 = jnp.float32
    frames_dev, plane_dev, tile_rows, tile_cols, local_width = query_in.shape
    heads_dev = local_width // HEAD_DIM
    row_tiles = window_mask.shape[1]
    col_tiles = window_mask.shape[2]
    frame_count = frames_dev * lax.axis_size("ta")
    time_index = lax.axis_index("ta")
    plane = lax.axis_index("ha")
    row_tile = plane // col_tiles
    col_tile = plane % col_tiles
    query_time = time_index * frames_dev // TILE_T
    score_scale = HEAD_DIM ** (-0.5)
    neighbours = [(row_move, col_move) for row_move in (-1, 0, 1) for col_move in (-1, 0, 1)]
    own_pair = (key_in[:, 0], value_in[:, 0])
    whole_frames = (
        lax.all_gather(own_pair[0], "ta", axis=0, tiled=True),
        lax.all_gather(own_pair[1], "ta", axis=0, tiled=True),
    )
    received = {(0, 0): whole_frames}
    for surround_row_move, surround_col_move in neighbours:
        if (surround_row_move, surround_col_move) != (0, 0):
            surround_offset = surround_row_move * col_tiles + surround_col_move
            received[surround_row_move, surround_col_move] = passed_along(
                (whole_frames[0], whole_frames[1]), "ha", -surround_offset
            )
    near_keys, near_values = tuple(
        (jnp.stack([received[place][member] for place in neighbours], 0) for member in range(2))
    )
    slot = jnp.arange(9, dtype=jnp.int32)
    row_step = slot // 3 - 1
    col_step = slot % 3 - 1
    time_step = jnp.arange(frame_count, dtype=jnp.int32) // TILE_T - query_time
    code = (time_step[None, :] + 1) * 9 + slot[:, None]
    window_row = (
        lax.dynamic_slice(window_mask, (query_time, row_tile, col_tile, 0), (1, 1, 1, 27))
        .reshape(27)
        .astype(f32)
    )
    matched = (code.reshape(-1)[:, None] == jnp.arange(27, dtype=jnp.int32)[None, :]).astype(f32)
    picked = jnp.dot(matched, window_row).reshape(9, frame_count)
    inside = (row_tile + row_step >= 0) & (row_tile + row_step < row_tiles)
    inside = inside & (col_tile + col_step >= 0) & (col_tile + col_step < col_tiles)
    slot_open = (picked > 0.5) & inside[:, None]
    slot_bias = jnp.where(slot_open, 0.0, -jnp.inf).astype(f32)
    key_bias = jnp.broadcast_to(
        slot_bias[:, :, None, None], (9, frame_count, tile_rows, tile_cols)
    ).reshape(-1)
    query_rows = query_in.reshape(-1, heads_dev, HEAD_DIM)
    saved_rows = saved_out.reshape(-1, heads_dev, HEAD_DIM)
    grad_rows = out_grad.reshape(-1, heads_dev, HEAD_DIM)
    key_rows = near_keys.reshape(-1, heads_dev, HEAD_DIM)
    value_rows = near_values.reshape(-1, heads_dev, HEAD_DIM)
    query_part, key_part, value_part = attend(
        query_rows, key_rows, value_rows, saved_rows, grad_rows, key_bias, score_scale
    )
    query_grad = query_part.reshape(frames_dev, 1, tile_rows, tile_cols, local_width)
    part_shape = (9, frame_count, tile_rows, tile_cols, local_width)
    key_block = key_part.reshape(part_shape)
    value_block = value_part.reshape(part_shape)
    key_sum = key_block[4].astype(f32)
    value_sum = value_block[4].astype(f32)
    for place_index, (row_move, col_move) in enumerate(neighbours):
        if (row_move, col_move) != (0, 0):
            offset = row_move * col_tiles + col_move
            returned = passed_along(
                (key_block[place_index], value_block[place_index]), "ha", offset
            )
            key_sum = key_sum + returned[0].astype(f32)
            value_sum = value_sum + returned[1].astype(f32)
    key_total, value_total = (
        lax.psum_scatter(key_sum, "ta", scatter_dimension=0, tiled=True),
        lax.psum_scatter(value_sum, "ta", scatter_dimension=0, tiled=True),
    )
    return (
        query_grad,
        key_total.astype(jnp.bfloat16)[:, None],
        value_total.astype(jnp.bfloat16)[:, None],
    )


def solution(mesh):
    return jax.shard_map(
        local,
        mesh=mesh,
        in_specs=(
            P("ta", "ha", None, None, "ga"),
            P("ta", "ha", None, None, "ga"),
            P("ta", "ha", None, None, "ga"),
            P("ta", "ha", None, None, "ga"),
            P("ta", "ha", None, None, "ga"),
            P(),
        ),
        out_specs=(
            P("ta", "ha", None, None, "ga"),
            P("ta", "ha", None, None, "ga"),
            P("ta", "ha", None, None, "ga"),
        ),
        check_vma=False,
    )
```

profile of v0, /device:TPU:65, one launch (start us, length us, event | category | flops | bytes accessed | tf_op | source)
XLA Modules:
  0.0 472.9 jit_solution(10750513817424661433)
XLA Ops:
  7.2 11.2 %all-gather = bf16[12,1,8,8,256]{4,3,2,1,0:T(8,128)(2,1)S(1)} all-gather(bf16[3,1,8,8,256]{4,3,2,1,0:T(8,128)(2,1)} %param.7), channel_id=2, replica_groups=mesh['ta'=4,'ha'=32,'ga'=2] {'ta'}, dimensions={0}, use_global_device_ids=true | all-gather | bytes 491520 | tf_op jit(solution)/shard_map/all_gather | solution.py:57
  18.4 9.5 %collective-permute-start = (bf16[12,8,8,256]{3,2,1,0:T(8,128)(2,1)S(1)}, bf16[12,8,8,256]{3,2,1,0:T(8,128)(2,1)S(1)}, u32[]{:S(2)}, u32[]{:S(2)}) collective-permute-start(bf16[12,8,8,256]{3,2,1,0:T(8,128)(2,1)S(1)} %bitcast.99), channel_id=1, source_target_pairs={{0,18},{2,20},{4,22},{6,24},{8,26},{10,28},{12,30},{14,32},{16,34}... | collective-permute-start | bytes 1179656 | tf_op jit(solution)/shard_map/ppermute | solution.py:13
  28.0 3.1 collective-permute-start.1
  33.0 3.4 collective-permute-start.3
  44.3 12.6 %all-gather.1 = bf16[12,1,8,8,256]{4,3,2,1,0:T(8,128)(2,1)} all-gather(bf16[3,1,8,8,256]{4,3,2,1,0:T(8,128)(2,1)} %param.8), channel_id=3, replica_groups=mesh['ta'=4,'ha'=32,'ga'=2] {'ta'}, dimensions={0}, use_global_device_ids=true | all-gather | bytes 491520 | tf_op jit(solution)/shard_map/all_gather | solution.py:58
  56.9 7.9 %collective-permute-start.5 = (bf16[12,8,8,256]{3,2,1,0:T(8,128)(2,1)S(1)}, bf16[12,8,8,256]{3,2,1,0:T(8,128)(2,1)S(1)}, u32[]{:S(2)}, u32[]{:S(2)}) collective-permute-start(bf16[12,8,8,256]{3,2,1,0:T(8,128)(2,1)S(1)} %bitcast.104), channel_id=1, source_target_pairs={{14,0},{16,2},{18,4},{20,6},{22,8},{24,10},{26,12},{28,14},{30,16}... | collective-permute-start | bytes 1179656 | tf_op jit(solution)/shard_map/ppermute | solution.py:13
  68.3 4.1 collective-permute-done.2
  75.1 15.5 %collective-permute-start.8 = (bf16[12,8,8,256]{3,2,1,0:T(8,128)(2,1)}, bf16[12,8,8,256]{3,2,1,0:T(8,128)(2,1)}, u32[]{:S(2)}, u32[]{:S(2)}) collective-permute-start(bf16[12,8,8,256]{3,2,1,0:T(8,128)(2,1)} %bitcast.17), channel_id=1, source_target_pairs={{0,18},{2,20},{4,22},{6,24},{8,26},{10,28},{12,30},{14,32},{16,34}... | collective-permute-start | bytes 1179656 | tf_op jit(solution)/shard_map/ppermute | solution.py:13
  92.3 3.2 collective-permute-start.9
  99.8 14.7 %collective-permute-start.11 = (bf16[12,8,8,256]{3,2,1,0:T(8,128)(2,1)}, bf16[12,8,8,256]{3,2,1,0:T(8,128)(2,1)}, u32[]{:S(2)}, u32[]{:S(2)}) collective-permute-start(bf16[12,8,8,256]{3,2,1,0:T(8,128)(2,1)} %bitcast.17), channel_id=1, source_target_pairs={{0,2},{2,4},{4,6},{6,8},{8,10},{10,12},{12,14},{14,16},{16,18},{18... | collective-permute-start | bytes 1179656 | tf_op jit(solution)/shard_map/ppermute | solution.py:13
  118.0 7.0 %reshape.154 = bf16[6912,2,128]{2,1,0:T(2,128)(2,1)S(1)} reshape(bf16[9,12,8,8,256]{4,3,2,1,0:T(8,128)(2,1)} %bitcast_dynamic-update-slice_fusion.9) | data formatting | bytes 7077888 | tf_op jit(solution)/shard_map/reshape | solution.py:92
  125.0 2.5 multiply_add_fusion
  127.4 5.9 %fusion.43 = (f32[2,192]{1,0:T(2,128)S(1)}, f32[2,192,6912]{2,1,0:T(8,128)}) fusion(f32[2,6912,192]{1,2,0:T(8,128)S(1)} %multiply_add_fusion), kind=kOutput, calls=%fused_computation.81 | output fusion | flops 5315327 | bytes 21235200 | tf_op jit(solution)/shard_map/sub | solution.py:23
  133.4 6.9 %fusion.9 = bf16[6912,2,128]{2,0,1:T(8,128)(2,1)S(1)} fusion(f32[2,192,6912]{2,1,0:T(8,128)} %get-tuple-element.28, f32[2,192]{1,0:T(2,128)S(1)} %get-tuple-element.27, bf16[192,2,128]{2,1,0:T(2,128)(2,1)S(1)} %copy-done.2), kind=kOutput, calls=%fused_computation.12 | convolution fusion | flops 686555136 | bytes 14255616 | tf_op jit(solution)/shard_map/hqk,qhd->khd/dot_general | solution.py:26
  145.3 2.2 copy.61
  166.1 2.2 copy.66
  170.2 2.3 copy.67
  174.5 8.5 %collective-permute-start.13 = (bf16[12,8,8,256]{3,2,1,0:T(8,128)(2,1)}, bf16[12,8,8,256]{3,2,1,0:T(8,128)(2,1)S(1)}, u32[]{:S(2)}, u32[]{:S(2)}) collective-permute-start(bf16[12,8,8,256]{3,2,1,0:T(8,128)(2,1)} %bitcast.17), channel_id=1, source_target_pairs={{14,0},{16,2},{18,4},{20,6},{22,8},{24,10},{26,12},{28,14},{30,16}... | collective-permute-start | bytes 1179656 | tf_op jit(solution)/shard_map/ppermute | solution.py:13
  201.4 10.1 %collective-permute-done.13 = bf16[12,8,8,256]{3,2,1,0:T(8,128)(2,1)S(1)} collective-permute-done((bf16[12,8,8,256]{3,2,1,0:T(8,128)(2,1)}, bf16[12,8,8,256]{3,2,1,0:T(8,128)(2,1)S(1)}, u32[]{:S(2)}, u32[]{:S(2)}) %collective-permute-start.13) | collective-permute-done | bytes 393248 | tf_op jit(solution)/shard_map/ppermute | solution.py:13
  211.5 6.3 %collective-permute-start.26 = (bf16[12,8,8,256]{3,2,1,0:T(8,128)(2,1)}, bf16[12,8,8,256]{3,2,1,0:T(8,128)(2,1)}, u32[]{:S(2)}, u32[]{:S(2)}) collective-permute-start(bf16[12,8,8,256]{3,2,1,0:T(8,128)(2,1)} %squeeze.68), channel_id=1, source_target_pairs={{14,0},{16,2},{18,4},{20,6},{22,8},{24,10},{26,12},{28,14},{30,16}... | collective-permute-start | bytes 1179656 | tf_op jit(solution)/shard_map/ppermute | solution.py:13
  218.6 23.4 %collective-permute-done.14 = bf16[12,8,8,256]{3,2,1,0:T(8,128)(2,1)S(1)} collective-permute-done((bf16[12,8,8,256]{3,2,1,0:T(8,128)(2,1)}, bf16[12,8,8,256]{3,2,1,0:T(8,128)(2,1)S(1)}, u32[]{:S(2)}, u32[]{:S(2)}) %collective-permute-start.14) | collective-permute-done | bytes 393248 | tf_op jit(solution)/shard_map/ppermute | solution.py:13
  244.7 4.7 %collective-permute-done.15 = bf16[12,8,8,256]{3,2,1,0:T(8,128)(2,1)S(1)} collective-permute-done((bf16[12,8,8,256]{3,2,1,0:T(8,128)(2,1)}, bf16[12,8,8,256]{3,2,1,0:T(8,128)(2,1)S(1)}, u32[]{:S(2)}, u32[]{:S(2)}) %collective-permute-start.15) | collective-permute-done | bytes 393248 | tf_op jit(solution)/shard_map/ppermute | solution.py:13
  249.4 3.1 collective-permute-start.28
  253.3 7.8 %reshape.156 = bf16[6912,2,128]{2,1,0:T(2,128)(2,1)} reshape(bf16[9,12,8,8,256]{4,3,2,1,0:T(8,128)(2,1)} %bitcast_dynamic-update-slice_fusion) | data formatting | bytes 7077888 | tf_op jit(solution)/shard_map/reshape | solution.py:93
  261.1 5.4 %collective-permute-done.24 = bf16[12,8,8,256]{3,2,1,0:T(8,128)(2,1)} collective-permute-done((bf16[12,8,8,256]{3,2,1,0:T(8,128)(2,1)}, bf16[12,8,8,256]{3,2,1,0:T(8,128)(2,1)}, u32[]{:S(2)}, u32[]{:S(2)}) %collective-permute-start.24) | collective-permute-done | bytes 393248 | tf_op jit(solution)/shard_map/ppermute | solution.py:13
  266.5 2.8 collective-permute-start.29
  269.4 6.4 %collective-permute-done.25 = bf16[12,8,8,256]{3,2,1,0:T(8,128)(2,1)} collective-permute-done((bf16[12,8,8,256]{3,2,1,0:T(8,128)(2,1)}, bf16[12,8,8,256]{3,2,1,0:T(8,128)(2,1)}, u32[]{:S(2)}, u32[]{:S(2)}) %collective-permute-start.25) | collective-permute-done | bytes 393248 | tf_op jit(solution)/shard_map/ppermute | solution.py:13
  279.7 4.8 %collective-permute-start.31 = (bf16[12,8,8,256]{3,2,1,0:T(8,128)(2,1)}, bf16[12,8,8,256]{3,2,1,0:T(8,128)(2,1)}, u32[]{:S(2)}, u32[]{:S(2)}) collective-permute-start(bf16[12,8,8,256]{3,2,1,0:T(8,128)(2,1)} %squeeze.73), channel_id=1, source_target_pairs={{0,18},{2,20},{4,22},{6,24},{8,26},{10,28},{12,30},{14,32},{16,34}... | collective-permute-start | bytes 1179656 | tf_op jit(solution)/shard_map/ppermute | solution.py:13
  284.5 9.9 %fusion.3 = bf16[2,192,6912]{2,1,0:T(8,128)(2,1)} fusion(f32[2,192]{1,0:T(2,128)S(1)} %copy.78, f32[2,192,6912]{2,1,0:T(8,128)} %get-tuple-element.28, f32[2,192]{1,0:T(2,128)S(1)} %get-tuple-element.27, bf16[6912,2,128]{2,1,0:T(2,128)(2,1)} %reshape.156, bf16[192,2,128]{2,1,0:T(2,128)(2,1)} %copy-done.1), kind=kOutput, calls=%fused_computation.4 | convolution fusion | flops 692748288 | bytes 19565568 | tf_op jit(solution)/shard_map/qhd,khd->hqk/dot_general | solution.py:29
  295.9 2.7 reshape.161
  298.6 3.5 convert_add_fusion
  302.2 5.4 %fusion.8 = bf16[6912,2,128]{2,0,1:T(8,128)(2,1)S(1)} fusion(bf16[2,192,6912]{2,1,0:T(8,128)(2,1)} %fusion.3, bf16[192,2,128]{2,1,0:T(2,128)(2,1)} %reshape.155), kind=kOutput, calls=%fused_computation.11 | convolution fusion | flops 681246720 | bytes 8945664 | tf_op jit(solution)/shard_map/hqk,qhd->khd/dot_general | solution.py:35
  312.6 2.4 collective-permute-start.16
  315.0 2.2 copy.51
  319.1 17.2 %collective-permute-start.17 = (bf16[12,8,8,256]{3,2,1,0:T(8,128)(2,1)}, bf16[12,8,8,256]{3,2,1,0:T(8,128)(2,1)}, u32[]{:S(2)}, u32[]{:S(2)}) collective-permute-start(bf16[12,8,8,256]{3,2,1,0:T(8,128)(2,1)} %squeeze.59), channel_id=1, source_target_pairs={{16,0},{18,2},{20,4},{22,6},{24,8},{26,10},{28,12},{30,14},{32,16}... | collective-permute-start | bytes 1179656 | tf_op jit(solution)/shard_map/ppermute | solution.py:13
  336.3 2.2 copy.52
  342.4 2.1 copy.53
  352.6 12.7 %collective-permute-start.20 = (bf16[12,8,8,256]{3,2,1,0:T(8,128)(2,1)}, bf16[12,8,8,256]{3,2,1,0:T(8,128)(2,1)}, u32[]{:S(2)}, u32[]{:S(2)}) collective-permute-start(bf16[12,8,8,256]{3,2,1,0:T(8,128)(2,1)} %squeeze.62), channel_id=1, source_target_pairs={{0,2},{2,4},{4,6},{6,8},{8,10},{10,12},{12,14},{14,16},{16,18},{18... | collective-permute-start | bytes 1179656 | tf_op jit(solution)/shard_map/ppermute | solution.py:13
  373.5 2.2 copy.57
  377.7 5.6 %collective-permute-start.21 = (bf16[12,8,8,256]{3,2,1,0:T(8,128)(2,1)}, bf16[12,8,8,256]{3,2,1,0:T(8,128)(2,1)}, u32[]{:S(2)}, u32[]{:S(2)}) collective-permute-start(bf16[12,8,8,256]{3,2,1,0:T(8,128)(2,1)} %squeeze.63), channel_id=1, source_target_pairs={{0,14},{2,16},{4,18},{6,20},{8,22},{10,24},{12,26},{14,28},{16,30}... | collective-permute-start | bytes 1179656 | tf_op jit(solution)/shard_map/ppermute | solution.py:13
  383.2 5.3 %collective-permute-start.22 = (bf16[12,8,8,256]{3,2,1,0:T(8,128)(2,1)}, bf16[12,8,8,256]{3,2,1,0:T(8,128)(2,1)}, u32[]{:S(2)}, u32[]{:S(2)}) collective-permute-start(bf16[12,8,8,256]{3,2,1,0:T(8,128)(2,1)} %squeeze.64), channel_id=1, source_target_pairs={{0,16},{2,18},{4,20},{6,22},{8,24},{10,26},{12,28},{14,30},{16,32}... | collective-permute-start | bytes 1179656 | tf_op jit(solution)/shard_map/ppermute | solution.py:13
  388.5 4.4 collective-permute-start.23
  393.0 2.6 copy.49
  395.6 2.7 reshape.160
  399.7 9.6 %collective-permute-done.23 = bf16[12,8,8,256]{3,2,1,0:T(8,128)(2,1)} collective-permute-done((bf16[12,8,8,256]{3,2,1,0:T(8,128)(2,1)}, bf16[12,8,8,256]{3,2,1,0:T(8,128)(2,1)}, u32[]{:S(2)}, u32[]{:S(2)}) %collective-permute-start.23) | collective-permute-done | bytes 393248 | tf_op jit(solution)/shard_map/ppermute | solution.py:13
  409.3 3.5 convert_add_fusion.1
  412.8 4.0 fusion.18
  419.2 45.0 %reduce-scatter.3.cloned.1.call-done = f32[3,8,8,256]{3,2,1,0:T(8,128)} async-done(((f32[12,8,8,256]{3,2,1,0:T(8,128)}), f32[3,8,8,256]{3,2,1,0:T(8,128)}) %reduce-scatter.3.cloned.1.call-update) | async-done | bytes 196624 | tf_op jit(solution)/shard_map/reduce_scatter | solution.py:112
  (112 shorter events, 115.4 us)
Async XLA Ops:
  7.2 410.5 %reduce-scatter.5.cloned.1.call-start = ((), (), s32[]{:S(2)}) async-start(), calls=%async_computation.3 | async-start | bytes 983040 | tf_op jit(solution)/shard_map/reduce_scatter | solution.py:113
  18.4 38.5 %collective-permute-start = (bf16[12,8,8,256]{3,2,1,0:T(8,128)(2,1)S(1)}, bf16[12,8,8,256]{3,2,1,0:T(8,128)(2,1)S(1)}, u32[]{:S(2)}, u32[]{:S(2)}) collective-permute-start(bf16[12,8,8,256]{3,2,1,0:T(8,128)(2,1)S(1)} %bitcast.99), channel_id=1, source_target_pairs={{0,18},{2,20},{4,22},{6,24},{8,26},{10,28},{12,30},{14,32},{16,34}... | collective-permute-start | bytes 1179656 | tf_op jit(solution)/shard_map/ppermute | solution.py:13
  28.0 37.7 %collective-permute-start.1 = (bf16[12,8,8,256]{3,2,1,0:T(8,128)(2,1)S(1)}, bf16[12,8,8,256]{3,2,1,0:T(8,128)(2,1)S(1)}, u32[]{:S(2)}, u32[]{:S(2)}) collective-permute-start(bf16[12,8,8,256]{3,2,1,0:T(8,128)(2,1)S(1)} %bitcast.100), channel_id=1, source_target_pairs={{0,16},{2,18},{4,20},{6,22},{8,24},{10,26},{12,28},{14,30},{16,32}... | collective-permute-start | bytes 1179656 | tf_op jit(solution)/shard_map/ppermute | solution.py:13
  31.1 41.4 %collective-permute-start.2 = (bf16[12,8,8,256]{3,2,1,0:T(8,128)(2,1)S(1)}, bf16[12,8,8,256]{3,2,1,0:T(8,128)(2,1)S(1)}, u32[]{:S(2)}, u32[]{:S(2)}) collective-permute-start(bf16[12,8,8,256]{3,2,1,0:T(8,128)(2,1)S(1)} %bitcast.101), channel_id=1, source_target_pairs={{0,14},{2,16},{4,18},{6,20},{8,22},{10,24},{12,26},{14,28},{16,30}... | collective-permute-start | bytes 1179656 | tf_op jit(solution)/shard_map/ppermute | solution.py:13
  33.0 42.1 %collective-permute-start.3 = (bf16[12,8,8,256]{3,2,1,0:T(8,128)(2,1)S(1)}, bf16[12,8,8,256]{3,2,1,0:T(8,128)(2,1)S(1)}, u32[]{:S(2)}, u32[]{:S(2)}) collective-permute-start(bf16[12,8,8,256]{3,2,1,0:T(8,128)(2,1)S(1)} %bitcast.102), channel_id=1, source_target_pairs={{0,2},{2,4},{4,6},{6,8},{8,10},{10,12},{12,14},{14,16},{16,18},{18... | collective-permute-start | bytes 1179656 | tf_op jit(solution)/shard_map/ppermute | solution.py:13
  36.4 55.9 %collective-permute-start.4 = (bf16[12,8,8,256]{3,2,1,0:T(8,128)(2,1)S(1)}, bf16[12,8,8,256]{3,2,1,0:T(8,128)(2,1)S(1)}, u32[]{:S(2)}, u32[]{:S(2)}) collective-permute-start(bf16[12,8,8,256]{3,2,1,0:T(8,128)(2,1)S(1)} %bitcast.103), channel_id=1, source_target_pairs={{2,0},{4,2},{6,4},{8,6},{10,8},{12,10},{14,12},{16,14},{18,16},{20... | collective-permute-start | bytes 1179656 | tf_op jit(solution)/shard_map/ppermute | solution.py:13
  40.4 1.0 copy-start.1
  56.9 39.4 %collective-permute-start.5 = (bf16[12,8,8,256]{3,2,1,0:T(8,128)(2,1)S(1)}, bf16[12,8,8,256]{3,2,1,0:T(8,128)(2,1)S(1)}, u32[]{:S(2)}, u32[]{:S(2)}) collective-permute-start(bf16[12,8,8,256]{3,2,1,0:T(8,128)(2,1)S(1)} %bitcast.104), channel_id=1, source_target_pairs={{14,0},{16,2},{18,4},{20,6},{22,8},{24,10},{26,12},{28,14},{30,16}... | collective-permute-start | bytes 1179656 | tf_op jit(solution)/shard_map/ppermute | solution.py:13
  65.6 34.2 %collective-permute-start.6 = (bf16[12,8,8,256]{3,2,1,0:T(8,128)(2,1)S(1)}, bf16[12,8,8,256]{3,2,1,0:T(8,128)(2,1)S(1)}, u32[]{:S(2)}, u32[]{:S(2)}) collective-permute-start(bf16[12,8,8,256]{3,2,1,0:T(8,128)(2,1)S(1)} %bitcast.105), channel_id=1, source_target_pairs={{16,0},{18,2},{20,4},{22,6},{24,8},{26,10},{28,12},{30,14},{32,16}... | collective-permute-start | bytes 1179656 | tf_op jit(solution)/shard_map/ppermute | solution.py:13
  72.4 42.9 %collective-permute-start.7 = (bf16[12,8,8,256]{3,2,1,0:T(8,128)(2,1)S(1)}, bf16[12,8,8,256]{3,2,1,0:T(8,128)(2,1)S(1)}, u32[]{:S(2)}, u32[]{:S(2)}) collective-permute-start(bf16[12,8,8,256]{3,2,1,0:T(8,128)(2,1)S(1)} %bitcast.106), channel_id=1, source_target_pairs={{18,0},{20,2},{22,4},{24,6},{26,8},{28,10},{30,12},{32,14},{34,16}... | collective-permute-start | bytes 1179656 | tf_op jit(solution)/shard_map/ppermute | solution.py:13
  75.1 99.4 %collective-permute-start.8 = (bf16[12,8,8,256]{3,2,1,0:T(8,128)(2,1)}, bf16[12,8,8,256]{3,2,1,0:T(8,128)(2,1)}, u32[]{:S(2)}, u32[]{:S(2)}) collective-permute-start(bf16[12,8,8,256]{3,2,1,0:T(8,128)(2,1)} %bitcast.17), channel_id=1, source_target_pairs={{0,18},{2,20},{4,22},{6,24},{8,26},{10,28},{12,30},{14,32},{16,34}... | collective-permute-start | bytes 1179656 | tf_op jit(solution)/shard_map/ppermute | solution.py:13
  92.3 92.5 %collective-permute-start.9 = (bf16[12,8,8,256]{3,2,1,0:T(8,128)(2,1)}, bf16[12,8,8,256]{3,2,1,0:T(8,128)(2,1)}, u32[]{:S(2)}, u32[]{:S(2)}) collective-permute-start(bf16[12,8,8,256]{3,2,1,0:T(8,128)(2,1)} %bitcast.17), channel_id=1, source_target_pairs={{0,16},{2,18},{4,20},{6,22},{8,24},{10,26},{12,28},{14,30},{16,32}... | collective-permute-start | bytes 1179656 | tf_op jit(solution)/shard_map/ppermute | solution.py:13
  96.3 92.2 %collective-permute-start.10 = (bf16[12,8,8,256]{3,2,1,0:T(8,128)(2,1)}, bf16[12,8,8,256]{3,2,1,0:T(8,128)(2,1)}, u32[]{:S(2)}, u32[]{:S(2)}) collective-permute-start(bf16[12,8,8,256]{3,2,1,0:T(8,128)(2,1)} %bitcast.17), channel_id=1, source_target_pairs={{0,14},{2,16},{4,18},{6,20},{8,22},{10,24},{12,26},{14,28},{16,30}... | collective-permute-start | bytes 1179656 | tf_op jit(solution)/shard_map/ppermute | solution.py:13
  99.8 92.4 %collective-permute-start.11 = (bf16[12,8,8,256]{3,2,1,0:T(8,128)(2,1)}, bf16[12,8,8,256]{3,2,1,0:T(8,128)(2,1)}, u32[]{:S(2)}, u32[]{:S(2)}) collective-permute-start(bf16[12,8,8,256]{3,2,1,0:T(8,128)(2,1)} %bitcast.17), channel_id=1, source_target_pairs={{0,2},{2,4},{4,6},{6,8},{8,10},{10,12},{12,14},{14,16},{16,18},{18... | collective-permute-start | bytes 1179656 | tf_op jit(solution)/shard_map/ppermute | solution.py:13
  115.3 82.4 %collective-permute-start.12 = (bf16[12,8,8,256]{3,2,1,0:T(8,128)(2,1)}, bf16[12,8,8,256]{3,2,1,0:T(8,128)(2,1)}, u32[]{:S(2)}, u32[]{:S(2)}) collective-permute-start(bf16[12,8,8,256]{3,2,1,0:T(8,128)(2,1)} %bitcast.17), channel_id=1, source_target_pairs={{2,0},{4,2},{6,4},{8,6},{10,8},{12,10},{14,12},{16,14},{18,16},{20... | collective-permute-start | bytes 1179656 | tf_op jit(solution)/shard_map/ppermute | solution.py:13
  127.4 5.9 %copy-start.2 = (bf16[192,2,128]{2,1,0:T(2,128)(2,1)S(1)}, bf16[192,2,128]{2,1,0:T(2,128)(2,1)}, u32[]{:S(2)}) copy-start(bf16[192,2,128]{2,1,0:T(2,128)(2,1)} %copy-done.1) | copy-start | bytes 294916
  174.5 37.0 %collective-permute-start.13 = (bf16[12,8,8,256]{3,2,1,0:T(8,128)(2,1)}, bf16[12,8,8,256]{3,2,1,0:T(8,128)(2,1)S(1)}, u32[]{:S(2)}, u32[]{:S(2)}) collective-permute-start(bf16[12,8,8,256]{3,2,1,0:T(8,128)(2,1)} %bitcast.17), channel_id=1, source_target_pairs={{14,0},{16,2},{18,4},{20,6},{22,8},{24,10},{26,12},{28,14},{30,16}... | collective-permute-start | bytes 1179656 | tf_op jit(solution)/shard_map/ppermute | solution.py:13
  184.8 57.2 %collective-permute-start.14 = (bf16[12,8,8,256]{3,2,1,0:T(8,128)(2,1)}, bf16[12,8,8,256]{3,2,1,0:T(8,128)(2,1)S(1)}, u32[]{:S(2)}, u32[]{:S(2)}) collective-permute-start(bf16[12,8,8,256]{3,2,1,0:T(8,128)(2,1)} %bitcast.17), channel_id=1, source_target_pairs={{16,0},{18,2},{20,4},{22,6},{24,8},{26,10},{28,12},{30,14},{32,16}... | collective-permute-start | bytes 1179656 | tf_op jit(solution)/shard_map/ppermute | solution.py:13
  188.5 60.9 %collective-permute-start.15 = (bf16[12,8,8,256]{3,2,1,0:T(8,128)(2,1)}, bf16[12,8,8,256]{3,2,1,0:T(8,128)(2,1)S(1)}, u32[]{:S(2)}, u32[]{:S(2)}) collective-permute-start(bf16[12,8,8,256]{3,2,1,0:T(8,128)(2,1)} %bitcast.17), channel_id=1, source_target_pairs={{18,0},{20,2},{22,4},{24,6},{26,8},{28,10},{30,12},{32,14},{34,16}... | collective-permute-start | bytes 1179656 | tf_op jit(solution)/shard_map/ppermute | solution.py:13
  192.2 74.3 %collective-permute-start.24 = (bf16[12,8,8,256]{3,2,1,0:T(8,128)(2,1)}, bf16[12,8,8,256]{3,2,1,0:T(8,128)(2,1)}, u32[]{:S(2)}, u32[]{:S(2)}) collective-permute-start(bf16[12,8,8,256]{3,2,1,0:T(8,128)(2,1)} %squeeze.66), channel_id=1, source_target_pairs={{18,0},{20,2},{22,4},{24,6},{26,8},{28,10},{30,12},{32,14},{34,16}... | collective-permute-start | bytes 1179656 | tf_op jit(solution)/shard_map/ppermute | solution.py:13
  197.7 78.1 %collective-permute-start.25 = (bf16[12,8,8,256]{3,2,1,0:T(8,128)(2,1)}, bf16[12,8,8,256]{3,2,1,0:T(8,128)(2,1)}, u32[]{:S(2)}, u32[]{:S(2)}) collective-permute-start(bf16[12,8,8,256]{3,2,1,0:T(8,128)(2,1)} %squeeze.67), channel_id=1, source_target_pairs={{16,0},{18,2},{20,4},{22,6},{24,8},{26,10},{28,12},{30,14},{32,16}... | collective-permute-start | bytes 1179656 | tf_op jit(solution)/shard_map/ppermute | solution.py:13
  211.5 68.2 %collective-permute-start.26 = (bf16[12,8,8,256]{3,2,1,0:T(8,128)(2,1)}, bf16[12,8,8,256]{3,2,1,0:T(8,128)(2,1)}, u32[]{:S(2)}, u32[]{:S(2)}) collective-permute-start(bf16[12,8,8,256]{3,2,1,0:T(8,128)(2,1)} %squeeze.68), channel_id=1, source_target_pairs={{14,0},{16,2},{18,4},{20,6},{22,8},{24,10},{26,12},{28,14},{30,16}... | collective-permute-start | bytes 1179656 | tf_op jit(solution)/shard_map/ppermute | solution.py:13
  242.0 56.6 %collective-permute-start.27 = (bf16[12,8,8,256]{3,2,1,0:T(8,128)(2,1)}, bf16[12,8,8,256]{3,2,1,0:T(8,128)(2,1)}, u32[]{:S(2)}, u32[]{:S(2)}) collective-permute-start(bf16[12,8,8,256]{3,2,1,0:T(8,128)(2,1)} %squeeze.69), channel_id=1, source_target_pairs={{2,0},{4,2},{6,4},{8,6},{10,8},{12,10},{14,12},{16,14},{18,16},{20... | collective-permute-start | bytes 1179656 | tf_op jit(solution)/shard_map/ppermute | solution.py:13
  249.4 49.2 %collective-permute-start.28 = (bf16[12,8,8,256]{3,2,1,0:T(8,128)(2,1)}, bf16[12,8,8,256]{3,2,1,0:T(8,128)(2,1)}, u32[]{:S(2)}, u32[]{:S(2)}) collective-permute-start(bf16[12,8,8,256]{3,2,1,0:T(8,128)(2,1)} %squeeze.70), channel_id=1, source_target_pairs={{0,2},{2,4},{4,6},{6,8},{8,10},{10,12},{12,14},{14,16},{16,18},{18... | collective-permute-start | bytes 1179656 | tf_op jit(solution)/shard_map/ppermute | solution.py:13
  261.1 33.3 %copy-start = (f32[768,2,128]{2,0,1:T(8,128)S(1)}, f32[768,2,128]{2,0,1:T(8,128)}, u32[]{:S(2)}) copy-start(f32[768,2,128]{2,0,1:T(8,128)} %get-tuple-element.17) | copy-start | bytes 2359300
  266.5 32.1 %collective-permute-start.29 = (bf16[12,8,8,256]{3,2,1,0:T(8,128)(2,1)}, bf16[12,8,8,256]{3,2,1,0:T(8,128)(2,1)}, u32[]{:S(2)}, u32[]{:S(2)}) collective-permute-start(bf16[12,8,8,256]{3,2,1,0:T(8,128)(2,1)} %squeeze.71), channel_id=1, source_target_pairs={{0,14},{2,16},{4,18},{6,20},{8,22},{10,24},{12,26},{14,28},{16,30}... | collective-permute-start | bytes 1179656 | tf_op jit(solution)/shard_map/ppermute | solution.py:13
  275.8 22.8 %collective-permute-start.30 = (bf16[12,8,8,256]{3,2,1,0:T(8,128)(2,1)}, bf16[12,8,8,256]{3,2,1,0:T(8,128)(2,1)}, u32[]{:S(2)}, u32[]{:S(2)}) collective-permute-start(bf16[12,8,8,256]{3,2,1,0:T(8,128)(2,1)} %squeeze.72), channel_id=1, source_target_pairs={{0,16},{2,18},{4,20},{6,22},{8,24},{10,26},{12,28},{14,30},{16,32}... | collective-permute-start | bytes 1179656 | tf_op jit(solution)/shard_map/ppermute | solution.py:13
  279.7 18.9 %collective-permute-start.31 = (bf16[12,8,8,256]{3,2,1,0:T(8,128)(2,1)}, bf16[12,8,8,256]{3,2,1,0:T(8,128)(2,1)}, u32[]{:S(2)}, u32[]{:S(2)}) collective-permute-start(bf16[12,8,8,256]{3,2,1,0:T(8,128)(2,1)} %squeeze.73), channel_id=1, source_target_pairs={{0,18},{2,20},{4,22},{6,24},{8,26},{10,28},{12,30},{14,32},{16,34}... | collective-permute-start | bytes 1179656 | tf_op jit(solution)/shard_map/ppermute | solution.py:13
  302.2 162.0 %reduce-scatter.3.cloned.1.call-start = ((), (), s32[]{:S(2)}) async-start(), calls=%async_computation.2 | async-start | bytes 983040 | tf_op jit(solution)/shard_map/reduce_scatter | solution.py:112
  312.6 65.1 %collective-permute-start.16 = (bf16[12,8,8,256]{3,2,1,0:T(8,128)(2,1)}, bf16[12,8,8,256]{3,2,1,0:T(8,128)(2,1)}, u32[]{:S(2)}, u32[]{:S(2)}) collective-permute-start(bf16[12,8,8,256]{3,2,1,0:T(8,128)(2,1)} %squeeze.58), channel_id=1, source_target_pairs={{18,0},{20,2},{22,4},{24,6},{26,8},{28,10},{30,12},{32,14},{34,16}... | collective-permute-start | bytes 1179656 | tf_op jit(solution)/shard_map/ppermute | solution.py:13
  319.1 64.1 %collective-permute-start.17 = (bf16[12,8,8,256]{3,2,1,0:T(8,128)(2,1)}, bf16[12,8,8,256]{3,2,1,0:T(8,128)(2,1)}, u32[]{:S(2)}, u32[]{:S(2)}) collective-permute-start(bf16[12,8,8,256]{3,2,1,0:T(8,128)(2,1)} %squeeze.59), channel_id=1, source_target_pairs={{16,0},{18,2},{20,4},{22,6},{24,8},{26,10},{28,12},{30,14},{32,16}... | collective-permute-start | bytes 1179656 | tf_op jit(solution)/shard_map/ppermute | solution.py:13
  340.5 48.1 %collective-permute-start.18 = (bf16[12,8,8,256]{3,2,1,0:T(8,128)(2,1)}, bf16[12,8,8,256]{3,2,1,0:T(8,128)(2,1)}, u32[]{:S(2)}, u32[]{:S(2)}) collective-permute-start(bf16[12,8,8,256]{3,2,1,0:T(8,128)(2,1)} %squeeze.60), channel_id=1, source_target_pairs={{14,0},{16,2},{18,4},{20,6},{22,8},{24,10},{26,12},{28,14},{30,16}... | collective-permute-start | bytes 1179656 | tf_op jit(solution)/shard_map/ppermute | solution.py:13
  346.5 51.7 %collective-permute-start.19 = (bf16[12,8,8,256]{3,2,1,0:T(8,128)(2,1)}, bf16[12,8,8,256]{3,2,1,0:T(8,128)(2,1)}, u32[]{:S(2)}, u32[]{:S(2)}) collective-permute-start(bf16[12,8,8,256]{3,2,1,0:T(8,128)(2,1)} %squeeze.61), channel_id=1, source_target_pairs={{2,0},{4,2},{6,4},{8,6},{10,8},{12,10},{14,12},{16,14},{18,16},{20... | collective-permute-start | bytes 1179656 | tf_op jit(solution)/shard_map/ppermute | solution.py:13
  352.6 45.7 %collective-permute-start.20 = (bf16[12,8,8,256]{3,2,1,0:T(8,128)(2,1)}, bf16[12,8,8,256]{3,2,1,0:T(8,128)(2,1)}, u32[]{:S(2)}, u32[]{:S(2)}) collective-permute-start(bf16[12,8,8,256]{3,2,1,0:T(8,128)(2,1)} %squeeze.62), channel_id=1, source_target_pairs={{0,2},{2,4},{4,6},{6,8},{8,10},{10,12},{12,14},{14,16},{16,18},{18... | collective-permute-start | bytes 1179656 | tf_op jit(solution)/shard_map/ppermute | solution.py:13
  377.7 20.6 %collective-permute-start.21 = (bf16[12,8,8,256]{3,2,1,0:T(8,128)(2,1)}, bf16[12,8,8,256]{3,2,1,0:T(8,128)(2,1)}, u32[]{:S(2)}, u32[]{:S(2)}) collective-permute-start(bf16[12,8,8,256]{3,2,1,0:T(8,128)(2,1)} %squeeze.63), channel_id=1, source_target_pairs={{0,14},{2,16},{4,18},{6,20},{8,22},{10,24},{12,26},{14,28},{16,30}... | collective-permute-start | bytes 1179656 | tf_op jit(solution)/shard_map/ppermute | solution.py:13
  383.2 16.4 %collective-permute-start.22 = (bf16[12,8,8,256]{3,2,1,0:T(8,128)(2,1)}, bf16[12,8,8,256]{3,2,1,0:T(8,128)(2,1)}, u32[]{:S(2)}, u32[]{:S(2)}) collective-permute-start(bf16[12,8,8,256]{3,2,1,0:T(8,128)(2,1)} %squeeze.64), channel_id=1, source_target_pairs={{0,16},{2,18},{4,20},{6,22},{8,24},{10,26},{12,28},{14,30},{16,32}... | collective-permute-start | bytes 1179656 | tf_op jit(solution)/shard_map/ppermute | solution.py:13
  388.5 20.8 %collective-permute-start.23 = (bf16[12,8,8,256]{3,2,1,0:T(8,128)(2,1)}, bf16[12,8,8,256]{3,2,1,0:T(8,128)(2,1)}, u32[]{:S(2)}, u32[]{:S(2)}) collective-permute-start(bf16[12,8,8,256]{3,2,1,0:T(8,128)(2,1)} %squeeze.65), channel_id=1, source_target_pairs={{0,18},{2,20},{4,22},{6,24},{8,26},{10,28},{12,30},{14,32},{16,34}... | collective-permute-start | bytes 1179656 | tf_op jit(solution)/shard_map/ppermute | solution.py:13
Sparse Core Ops, SparseCore 0:
  302.3 51.7 reduce-scatter.4
  412.9 51.2 reduce-scatter.2
where the time goes:
time: 481 us; the launch traced here: 473 us
  starting transfers between devices  157 us (33%)
  local copies, waits for them, and re-layouts  114 us (24%)
  waiting for transfers between devices  113 us (23%)
  matrix products  29.7 us (6%)
  blocking collectives  23.8 us (5%)
  other arithmetic  20.1 us (4%)
  between operations  14.8 us (3%)
    ppermute x32, starting transfers between devices, passed_along(): return lax.ppermute(block, axis, route)  157 us
    ppermute x32, waiting for transfers between devices, passed_along(): return lax.ppermute(block, axis, route)  68 us
    reduce_scatter x1, waiting for transfers between devices, local(): lax.psum_scatter(key_sum, 'ta', scatter_dimension=0, tiled=True)  45 us
    unnamed x22, local copies, waits for them, and re-layouts  18.6 us
    slice x8, local copies, waits for them, and re-layouts, local(): value_block[place_index]  16.4 us
    slice x8, local copies, waits for them, and re-layouts, local(): key_block[place_index]  16.2 us
    squeeze x8, local copies, waits for them, and re-layouts, local(): value_block[place_index]  16 us
    squeeze x8, local copies, waits for them, and re-layouts, local(): key_block[place_index]  15.9 us
  transfers between devices with their start and end apart: 34, of which 11 were waited for; matrix products, arithmetic and copies ran while one was open for 34% of the time, Pallas kernels for 0%

commit v1 on v0

v1 whole, which is shorter than its diff:
```python
import functools

import jax
import jax.numpy as jnp
from jax import lax
from jax.experimental import pallas as pl
from jax.experimental.pallas import tpu as pltpu
from jax.sharding import PartitionSpec as P

HEAD_DIM = 128
TILE_T = 6
CLOSED = 1e30
SCALE = HEAD_DIM ** (-0.5)
SCALE2 = SCALE * 1.4426950408889634
F32 = jnp.float32
BF16 = jnp.bfloat16
NT = (((1,), (1,)), ((), ()))
NN = (((1,), (0,)), ((), ()))
TN = (((0,), (0,)), ((), ()))


def dot(a, b, dims, precision=None):
    return lax.dot_general(a, b, dims, precision=precision, preferred_element_type=F32)


def moved(block, axis, route):
    return lax.ppermute(block, axis, route)


def head_cols(head):
    return pl.ds(head * HEAD_DIM, HEAD_DIM)


def query_columns(own_ref, piece_refs, start, head):
    rows = own_ref.shape[0]
    cols = head_cols(head)
    parts = [own_ref[:, cols]] + [r[pl.ds(start, rows), cols] for r in piece_refs]
    return jnp.concatenate(parts, axis=0)


def stats_kernel(blocks, slots, first, *refs):
    if first:
        bias_ref, own_ref, saved_ref, grad_ref, *refs = refs
        pieces, keys, (out_ref,) = refs[:3], refs[3:-1], refs[-1:]
    else:
        bias_ref, prior_ref, own_ref, *refs = refs
        pieces, keys, (out_ref,) = refs[:3], refs[3:-1], refs[-1:]
    heads = own_ref.shape[1] // HEAD_DIM
    rows = own_ref.shape[0]
    out_ref[...] = jnp.zeros_like(out_ref)
    for head in range(heads):
        query = query_columns(own_ref, pieces, 0, head)
        cols = head_cols(head)
        scores = []
        tops = []
        for (ref, start), slot in zip(blocks, slots):
            s = dot(keys[ref][pl.ds(start, rows), cols], query, NT)
            scores.append(s)
            tops.append(jnp.max(s, axis=0, keepdims=True) * SCALE2 - bias_ref[slot : slot + 1, :])
        top = jnp.maximum(functools.reduce(jnp.maximum, tops), -0.5 * CLOSED)
        if not first:
            top = jnp.maximum(top, prior_ref[head : head + 1, :])
        total = jnp.zeros_like(top)
        for s, slot in zip(scores, slots):
            raised = jnp.exp2(s * SCALE2 - (top + bias_ref[slot : slot + 1, :]))
            total = total + jnp.sum(raised, axis=0, keepdims=True)
        if first:
            product = grad_ref[:, cols].astype(F32) * saved_ref[:, cols].astype(F32)
            ones = jnp.ones((8, HEAD_DIM), F32)
            row_dot = dot(ones, product, NT, lax.Precision.HIGHEST)[:1]
            out_ref[2 * heads + head : 2 * heads + head + 1, 0:rows] = row_dot
        else:
            total = total + prior_ref[heads + head : heads + head + 1, :] * jnp.exp2(
                prior_ref[head : head + 1, :] - top
            )
            out_ref[2 * heads + head : 2 * heads + head + 1, :] = prior_ref[
                2 * heads + head : 2 * heads + head + 1, :
            ]
        out_ref[head : head + 1, :] = top
        out_ref[heads + head : heads + head + 1, :] = total


def rolled(row, shift):
    if shift == 0:
        return row
    width = row.shape[1]
    return jnp.concatenate([row[:, width - shift :], row[:, : width - shift]], axis=1)


def merge_kernel(heads, rows, *refs):
    *stats, out_ref = refs
    tables = [rolled(ref[...], rows * place) for place, ref in enumerate(stats)]
    out_ref[...] = jnp.zeros_like(out_ref)
    top = functools.reduce(jnp.maximum, [t[0:heads] for t in tables])
    total = sum(t[heads : 2 * heads] * jnp.exp2(t[0:heads] - top) for t in tables)
    out_ref[0:heads, :] = top + jnp.log2(total)
    out_ref[heads : 2 * heads, :] = sum(t[2 * heads : 3 * heads] for t in tables)


def grads_kernel(blocks, slots, outs, first, *refs):
    bias_ref, lse_ref, own_q, own_g, p1, p2, p3, *refs = refs
    pieces = (p1, p2, p3)
    n_in = max(b[0] for b in blocks) + 1
    keys, refs = refs[:n_in], refs[n_in:]
    values, refs = refs[:n_in], refs[n_in:]
    if not first:
        prior_ref, *refs = refs
    *part_refs, dq_ref = refs
    heads = own_q.shape[1] // HEAD_DIM
    rows = own_q.shape[0]
    for head in range(heads):
        cols = head_cols(head)
        query = query_columns(own_q, pieces, 0, head)
        grad = query_columns(own_g, pieces, rows, head)
        lse = lse_ref[head : head + 1, :]
        row_dot = lse_ref[heads + head : heads + head + 1, :] * SCALE
        dq = None if first else prior_ref[:, cols]
        for (ref, start), slot, (out, at) in zip(blocks, slots, outs):
            key = keys[ref][pl.ds(start, rows), cols]
            value = values[ref][pl.ds(start, rows), cols]
            s = dot(key, query, NT)
            weights = jnp.exp2(s * SCALE2 - (lse + bias_ref[slot : slot + 1, :]))
            dp = dot(value, grad, NT)
            score_grad = (weights * (dp * SCALE - row_dot)).astype(BF16)
            part = part_refs[out]
            half = part.shape[0] // 2
            part[pl.ds(at, rows), cols] = dot(score_grad, query, NN).astype(part.dtype)
            part[pl.ds(half + at, rows), cols] = dot(weights.astype(BF16), grad, NN).astype(
                part.dtype
            )
            step = dot(score_grad, key, TN)
            dq = step if dq is None else dq + step
        dq_ref[:, cols] = dq


def call(kernel, out_shape, *args):
    many = isinstance(out_shape, (tuple, list))
    vmem = pl.BlockSpec(memory_space=pltpu.VMEM)
    return pl.pallas_call(
        kernel,
        out_shape=out_shape,
        in_specs=[vmem] * len(args),
        out_specs=[vmem] * len(out_shape) if many else vmem,
        compiler_params=pltpu.CompilerParams(vmem_limit_bytes=32 * 1024 * 1024),
    )(*args)


def local(query_in, key_in, value_in, saved_out, out_grad, window_mask):
    frames_dev, _, tile_rows, tile_cols, width = query_in.shape
    rows = frames_dev * tile_rows * tile_cols
    heads = width // HEAD_DIM
    n_ta = lax.axis_size("ta")
    n_ha = lax.axis_size("ha")
    row_tiles, col_tiles = window_mask.shape[1:3]
    me = lax.axis_index("ta")
    plane = lax.axis_index("ha")
    row_tile = plane // col_tiles
    col_tile = plane % col_tiles

    down = [(i, i + col_tiles) for i in range(n_ha - col_tiles)]
    up = [(d, s) for s, d in down]
    right = [(i, i + 1) for i in range(n_ha) if (i + 1) % col_tiles]
    left = [(d, s) for s, d in right]

    q, k, v, o, g = (
        x.reshape(rows, width) for x in (query_in, key_in, value_in, saved_out, out_grad)
    )
    k_up = moved(k, "ha", down)
    k_down = moved(k, "ha", up)
    qg = jnp.concatenate([q, g], axis=0)
    pieces = [
        moved(qg, "ta", [(i, (i + d) % n_ta) for i in range(n_ta)]) for d in range(1, n_ta)
    ]
    k_col = jnp.concatenate([k_up, k, k_down], axis=0)
    k_left = moved(k_col, "ha", right)
    k_right = moved(k_col, "ha", left)
    v_up = moved(v, "ha", down)
    v_down = moved(v, "ha", up)
    v_col = jnp.concatenate([v_up, v, v_down], axis=0)
    v_left = moved(v_col, "ha", right)
    v_right = moved(v_col, "ha", left)

    slot = jnp.arange(16, dtype=jnp.int32)
    row_step = slot // 3 - 1
    col_step = slot % 3 - 1
    inside = (row_tile + row_step >= 0) & (row_tile + row_step < row_tiles)
    inside = inside & (col_tile + col_step >= 0) & (col_tile + col_step < col_tiles) & (slot < 9)
    key_time = me * frames_dev // TILE_T
    owner = (me - jnp.arange(n_ta, dtype=jnp.int32)) % n_ta
    query_time = owner * frames_dev // TILE_T
    windows = lax.dynamic_slice(
        window_mask, (0, row_tile, col_tile, 0), (window_mask.shape[0], 1, 1, 27)
    ).reshape(-1, 27)
    padded = jnp.pad(windows, ((0, 0), (0, 16)))
    table = jnp.zeros((16, n_ta), jnp.int32)
    for t in range(window_mask.shape[0]):
        part = lax.dynamic_slice(padded, (t, (key_time - t + 1) * 9), (1, 16)).reshape(16, 1)
        table = jnp.where(query_time[None, :] == t, part, table)
    bias = jnp.where((table == 1) & inside[:, None], 0.0, CLOSED).astype(F32)
    bias = jnp.repeat(bias, rows, axis=1)

    n_q = n_ta * rows
    stat_shape = jax.ShapeDtypeStruct((8, n_q), F32)
    col_blocks = [(0, 0), (0, rows), (0, 2 * rows)]
    side_blocks = col_blocks + [(1, 0), (1, rows), (1, 2 * rows)]
    mid_slots = (1, 4, 7)
    side_slots = (0, 3, 6, 2, 5, 8)
    stats = call(
        functools.partial(stats_kernel, col_blocks, mid_slots, True),
        stat_shape, bias, q, o, g, *pieces, k_col,
    )
    stats = call(
        functools.partial(stats_kernel, side_blocks, side_slots, False),
        stat_shape, bias, stats, q, *pieces, k_left, k_right,
    )
    others = [
        moved(stats, "ta", [(i, (i + d) % n_ta) for i in range(n_ta)]) for d in range(1, n_ta)
    ]
    lse = call(functools.partial(merge_kernel, heads, rows), stat_shape, stats, *others)
    part_shape = jax.ShapeDtypeStruct((6 * rows, width), BF16)
    mid_shape = jax.ShapeDtypeStruct((6 * rows, width), F32)
    dq_shape = jax.ShapeDtypeStruct((n_q, width), F32)
    col_outs = [(0, 0), (0, rows), (0, 2 * rows)]
    side_outs = col_outs + [(1, 0), (1, rows), (1, 2 * rows)]
    part_left, part_right, dq_side = call(
        functools.partial(grads_kernel, side_blocks, side_slots, side_outs, True),
        (part_shape, part_shape, dq_shape),
        bias, lse, q, g, *pieces, k_left, k_right, v_left, v_right,
    )
    back_left = moved(part_left, "ha", left)
    back_right = moved(part_right, "ha", right)
    part_mid, dq = call(
        functools.partial(grads_kernel, col_blocks, mid_slots, col_outs, False),
        (mid_shape, dq_shape),
        bias, lse, q, g, *pieces, k_col, v_col, dq_side,
    )
    dq_parts = dq.reshape(n_ta, rows, width)
    dq_back = [
        moved(dq_parts[d].astype(BF16), "ta", [(i, (i - d) % n_ta) for i in range(n_ta)])
        for d in range(1, n_ta)
    ]
    total = part_mid + back_left.astype(F32) + back_right.astype(F32)
    total = total.reshape(2, 3, rows, width)
    from_down = moved(total[:, 0].astype(BF16), "ha", up)
    from_up = moved(total[:, 2].astype(BF16), "ha", down)
    whole = (total[:, 1] + from_down.astype(F32) + from_up.astype(F32)).astype(BF16)
    query_grad = (dq_parts[0] + sum(x.astype(F32) for x in dq_back)).astype(BF16)
    shape = query_in.shape
    return query_grad.reshape(shape), whole[0].reshape(shape), whole[1].reshape(shape)


def solution(mesh):
    spec = P("ta", "ha", None, None, "ga")
    return jax.shard_map(
        local,
        mesh=mesh,
        in_specs=(spec,) * 5 + (P(),),
        out_specs=(spec,) * 3,
        check_vma=False,
    )
```

time: 481 us -> 92 us (0.19)
  the two profiles are of different devices: /device:TPU:65 before, /device:TPU:163 now
where the time goes in v1:
time: 92 us; the launch traced here: 91.5 us
  starting transfers between devices  49.8 us (54%)
  waiting for transfers between devices  23.1 us (25%)
  Pallas kernels  12.6 us (14%)
  other arithmetic  3.94 us (4%)
  local copies, waits for them, and re-layouts  1.02 us (1%)
  between operations  0.99 us (1%)
    ppermute x21, starting transfers between devices, moved(): return lax.ppermute(block, axis, route)  49.8 us
    ppermute x21, waiting for transfers between devices, moved(): return lax.ppermute(block, axis, route)  23.1 us
    pallas_call x5, Pallas kernels, call(): pl.pallas_call(kernel, out_shape=out_shape, in_specs=[vmem] * len(args),...  12.6 us
  transfers between devices with their start and end apart: 21, of which 6 were waited for; matrix products, arithmetic and copies ran while one was open for 5% of the time, Pallas kernels for 7%

profile of v1, /device:TPU:163, one launch (start us, length us, event | category | flops | bytes accessed | tf_op | source)
XLA Modules:
  0.0 91.5 jit_solution(17582770124524903975)
XLA Ops:
  0.6 0.0 copy-start
  0.7 2.3 %collective-permute-start.4 = (bf16[192,256]{1,0:T(8,128)(2,1)}, bf16[192,256]{1,0:T(8,128)(2,1)S(1)}, u32[]{:S(2)}, u32[]{:S(2)}) collective-permute-start(bf16[192,256]{1,0:T(8,128)(2,1)} %bitcast.47), channel_id=1, source_target_pairs={{16,0},{18,2},{20,4},{22,6},{24,8},{26,10},{28,12},{30,14},{32,16}... | collective-permute-start | bytes 294920 | tf_op jit(solution)/shard_map/ppermute | solution.py:27
  3.0 4.0 %collective-permute-start.3 = (bf16[192,256]{1,0:T(8,128)(2,1)}, bf16[192,256]{1,0:T(8,128)(2,1)S(1)}, u32[]{:S(2)}, u32[]{:S(2)}) collective-permute-start(bf16[192,256]{1,0:T(8,128)(2,1)} %bitcast.48), channel_id=1, source_target_pairs={{0,16},{2,18},{4,20},{6,22},{8,24},{10,26},{12,28},{14,30},{16,32}... | collective-permute-start | bytes 294920 | tf_op jit(solution)/shard_map/ppermute | solution.py:27
  7.0 3.4 %collective-permute-start.11 = (bf16[192,256]{1,0:T(8,128)(2,1)}, bf16[192,256]{1,0:T(8,128)(2,1)S(1)}, u32[]{:S(2)}, u32[]{:S(2)}) collective-permute-start(bf16[192,256]{1,0:T(8,128)(2,1)} %bitcast.44), channel_id=1, source_target_pairs={{16,0},{18,2},{20,4},{22,6},{24,8},{26,10},{28,12},{30,14},{32,16}... | collective-permute-start | bytes 294920 | tf_op jit(solution)/shard_map/ppermute | solution.py:27
  10.4 2.8 %collective-permute-start.10 = (bf16[192,256]{1,0:T(8,128)(2,1)}, bf16[192,256]{1,0:T(8,128)(2,1)S(1)}, u32[]{:S(2)}, u32[]{:S(2)}) collective-permute-start(bf16[192,256]{1,0:T(8,128)(2,1)} %bitcast.45), channel_id=1, source_target_pairs={{0,16},{2,18},{4,20},{6,22},{8,24},{10,26},{12,28},{14,30},{16,32}... | collective-permute-start | bytes 294920 | tf_op jit(solution)/shard_map/ppermute | solution.py:27
  13.2 1.0 %pad_maximum_fusion.2 = bf16[384,256]{1,0:T(8,128)(2,1)S(1)} fusion(bf16[192,256]{1,0:T(8,128)(2,1)} %bitcast.37, bf16[192,256]{1,0:T(8,128)(2,1)} %bitcast.32), kind=kLoop, calls=%fused_computation.9 | loop fusion | flops 393216 | bytes 393216 | tf_op jit(solution)/shard_map/concatenate | solution.py:170
  14.2 0.3 collective-permute-start.2
  14.6 0.1 fusion.7
  14.7 0.0 collective-permute-done.11
  14.7 2.2 %collective-permute-start.1 = (bf16[384,256]{1,0:T(8,128)(2,1)S(1)}, bf16[384,256]{1,0:T(8,128)(2,1)S(1)}, u32[]{:S(2)}, u32[]{:S(2)}) collective-permute-start(bf16[384,256]{1,0:T(8,128)(2,1)S(1)} %pad_maximum_fusion.2), channel_id=1, source_target_pairs={{0,128},{64,192},{128,0},{192,64},{1,129},{65,193},{129,1},{193,65... | collective-permute-start | bytes 589832 | tf_op jit(solution)/shard_map/ppermute | solution.py:27
  16.9 2.7 %collective-permute-done.10 = bf16[192,256]{1,0:T(8,128)(2,1)S(1)} collective-permute-done((bf16[192,256]{1,0:T(8,128)(2,1)}, bf16[192,256]{1,0:T(8,128)(2,1)S(1)}, u32[]{:S(2)}, u32[]{:S(2)}) %collective-permute-start.10) | collective-permute-done | bytes 98336 | tf_op jit(solution)/shard_map/ppermute | solution.py:27
  19.5 0.9 pad_maximum_fusion.1.refs_8_
  20.4 4.3 %collective-permute-start.13 = (bf16[576,256]{1,0:T(8,128)(2,1)S(1)}, bf16[576,256]{1,0:T(8,128)(2,1)S(1)}, u32[]{:S(2)}, u32[]{:S(2)}) collective-permute-start(bf16[576,256]{1,0:T(8,128)(2,1)S(1)} %pad_maximum_fusion.1.refs_8_), channel_id=1, source_target_pairs={{2,0},{4,2},{6,4},{8,6},{10,8},{12,10},{14,12},{18,16},{20,18},{22... | collective-permute-start | bytes 884744 | tf_op jit(solution)/shard_map/ppermute | solution.py:27
  24.8 3.1 %collective-permute-start.12 = (bf16[576,256]{1,0:T(8,128)(2,1)S(1)}, bf16[576,256]{1,0:T(8,128)(2,1)S(1)}, u32[]{:S(2)}, u32[]{:S(2)}) collective-permute-start(bf16[576,256]{1,0:T(8,128)(2,1)S(1)} %pad_maximum_fusion.1.refs_8_), channel_id=1, source_target_pairs={{0,2},{2,4},{4,6},{6,8},{8,10},{10,12},{12,14},{16,18},{18,20},{20... | collective-permute-start | bytes 884744 | tf_op jit(solution)/shard_map/ppermute | solution.py:27
  27.9 0.9 %pad_maximum_fusion.refs_7_ = bf16[576,256]{1,0:T(8,128)(2,1)S(1)} fusion(bf16[192,256]{1,0:T(8,128)(2,1)S(1)} %collective-permute-done.4, bf16[192,256]{1,0:T(8,128)(2,1)} %bitcast.49, bf16[192,256]{1,0:T(8,128)(2,1)S(1)} %collective-permute-done.3), kind=kLoop, calls=%fused_computation.5 | loop fusion | flops 884736 | bytes 589824 | tf_op jit(solution)/shard_map/concatenate | solution.py:174
  28.8 1.9 %collective-permute-start.6 = (bf16[576,256]{1,0:T(8,128)(2,1)S(1)}, bf16[576,256]{1,0:T(8,128)(2,1)S(1)}, u32[]{:S(2)}, u32[]{:S(2)}) collective-permute-start(bf16[576,256]{1,0:T(8,128)(2,1)S(1)} %pad_maximum_fusion.refs_7_), channel_id=1, source_target_pairs={{2,0},{4,2},{6,4},{8,6},{10,8},{12,10},{14,12},{18,16},{20,18},{22... | collective-permute-start | bytes 884744 | tf_op jit(solution)/shard_map/ppermute | solution.py:27
  30.8 0.0 collective-permute-done.2.refs_6_.refs_5_
  30.8 3.6 %collective-permute-start.5 = (bf16[576,256]{1,0:T(8,128)(2,1)S(1)}, bf16[576,256]{1,0:T(8,128)(2,1)S(1)}, u32[]{:S(2)}, u32[]{:S(2)}) collective-permute-start(bf16[576,256]{1,0:T(8,128)(2,1)S(1)} %pad_maximum_fusion.refs_7_), channel_id=1, source_target_pairs={{0,2},{2,4},{4,6},{6,8},{8,10},{10,12},{12,14},{16,18},{18,20},{20... | collective-permute-start | bytes 884744 | tf_op jit(solution)/shard_map/ppermute | solution.py:27
  34.4 0.0 collective-permute-done.1.refs_5_.refs_4_
  34.4 1.3 %collective-permute-start = (bf16[384,256]{1,0:T(8,128)(2,1)S(1)}, bf16[384,256]{1,0:T(8,128)(2,1)S(1)}, u32[]{:S(2)}, u32[]{:S(2)}) collective-permute-start(bf16[384,256]{1,0:T(8,128)(2,1)S(1)} %pad_maximum_fusion.2), channel_id=1, source_target_pairs={{0,64},{64,128},{128,192},{192,0},{1,65},{65,129},{129,193},{193,1... | collective-permute-start | bytes 589832 | tf_op jit(solution)/shard_map/ppermute | solution.py:27
  35.7 0.1 fusion.4
  35.8 0.1 broadcast_in_dim.56
  35.9 0.1 reshape.110.refs_0_
  36.0 5.3 %collective-permute-done.refs_4_.refs_3_ = bf16[384,256]{1,0:T(8,128)(2,1)S(1)} collective-permute-done((bf16[384,256]{1,0:T(8,128)(2,1)S(1)}, bf16[384,256]{1,0:T(8,128)(2,1)S(1)}, u32[]{:S(2)}, u32[]{:S(2)}) %collective-permute-start) | collective-permute-done | bytes 196640 | tf_op jit(solution)/shard_map/ppermute | solution.py:27
  41.3 1.3 %shard_map.85.refs_1_ = f32[8,768]{1,0:T(8,128)S(1)} custom-call(f32[16,768]{1,0:T(8,128)S(1)} %reshape.110.refs_0_, bf16[192,256]{1,0:T(8,128)(2,1)S(1)} %bitcast.33, bf16[192,256]{1,0:T(8,128)(2,1)S(1)} %bitcast.41, bf16[192,256]{1,0:T(8,128)(2,1)S(1)} %bitcast.38, bf16[384,256]{1,0:T(8,128)(2,1)S(1)} %collective-permute-done.refs_4_.refs_3_, ...), custom_call_target="tpu_custom_call" | custom-call | tf_op jit(solution)/shard_map/pallas_call | solution.py:139
  42.6 2.1 %shard_map.86.refs_0_ = f32[8,768]{1,0:T(8,128)S(1)} custom-call(f32[16,768]{1,0:T(8,128)S(1)} %reshape.110.refs_0_, f32[8,768]{1,0:T(8,128)S(1)} %shard_map.85.refs_1_, bf16[192,256]{1,0:T(8,128)(2,1)S(1)} %bitcast.34, bf16[384,256]{1,0:T(8,128)(2,1)S(1)} %collective-permute-done.refs_4_.refs_3_, ...), custom_call_target="tpu_custom_call" | custom-call | tf_op jit(solution)/shard_map/pallas_call | solution.py:139
  44.7 1.5 %collective-permute-start.9 = (f32[8,768]{1,0:T(8,128)S(1)}, f32[8,768]{1,0:T(8,128)S(1)}, u32[]{:S(2)}, u32[]{:S(2)}) collective-permute-start(f32[8,768]{1,0:T(8,128)S(1)} %shard_map.86.refs_0_), channel_id=1, source_target_pairs={{0,192},{64,0},{128,64},{192,128},{1,193},{65,1},{129,65},{193,129... | collective-permute-start | bytes 73736 | tf_op jit(solution)/shard_map/ppermute | solution.py:27
  46.3 0.9 %collective-permute-start.8 = (f32[8,768]{1,0:T(8,128)S(1)}, f32[8,768]{1,0:T(8,128)S(1)}, u32[]{:S(2)}, u32[]{:S(2)}) collective-permute-start(f32[8,768]{1,0:T(8,128)S(1)} %shard_map.86.refs_0_), channel_id=1, source_target_pairs={{0,128},{64,192},{128,0},{192,64},{1,129},{65,193},{129,1},{193,65... | collective-permute-start | bytes 73736 | tf_op jit(solution)/shard_map/ppermute | solution.py:27
  47.2 1.5 %collective-permute-start.7 = (f32[8,768]{1,0:T(8,128)S(1)}, f32[8,768]{1,0:T(8,128)S(1)}, u32[]{:S(2)}, u32[]{:S(2)}) collective-permute-start(f32[8,768]{1,0:T(8,128)S(1)} %shard_map.86.refs_0_), channel_id=1, source_target_pairs={{0,64},{64,128},{128,192},{192,0},{1,65},{65,129},{129,193},{193,1... | collective-permute-start | bytes 73736 | tf_op jit(solution)/shard_map/ppermute | solution.py:27
  48.7 0.0 collective-permute-done.9.refs_3_
  48.7 1.7 %collective-permute-done.8.refs_2_ = f32[8,768]{1,0:T(8,128)S(1)} collective-permute-done((f32[8,768]{1,0:T(8,128)S(1)}, f32[8,768]{1,0:T(8,128)S(1)}, u32[]{:S(2)}, u32[]{:S(2)}) %collective-permute-start.8) | collective-permute-done | bytes 24608 | tf_op jit(solution)/shard_map/ppermute | solution.py:27
  50.5 0.1 shard_map.87.refs_1_
  50.6 5.9 %shard_map.88 = (bf16[1152,256]{1,0:T(8,128)(2,1)S(1)}, bf16[1152,256]{1,0:T(8,128)(2,1)S(1)}, f32[768,256]{1,0:T(8,128)S(1)}) custom-call(f32[16,768]{1,0:T(8,128)S(1)} %reshape.110.refs_0_, f32[8,768]{1,0:T(8,128)S(1)} %shard_map.87.refs_1_, bf16[192,256]{1,0:T(8,128)(2,1)S(1)} %bitcast.35, bf16[192,256]{1,0:T(8,128)(2,1)S(1)} %bitcast.39, ...), custom_call_target="tpu_custom_call" | custom-call | tf_op jit(solution)/shard_map/pallas_call | solution.py:139
  56.5 3.9 %collective-permute-start.17 = (bf16[1152,256]{1,0:T(8,128)(2,1)S(1)}, bf16[1152,256]{1,0:T(8,128)(2,1)S(1)}, u32[]{:S(2)}, u32[]{:S(2)}) collective-permute-start(bf16[1152,256]{1,0:T(8,128)(2,1)S(1)} %get-tuple-element.11), channel_id=1, source_target_pairs={{2,0},{4,2},{6,4},{8,6},{10,8},{12,10},{14,12},{18,16},{20,18},{22... | collective-permute-start | bytes 1769480 | tf_op jit(solution)/shard_map/ppermute | solution.py:27
  60.4 1.9 %collective-permute-start.18 = (bf16[1152,256]{1,0:T(8,128)(2,1)S(1)}, bf16[1152,256]{1,0:T(8,128)(2,1)S(1)}, u32[]{:S(2)}, u32[]{:S(2)}) collective-permute-start(bf16[1152,256]{1,0:T(8,128)(2,1)S(1)} %get-tuple-element.12), channel_id=1, source_target_pairs={{0,2},{2,4},{4,6},{6,8},{8,10},{10,12},{12,14},{16,18},{18,20},{20... | collective-permute-start | bytes 1769480 | tf_op jit(solution)/shard_map/ppermute | solution.py:27
  62.4 3.2 %shard_map.89 = (f32[1152,256]{1,0:T(8,128)S(1)}, f32[768,256]{1,0:T(8,128)S(1)}) custom-call(f32[16,768]{1,0:T(8,128)S(1)} %reshape.110.refs_0_, f32[8,768]{1,0:T(8,128)S(1)} %shard_map.87.refs_1_, bf16[192,256]{1,0:T(8,128)(2,1)S(1)} %bitcast.36, bf16[192,256]{1,0:T(8,128)(2,1)S(1)} %bitcast.40, bf16[384,256]{1,0:T(8,128)(2,1)S(1)} %collective-permute-done.refs_4_.refs_3_, ...), custom_call_target="tpu_custom_call" | custom-call | tf_op jit(solution)/shard_map/pallas_call | solution.py:139
  65.6 1.9 %collective-permute-start.14 = (bf16[192,256]{1,0:T(8,128)(2,1)S(1)}, bf16[192,256]{1,0:T(8,128)(2,1)S(1)}, u32[]{:S(2)}, u32[]{:S(2)}) collective-permute-start(bf16[192,256]{1,0:T(8,128)(2,1)S(1)} %get-tuple-element.18), channel_id=1, source_target_pairs={{0,192},{64,0},{128,64},{192,128},{1,193},{65,1},{129,65},{193,129... | collective-permute-start | bytes 294920 | tf_op jit(solution)/shard_map/ppermute | solution.py:27
  67.4 2.6 %collective-permute-start.15 = (bf16[192,256]{1,0:T(8,128)(2,1)S(1)}, bf16[192,256]{1,0:T(8,128)(2,1)S(1)}, u32[]{:S(2)}, u32[]{:S(2)}) collective-permute-start(bf16[192,256]{1,0:T(8,128)(2,1)S(1)} %get-tuple-element.20), channel_id=1, source_target_pairs={{0,128},{64,192},{128,0},{192,64},{1,129},{65,193},{129,1},{193,65... | collective-permute-start | bytes 294920 | tf_op jit(solution)/shard_map/ppermute | solution.py:27
  70.1 3.9 %collective-permute-done.17 = bf16[1152,256]{1,0:T(8,128)(2,1)S(1)} collective-permute-done((bf16[1152,256]{1,0:T(8,128)(2,1)S(1)}, bf16[1152,256]{1,0:T(8,128)(2,1)S(1)}, u32[]{:S(2)}, u32[]{:S(2)}) %collective-permute-start.17) | collective-permute-done | bytes 589856 | tf_op jit(solution)/shard_map/ppermute | solution.py:27
  74.0 0.2 convert_add_fusion
  74.2 0.1 convert.10
  74.3 2.5 %collective-permute-start.19 = (bf16[2,192,256]{2,1,0:T(8,128)(2,1)S(1)}, bf16[2,192,256]{2,1,0:T(8,128)(2,1)S(1)}, u32[]{:S(2)}, u32[]{:S(2)}) collective-permute-start(bf16[2,192,256]{2,1,0:T(8,128)(2,1)S(1)} %get-tuple-element.16), channel_id=1, source_target_pairs={{16,0},{18,2},{20,4},{22,6},{24,8},{26,10},{28,12},{30,14},{32,16}... | collective-permute-start | bytes 589832 | tf_op jit(solution)/shard_map/ppermute | solution.py:27
  76.8 3.7 %collective-permute-start.20 = (bf16[2,192,256]{2,1,0:T(8,128)(2,1)S(1)}, bf16[2,192,256]{2,1,0:T(8,128)(2,1)S(1)}, u32[]{:S(2)}, u32[]{:S(2)}) collective-permute-start(bf16[2,192,256]{2,1,0:T(8,128)(2,1)S(1)} %get-tuple-element.17), channel_id=1, source_target_pairs={{0,16},{2,18},{4,20},{6,22},{8,24},{10,26},{12,28},{14,30},{16,32}... | collective-permute-start | bytes 589832 | tf_op jit(solution)/shard_map/ppermute | solution.py:27
  80.5 0.7 add_convert_fusion
  81.2 1.9 %collective-permute-done.19 = bf16[2,192,256]{2,1,0:T(8,128)(2,1)S(1)} collective-permute-done((bf16[2,192,256]{2,1,0:T(8,128)(2,1)S(1)}, bf16[2,192,256]{2,1,0:T(8,128)(2,1)S(1)}, u32[]{:S(2)}, u32[]{:S(2)}) %collective-permute-start.19) | collective-permute-done | bytes 196640 | tf_op jit(solution)/shard_map/ppermute | solution.py:27
  83.1 7.6 %collective-permute-done.20 = bf16[2,192,256]{2,1,0:T(8,128)(2,1)S(1)} collective-permute-done((bf16[2,192,256]{2,1,0:T(8,128)(2,1)S(1)}, bf16[2,192,256]{2,1,0:T(8,128)(2,1)S(1)}, u32[]{:S(2)}, u32[]{:S(2)}) %collective-permute-start.20) | collective-permute-done | bytes 196640 | tf_op jit(solution)/shard_map/ppermute | solution.py:27
  90.7 0.1 fusion.2
  90.8 0.7 fusion.14
  (25 shorter events, 0.2 us)
Async XLA Ops:
  0.6 13.9 %copy-start = (s32[2,4,8,27]{3,2,1,0:T(8,128)S(1)}, s32[2,4,8,27]{3,2,1,0:T(8,128)}, u32[]{:S(2)}) copy-start(s32[2,4,8,27]{3,2,1,0:T(8,128)} %param.11) | copy-start | bytes 20740
  0.6 40.6 %copy-start.2 = (bf16[3,1,8,8,256]{4,3,2,1,0:T(8,128)(2,1)S(1)}, bf16[3,1,8,8,256]{4,3,2,1,0:T(8,128)(2,1)}, u32[]{:S(2)}) copy-start(bf16[3,1,8,8,256]{4,3,2,1,0:T(8,128)(2,1)} %param.10) | copy-start | bytes 294916
  0.7 40.6 %copy-start.1 = (bf16[3,1,8,8,256]{4,3,2,1,0:T(8,128)(2,1)S(1)}, bf16[3,1,8,8,256]{4,3,2,1,0:T(8,128)(2,1)}, u32[]{:S(2)}) copy-start(bf16[3,1,8,8,256]{4,3,2,1,0:T(8,128)(2,1)} %param.6) | copy-start | bytes 294916
  0.7 40.6 %copy-start.3 = (bf16[3,1,8,8,256]{4,3,2,1,0:T(8,128)(2,1)S(1)}, bf16[3,1,8,8,256]{4,3,2,1,0:T(8,128)(2,1)}, u32[]{:S(2)}) copy-start(bf16[3,1,8,8,256]{4,3,2,1,0:T(8,128)(2,1)} %param.9) | copy-start | bytes 294916
  0.7 24.1 %collective-permute-start.4 = (bf16[192,256]{1,0:T(8,128)(2,1)}, bf16[192,256]{1,0:T(8,128)(2,1)S(1)}, u32[]{:S(2)}, u32[]{:S(2)}) collective-permute-start(bf16[192,256]{1,0:T(8,128)(2,1)} %bitcast.47), channel_id=1, source_target_pairs={{16,0},{18,2},{20,4},{22,6},{24,8},{26,10},{28,12},{30,14},{32,16}... | collective-permute-start | bytes 294920 | tf_op jit(solution)/shard_map/ppermute | solution.py:27
  3.0 24.9 %collective-permute-start.3 = (bf16[192,256]{1,0:T(8,128)(2,1)}, bf16[192,256]{1,0:T(8,128)(2,1)S(1)}, u32[]{:S(2)}, u32[]{:S(2)}) collective-permute-start(bf16[192,256]{1,0:T(8,128)(2,1)} %bitcast.48), channel_id=1, source_target_pairs={{0,16},{2,18},{4,20},{6,22},{8,24},{10,26},{12,28},{14,30},{16,32}... | collective-permute-start | bytes 294920 | tf_op jit(solution)/shard_map/ppermute | solution.py:27
  7.0 7.7 %collective-permute-start.11 = (bf16[192,256]{1,0:T(8,128)(2,1)}, bf16[192,256]{1,0:T(8,128)(2,1)S(1)}, u32[]{:S(2)}, u32[]{:S(2)}) collective-permute-start(bf16[192,256]{1,0:T(8,128)(2,1)} %bitcast.44), channel_id=1, source_target_pairs={{16,0},{18,2},{20,4},{22,6},{24,8},{26,10},{28,12},{30,14},{32,16}... | collective-permute-start | bytes 294920 | tf_op jit(solution)/shard_map/ppermute | solution.py:27
  10.4 9.1 %collective-permute-start.10 = (bf16[192,256]{1,0:T(8,128)(2,1)}, bf16[192,256]{1,0:T(8,128)(2,1)S(1)}, u32[]{:S(2)}, u32[]{:S(2)}) collective-permute-start(bf16[192,256]{1,0:T(8,128)(2,1)} %bitcast.45), channel_id=1, source_target_pairs={{0,16},{2,18},{4,20},{6,22},{8,24},{10,26},{12,28},{14,30},{16,32}... | collective-permute-start | bytes 294920 | tf_op jit(solution)/shard_map/ppermute | solution.py:27
  14.2 16.6 %collective-permute-start.2 = (bf16[384,256]{1,0:T(8,128)(2,1)S(1)}, bf16[384,256]{1,0:T(8,128)(2,1)S(1)}, u32[]{:S(2)}, u32[]{:S(2)}) collective-permute-start(bf16[384,256]{1,0:T(8,128)(2,1)S(1)} %pad_maximum_fusion.2), channel_id=1, source_target_pairs={{0,192},{64,0},{128,64},{192,128},{1,193},{65,1},{129,65},{193,129... | collective-permute-start | bytes 589832 | tf_op jit(solution)/shard_map/ppermute | solution.py:27
  14.7 19.8 %collective-permute-start.1 = (bf16[384,256]{1,0:T(8,128)(2,1)S(1)}, bf16[384,256]{1,0:T(8,128)(2,1)S(1)}, u32[]{:S(2)}, u32[]{:S(2)}) collective-permute-start(bf16[384,256]{1,0:T(8,128)(2,1)S(1)} %pad_maximum_fusion.2), channel_id=1, source_target_pairs={{0,128},{64,192},{128,0},{192,64},{1,129},{65,193},{129,1},{193,65... | collective-permute-start | bytes 589832 | tf_op jit(solution)/shard_map/ppermute | solution.py:27
  20.4 30.1 %collective-permute-start.13 = (bf16[576,256]{1,0:T(8,128)(2,1)S(1)}, bf16[576,256]{1,0:T(8,128)(2,1)S(1)}, u32[]{:S(2)}, u32[]{:S(2)}) collective-permute-start(bf16[576,256]{1,0:T(8,128)(2,1)S(1)} %pad_maximum_fusion.1.refs_8_), channel_id=1, source_target_pairs={{2,0},{4,2},{6,4},{8,6},{10,8},{12,10},{14,12},{18,16},{20,18},{22... | collective-permute-start | bytes 884744 | tf_op jit(solution)/shard_map/ppermute | solution.py:27
  24.8 25.8 %collective-permute-start.12 = (bf16[576,256]{1,0:T(8,128)(2,1)S(1)}, bf16[576,256]{1,0:T(8,128)(2,1)S(1)}, u32[]{:S(2)}, u32[]{:S(2)}) collective-permute-start(bf16[576,256]{1,0:T(8,128)(2,1)S(1)} %pad_maximum_fusion.1.refs_8_), channel_id=1, source_target_pairs={{0,2},{2,4},{4,6},{6,8},{8,10},{10,12},{12,14},{16,18},{18,20},{20... | collective-permute-start | bytes 884744 | tf_op jit(solution)/shard_map/ppermute | solution.py:27
  28.8 13.8 %collective-permute-start.6 = (bf16[576,256]{1,0:T(8,128)(2,1)S(1)}, bf16[576,256]{1,0:T(8,128)(2,1)S(1)}, u32[]{:S(2)}, u32[]{:S(2)}) collective-permute-start(bf16[576,256]{1,0:T(8,128)(2,1)S(1)} %pad_maximum_fusion.refs_7_), channel_id=1, source_target_pairs={{2,0},{4,2},{6,4},{8,6},{10,8},{12,10},{14,12},{18,16},{20,18},{22... | collective-permute-start | bytes 884744 | tf_op jit(solution)/shard_map/ppermute | solution.py:27
  30.8 11.8 %collective-permute-start.5 = (bf16[576,256]{1,0:T(8,128)(2,1)S(1)}, bf16[576,256]{1,0:T(8,128)(2,1)S(1)}, u32[]{:S(2)}, u32[]{:S(2)}) collective-permute-start(bf16[576,256]{1,0:T(8,128)(2,1)S(1)} %pad_maximum_fusion.refs_7_), channel_id=1, source_target_pairs={{0,2},{2,4},{4,6},{6,8},{8,10},{10,12},{12,14},{16,18},{18,20},{20... | collective-permute-start | bytes 884744 | tf_op jit(solution)/shard_map/ppermute | solution.py:27
  34.4 6.8 %collective-permute-start = (bf16[384,256]{1,0:T(8,128)(2,1)S(1)}, bf16[384,256]{1,0:T(8,128)(2,1)S(1)}, u32[]{:S(2)}, u32[]{:S(2)}) collective-permute-start(bf16[384,256]{1,0:T(8,128)(2,1)S(1)} %pad_maximum_fusion.2), channel_id=1, source_target_pairs={{0,64},{64,128},{128,192},{192,0},{1,65},{65,129},{129,193},{193,1... | collective-permute-start | bytes 589832 | tf_op jit(solution)/shard_map/ppermute | solution.py:27
  44.7 4.0 %collective-permute-start.9 = (f32[8,768]{1,0:T(8,128)S(1)}, f32[8,768]{1,0:T(8,128)S(1)}, u32[]{:S(2)}, u32[]{:S(2)}) collective-permute-start(f32[8,768]{1,0:T(8,128)S(1)} %shard_map.86.refs_0_), channel_id=1, source_target_pairs={{0,192},{64,0},{128,64},{192,128},{1,193},{65,1},{129,65},{193,129... | collective-permute-start | bytes 73736 | tf_op jit(solution)/shard_map/ppermute | solution.py:27
  46.3 4.2 %collective-permute-start.8 = (f32[8,768]{1,0:T(8,128)S(1)}, f32[8,768]{1,0:T(8,128)S(1)}, u32[]{:S(2)}, u32[]{:S(2)}) collective-permute-start(f32[8,768]{1,0:T(8,128)S(1)} %shard_map.86.refs_0_), channel_id=1, source_target_pairs={{0,128},{64,192},{128,0},{192,64},{1,129},{65,193},{129,1},{193,65... | collective-permute-start | bytes 73736 | tf_op jit(solution)/shard_map/ppermute | solution.py:27
  47.2 3.3 %collective-permute-start.7 = (f32[8,768]{1,0:T(8,128)S(1)}, f32[8,768]{1,0:T(8,128)S(1)}, u32[]{:S(2)}, u32[]{:S(2)}) collective-permute-start(f32[8,768]{1,0:T(8,128)S(1)} %shard_map.86.refs_0_), channel_id=1, source_target_pairs={{0,64},{64,128},{128,192},{192,0},{1,65},{65,129},{129,193},{193,1... | collective-permute-start | bytes 73736 | tf_op jit(solution)/shard_map/ppermute | solution.py:27
  56.5 17.5 %collective-permute-start.17 = (bf16[1152,256]{1,0:T(8,128)(2,1)S(1)}, bf16[1152,256]{1,0:T(8,128)(2,1)S(1)}, u32[]{:S(2)}, u32[]{:S(2)}) collective-permute-start(bf16[1152,256]{1,0:T(8,128)(2,1)S(1)} %get-tuple-element.11), channel_id=1, source_target_pairs={{2,0},{4,2},{6,4},{8,6},{10,8},{12,10},{14,12},{18,16},{20,18},{22... | collective-permute-start | bytes 1769480 | tf_op jit(solution)/shard_map/ppermute | solution.py:27
  60.4 13.6 %collective-permute-start.18 = (bf16[1152,256]{1,0:T(8,128)(2,1)S(1)}, bf16[1152,256]{1,0:T(8,128)(2,1)S(1)}, u32[]{:S(2)}, u32[]{:S(2)}) collective-permute-start(bf16[1152,256]{1,0:T(8,128)(2,1)S(1)} %get-tuple-element.12), channel_id=1, source_target_pairs={{0,2},{2,4},{4,6},{6,8},{8,10},{10,12},{12,14},{16,18},{18,20},{20... | collective-permute-start | bytes 1769480 | tf_op jit(solution)/shard_map/ppermute | solution.py:27
  65.6 14.9 %collective-permute-start.14 = (bf16[192,256]{1,0:T(8,128)(2,1)S(1)}, bf16[192,256]{1,0:T(8,128)(2,1)S(1)}, u32[]{:S(2)}, u32[]{:S(2)}) collective-permute-start(bf16[192,256]{1,0:T(8,128)(2,1)S(1)} %get-tuple-element.18), channel_id=1, source_target_pairs={{0,192},{64,0},{128,64},{192,128},{1,193},{65,1},{129,65},{193,129... | collective-permute-start | bytes 294920 | tf_op jit(solution)/shard_map/ppermute | solution.py:27
  67.4 13.1 %collective-permute-start.16 = (bf16[192,256]{1,0:T(8,128)(2,1)S(1)}, bf16[192,256]{1,0:T(8,128)(2,1)S(1)}, u32[]{:S(2)}, u32[]{:S(2)}) collective-permute-start(bf16[192,256]{1,0:T(8,128)(2,1)S(1)} %get-tuple-element.19), channel_id=1, source_target_pairs={{0,64},{64,128},{128,192},{192,0},{1,65},{65,129},{129,193},{193,1... | collective-permute-start | bytes 294920 | tf_op jit(solution)/shard_map/ppermute | solution.py:27
  67.4 13.1 %collective-permute-start.15 = (bf16[192,256]{1,0:T(8,128)(2,1)S(1)}, bf16[192,256]{1,0:T(8,128)(2,1)S(1)}, u32[]{:S(2)}, u32[]{:S(2)}) collective-permute-start(bf16[192,256]{1,0:T(8,128)(2,1)S(1)} %get-tuple-element.20), channel_id=1, source_target_pairs={{0,128},{64,192},{128,0},{192,64},{1,129},{65,193},{129,1},{193,65... | collective-permute-start | bytes 294920 | tf_op jit(solution)/shard_map/ppermute | solution.py:27
  74.3 8.9 %collective-permute-start.19 = (bf16[2,192,256]{2,1,0:T(8,128)(2,1)S(1)}, bf16[2,192,256]{2,1,0:T(8,128)(2,1)S(1)}, u32[]{:S(2)}, u32[]{:S(2)}) collective-permute-start(bf16[2,192,256]{2,1,0:T(8,128)(2,1)S(1)} %get-tuple-element.16), channel_id=1, source_target_pairs={{16,0},{18,2},{20,4},{22,6},{24,8},{26,10},{28,12},{30,14},{32,16}... | collective-permute-start | bytes 589832 | tf_op jit(solution)/shard_map/ppermute | solution.py:27
  76.8 13.9 %collective-permute-start.20 = (bf16[2,192,256]{2,1,0:T(8,128)(2,1)S(1)}, bf16[2,192,256]{2,1,0:T(8,128)(2,1)S(1)}, u32[]{:S(2)}, u32[]{:S(2)}) collective-permute-start(bf16[2,192,256]{2,1,0:T(8,128)(2,1)S(1)} %get-tuple-element.17), channel_id=1, source_target_pairs={{0,16},{2,18},{4,20},{6,22},{8,24},{10,26},{12,28},{14,30},{16,32}... | collective-permute-start | bytes 589832 | tf_op jit(solution)/shard_map/ppermute | solution.py:27

commit v2 on v1

v2 whole, which is shorter than its diff:
```python
import functools

import jax
import jax.numpy as jnp
from jax import lax
from jax.experimental import pallas as pl
from jax.experimental.pallas import tpu as pltpu
from jax.sharding import PartitionSpec as P

HEAD_DIM = 128
TILE_T = 6
CLOSED = 1e30
SCALE = HEAD_DIM ** (-0.5)
SCALE2 = SCALE * 1.4426950408889634
F32 = jnp.float32
BF16 = jnp.bfloat16
NT = (((1,), (1,)), ((), ()))
NN = (((1,), (0,)), ((), ()))
TN = (((0,), (0,)), ((), ()))


def dot(a, b, dims, precision=None):
    return lax.dot_general(a, b, dims, precision=precision, preferred_element_type=F32)


def head_cols(head):
    return pl.ds(head * HEAD_DIM, HEAD_DIM)


def gathered(piece_refs, half, head):
    rows = piece_refs[0].shape[0] // 2
    return jnp.concatenate(
        [r[pl.ds(half * rows, rows), head_cols(head)] for r in piece_refs], axis=0
    )


def stack_kernel(rows, *refs):
    *parts, out_ref = refs
    for half in range(2):
        for i, ref in enumerate(parts):
            out_ref[pl.ds((3 * half + i) * rows, rows), :] = ref[pl.ds(half * rows, rows), :]


def scores_kernel(position, *refs):
    bias_ref, *refs = refs
    *pieces, kv_ref, weights_ref, stats_ref = refs
    heads = pieces[0].shape[1] // HEAD_DIM
    rows = pieces[0].shape[0] // 2
    stats_ref[...] = jnp.zeros_like(stats_ref)
    for head in range(heads):
        cols = head_cols(head)
        query = gathered(pieces, 0, head)
        scores = []
        tops = []
        for row in range(3):
            key = kv_ref[pl.ds(row * rows, rows), cols]
            at = 3 * position + row
            s = dot(key, query, NT)
            scores.append(s)
            tops.append(jnp.max(s, axis=0, keepdims=True) * SCALE2 - bias_ref[at : at + 1, :])
        top = jnp.maximum(functools.reduce(jnp.maximum, tops), -0.5 * CLOSED)
        total = jnp.zeros_like(top)
        for row, s in enumerate(scores):
            at = 3 * position + row
            raised = jnp.exp2(s * SCALE2 - (top + bias_ref[at : at + 1, :]))
            weights_ref[head, pl.ds(row * rows, rows), :] = raised
            total = total + jnp.sum(raised, axis=0, keepdims=True)
        stats_ref[head : head + 1, :] = top
        stats_ref[heads + head : heads + head + 1, :] = total


def table_kernel(heads, own_o, own_qg, *refs):
    *stats, out_ref = refs
    rows = own_o.shape[0]
    out_ref[...] = jnp.zeros_like(out_ref)
    top = functools.reduce(jnp.maximum, [ref[0:heads, :] for ref in stats])
    total = sum(ref[heads : 2 * heads, :] * jnp.exp2(ref[0:heads, :] - top) for ref in stats)
    out_ref[0:heads, :] = top
    out_ref[heads : 2 * heads, :] = total
    ones = jnp.ones((8, HEAD_DIM), F32)
    for head in range(heads):
        cols = head_cols(head)
        product = own_qg[pl.ds(rows, rows), cols].astype(F32) * own_o[:, cols].astype(F32)
        row_dot = dot(ones, product, NT, lax.Precision.HIGHEST)[:1]
        out_ref[2 * heads + head : 2 * heads + head + 1, 0:rows] = row_dot


def reordered(table, rows, flip):
    if flip == 0:
        return table
    return jnp.concatenate(
        [table[:, (j ^ flip) * rows : ((j ^ flip) + 1) * rows] for j in range(4)], axis=1
    )


def merge_kernel(heads, rows, *refs):
    *tables, out_ref = refs
    tables = [reordered(ref[...], rows, flip) for flip, ref in zip((1, 2, 3, 0), tables)]
    out_ref[...] = jnp.zeros_like(out_ref)
    top = functools.reduce(jnp.maximum, [t[0:heads] for t in tables])
    total = sum(t[heads : 2 * heads] * jnp.exp2(t[0:heads] - top) for t in tables)
    out_ref[0:heads, :] = top + jnp.log2(total)
    out_ref[heads : 2 * heads, :] = sum(t[2 * heads : 3 * heads] for t in tables)


def product_kernel(*refs):
    *pieces, kv_ref, out_ref = refs
    rows = pieces[0].shape[0] // 2
    for head in range(pieces[0].shape[1] // HEAD_DIM):
        cols = head_cols(head)
        grad = gathered(pieces, 1, head)
        for row in range(3):
            value = kv_ref[pl.ds((3 + row) * rows, rows), cols]
            out_ref[head, pl.ds(row * rows, rows), :] = dot(value, grad, NT)


def grads_kernel(first, *refs):
    lse_ref, stats_ref, weights_ref, p0, p1, p2, p3, product_ref, kv_ref, *refs = refs
    pieces = (p0, p1, p2, p3)
    if not first:
        prior_ref, *refs = refs
    out_ref, dq_ref = refs
    heads = p0.shape[1] // HEAD_DIM
    rows = p0.shape[0] // 2
    for head in range(heads):
        cols = head_cols(head)
        query = gathered(pieces, 0, head)
        grad = gathered(pieces, 1, head)
        scale = jnp.exp2(stats_ref[head : head + 1, :] - lse_ref[head : head + 1, :])
        row_dot = lse_ref[heads + head : heads + head + 1, :] * SCALE
        dq = None if first else prior_ref[:, cols]
        for row in range(3):
            place = pl.ds(row * rows, rows)
            weights = weights_ref[head, place, :] * scale
            score_grad = weights * (product_ref[head, place, :] * SCALE - row_dot)
            score_grad = score_grad.astype(BF16)
            out_ref[place, cols] = dot(score_grad, query, NN).astype(out_ref.dtype)
            value_part = dot(weights.astype(BF16), grad, NN).astype(out_ref.dtype)
            out_ref[pl.ds((3 + row) * rows, rows), cols] = value_part
            step = dot(score_grad, kv_ref[place, cols], TN)
            dq = step if dq is None else dq + step
        dq_ref[:, cols] = dq


def add_kernel(x_ref, y_ref, out_ref):
    out_ref[...] = x_ref[...] + y_ref[...].astype(F32)


def column_kernel(rows, mid_ref, a_ref, own_ref, to_a_ref, to_b_ref):
    for half in range(2):
        for row, out in enumerate((own_ref, to_a_ref, to_b_ref)):
            place = pl.ds((3 * half + row) * rows, rows)
            total = mid_ref[place, :] + a_ref[place, :].astype(F32)
            out[pl.ds(half * rows, rows), :] = total.astype(out.dtype)


def query_kernel(own_ref, a_ref, b_ref, c_ref, out_ref):
    total = own_ref[...] + a_ref[...].astype(F32) + b_ref[...].astype(F32)
    out_ref[...] = (total + c_ref[...].astype(F32)).astype(BF16)


def finish_kernel(dq_ref, own_ref, a_ref, b_ref, query_ref, key_ref, value_ref):
    rows = dq_ref.shape[0]
    query_ref[...] = dq_ref[...]
    for half, out in enumerate((key_ref, value_ref)):
        place = pl.ds(half * rows, rows)
        total = own_ref[place, :] + a_ref[place, :].astype(F32) + b_ref[place, :].astype(F32)
        out[...] = total.astype(BF16)


def call(kernel, out_shape, *args):
    many = isinstance(out_shape, (tuple, list))
    vmem = pl.BlockSpec(memory_space=pltpu.VMEM)
    return pl.pallas_call(
        kernel,
        out_shape=out_shape,
        in_specs=[vmem] * len(args),
        out_specs=[vmem] * len(out_shape) if many else vmem,
        compiler_params=pltpu.CompilerParams(vmem_limit_bytes=16 * 1024 * 1024),
        name=getattr(kernel, "func", kernel).__name__[:-7],
        cost_estimate=pl.CostEstimate(flops=0, bytes_accessed=0, transcendentals=0),
    )(*args)


def after(x, *others):
    return lax.optimization_barrier((x, *others))[0]


def local(query_in, key_in, value_in, saved_out, out_grad, window_mask):
    frames_dev, _, tile_rows, tile_cols, width = query_in.shape
    rows = frames_dev * tile_rows * tile_cols
    heads = width // HEAD_DIM
    n_ta = lax.axis_size("ta")
    row_tiles, col_tiles = window_mask.shape[1:3]
    me = lax.axis_index("ta")
    plane = lax.axis_index("ha")
    row_tile = plane // col_tiles
    col_tile = plane % col_tiles

    def pairs(count, first):
        ends = [(i, i + 1) for i in range(first, count - 1, 2)]
        return ends + [(d, s) for s, d in ends]

    def row_swap(x, first, name):
        route = [
            (s * col_tiles + c, d * col_tiles + c)
            for s, d in pairs(row_tiles, first)
            for c in range(col_tiles)
        ]
        with jax.named_scope(name):
            return lax.ppermute(x, "ha", route)

    def col_swap(x, first, name):
        route = [
            (r * col_tiles + s, r * col_tiles + d)
            for s, d in pairs(col_tiles, first)
            for r in range(row_tiles)
        ]
        with jax.named_scope(name):
            return lax.ppermute(x, "ha", route)

    def ta_swap(x, flip, name):
        with jax.named_scope(name):
            return lax.ppermute(x, "ta", [(i, i ^ flip) for i in range(n_ta)])

    q, k, v, o, g = (
        x.reshape(rows, width) for x in (query_in, key_in, value_in, saved_out, out_grad)
    )
    kv = jnp.concatenate([k, v], axis=0)
    kv_b = row_swap(kv, 1, "kv_row_1")
    kv_a = row_swap(kv, 0, "kv_row_0")
    qg = jnp.concatenate([q, g], axis=0)
    swapped = {flip: ta_swap(qg, flip, "query_ta") for flip in (2, 1, 3)}
    pieces = [qg] + [swapped[flip] for flip in (1, 2, 3)]
    stack_shape = jax.ShapeDtypeStruct((6 * rows, width), BF16)
    kv_mid = call(functools.partial(stack_kernel, rows), stack_shape, kv, kv_a, kv_b)
    kv_right = col_swap(kv_mid, 1, "kv_col_1")
    kv_left = col_swap(kv_mid, 0, "kv_col_0")

    place = jnp.arange(16, dtype=jnp.int32)
    row_step = jnp.where(place < 9, place % 3, 0)
    row_step = jnp.where(row_step == 2, -1, row_step) * (1 - 2 * (row_tile % 2))
    col_step = jnp.where(place < 9, place // 3, 0)
    col_step = jnp.where(col_step == 2, -1, col_step) * (1 - 2 * (col_tile % 2))
    inside = (row_tile + row_step >= 0) & (row_tile + row_step < row_tiles)
    inside = inside & (col_tile + col_step >= 0) & (col_tile + col_step < col_tiles) & (place < 9)
    key_time = me * frames_dev // TILE_T
    owner = me ^ jnp.arange(n_ta, dtype=jnp.int32)
    query_time = owner * frames_dev // TILE_T
    windows = lax.dynamic_slice(
        window_mask, (0, row_tile, col_tile, 0), (window_mask.shape[0], 1, 1, 27)
    ).reshape(-1, 27)
    code = (key_time - query_time[None, :] + 1) * 9 + ((row_step + 1) * 3 + col_step + 1)[:, None]
    number = jnp.arange(27, dtype=jnp.int32)
    hit = code[:, :, None] == number
    table = jnp.zeros((16, n_ta), jnp.int32)
    for t in range(window_mask.shape[0]):
        found = jnp.sum(jnp.where(hit, windows[t], 0), axis=-1)
        table = jnp.where(query_time[None, :] == t, found, table)
    bias = jnp.where((table == 1) & inside[:, None], 0.0, CLOSED).astype(F32)
    bias = jnp.repeat(bias, rows, axis=1)

    n_q = n_ta * rows
    stat_shape = jax.ShapeDtypeStruct((8, n_q), F32)
    weight_shape = jax.ShapeDtypeStruct((heads, 3 * rows, n_q), F32)
    dq_shape = jax.ShapeDtypeStruct((n_q, width), F32)

    def scores(position, kv):
        kernel = functools.partial(scores_kernel, position)
        return call(kernel, (weight_shape, stat_shape), bias, *pieces, kv)

    def products(kv):
        return call(product_kernel, weight_shape, *pieces, kv)

    w_mid, s_mid = scores(0, kv_mid)
    w_a, s_a = scores(1, kv_left)
    w_b, s_b = scores(2, kv_right)
    mine = call(functools.partial(table_kernel, heads), stat_shape, o, qg, s_mid, s_a, s_b)
    swapped = {flip: ta_swap(mine, flip, "stats_ta") for flip in (2, 1, 3)}
    others = tuple(swapped[flip] for flip in (1, 2, 3))
    p_mid, p_a, p_b = products(kv_mid), products(kv_left), products(kv_right)
    others = after(others, p_a, p_b, p_mid)
    lse = call(functools.partial(merge_kernel, heads, rows), stat_shape, *others, mine)

    def grads(stats, weights, product, kv, dtype, *prior):
        part = jax.ShapeDtypeStruct((6 * rows, width), dtype)
        kernel = functools.partial(grads_kernel, not prior)
        return call(
            kernel, (part, dq_shape), lse, stats, weights, *pieces, product, kv, *prior
        )

    d_b, dq = grads(s_b, w_b, p_b, kv_right, BF16)
    d_b = col_swap(d_b, 1, "d_col_1")
    d_a, dq = grads(s_a, w_a, p_a, kv_left, BF16, dq)
    d_a = col_swap(d_a, 0, "d_col_0")
    d_mid, dq = grads(s_mid, w_mid, p_mid, kv_mid, F32, dq)
    dq = dq.reshape(n_ta, rows, width)
    dq_parts = [ta_swap(dq[flip].astype(BF16), flip, "dq_ta") for flip in (2, 1, 3)]
    d_mid = call(add_kernel, jax.ShapeDtypeStruct(d_mid.shape, F32), d_mid, d_b)
    own = jax.ShapeDtypeStruct((2 * rows, width), F32)
    sent = jax.ShapeDtypeStruct((2 * rows, width), BF16)
    own, to_a, to_b = call(
        functools.partial(column_kernel, rows), (own, sent, sent), d_mid, d_a
    )
    d_b = row_swap(to_b, 1, "d_row_1")
    d_a = row_swap(to_a, 0, "d_row_0")
    one = jax.ShapeDtypeStruct((rows, width), BF16)
    dq = call(query_kernel, one, dq[0], *dq_parts)
    outs = call(finish_kernel, (one, one, one), dq, own, d_a, d_b)
    return tuple(x.reshape(query_in.shape) for x in outs)


def solution(mesh):
    spec = P("ta", "ha", None, None, "ga")
    return jax.shard_map(
        local,
        mesh=mesh,
        in_specs=(spec,) * 5 + (P(),),
        out_specs=(spec,) * 3,
        check_vma=False,
    )
```

time: 92 us -> 74.6 us (0.81)
  the two profiles are of different devices: /device:TPU:163 before, /device:TPU:65 now
where the time goes in v2:
time: 74.6 us; the launch traced here: 73.8 us
  starting transfers between devices  30.2 us (40%)
  waiting for transfers between devices  26.7 us (36%)
  Pallas kernels  12.5 us (17%)
  other arithmetic  2.49 us (3%)
  local copies, waits for them, and re-layouts  1.02 us (1%)
  between operations  0.92 us (1%)
    ppermute x4, waiting for transfers between devices, col_swap(): return lax.ppermute(x, 'ha', route)  15.7 us
    pallas_call x16, Pallas kernels, call(): pl.pallas_call(kernel, out_shape=out_shape, in_specs=[vmem] * len(args),...  12.5 us
    ppermute x9, starting transfers between devices, ta_swap(): return lax.ppermute(x, 'ta', [(i, i ^ flip) for i in range(n_ta)])  10.5 us
    ppermute x4, starting transfers between devices, col_swap(): return lax.ppermute(x, 'ha', route)  10.4 us
    ppermute x4, starting transfers between devices, row_swap(): return lax.ppermute(x, 'ha', route)  9.32 us
    ppermute x4, waiting for transfers between devices, row_swap(): return lax.ppermute(x, 'ha', route)  6.42 us
    ppermute x9, waiting for transfers between devices, ta_swap(): return lax.ppermute(x, 'ta', [(i, i ^ flip) for i in range(n_ta)])  4.57 us
  transfers between devices with their start and end apart: 17, of which 7 were waited for; matrix products, arithmetic and copies ran while one was open for 3% of the time, Pallas kernels for 11%

profile of v2, /device:TPU:65, one launch (start us, length us, event | category | flops | bytes accessed | tf_op | source)
XLA Modules:
  0.0 73.8 jit_solution(7712890745576614905)
XLA Ops:
  0.6 1.0 %pad_maximum_fusion.1.refs_0_ = bf16[384,256]{1,0:T(8,128)(2,1)S(1)} fusion(bf16[192,256]{1,0:T(8,128)(2,1)} %bitcast.19, bf16[192,256]{1,0:T(8,128)(2,1)} %bitcast.20), kind=kLoop, calls=%fused_computation.1 | loop fusion | flops 393216 | bytes 393216 | tf_op jit(solution)/shard_map/concatenate | solution.py:229
  1.6 6.1 %collective-permute-start.4 = (bf16[384,256]{1,0:T(8,128)(2,1)S(1)}, bf16[384,256]{1,0:T(8,128)(2,1)S(1)}, u32[]{:S(2)}, u32[]{:S(2)}) collective-permute-start(bf16[384,256]{1,0:T(8,128)(2,1)S(1)} %pad_maximum_fusion.1.refs_0_), channel_id=1, source_target_pairs={{16,32},{18,34},{20,36},{22,38},{24,40},{26,42},{28,44},{30,46},{3... | collective-permute-start | bytes 589832 | tf_op jit(solution)/shard_map/kv_row_1/ppermute | solution.py:211
  7.8 0.1 collective-permute-start.3
  7.8 1.0 %pad_maximum_fusion.refs_1_.own_qg.refs_0_.refs_3_ = bf16[384,256]{1,0:T(8,128)(2,1)S(1)} fusion(bf16[192,256]{1,0:T(8,128)(2,1)} %bitcast.21, bf16[192,256]{1,0:T(8,128)(2,1)} %bitcast.22), kind=kLoop, calls=%fused_computation | loop fusion | flops 393216 | bytes 393216 | tf_op jit(solution)/shard_map/concatenate | solution.py:232
  8.8 2.6 %collective-permute-start.2 = (bf16[384,256]{1,0:T(8,128)(2,1)S(1)}, bf16[384,256]{1,0:T(8,128)(2,1)S(1)}, u32[]{:S(2)}, u32[]{:S(2)}) collective-permute-start(bf16[384,256]{1,0:T(8,128)(2,1)S(1)} %pad_maximum_fusion.refs_1_.own_qg.refs_0_.refs_3_), channel_id=1, source_target_pairs={{0,192},{64,128},{128,64},{192,0},{1,193},{65,129},{129,65},{193,1... | collective-permute-start | bytes 589832 | tf_op jit(solution)/shard_map/query_ta/ppermute | solution.py:224
  11.4 0.5 collective-permute-start.1
  11.9 0.3 collective-permute-start
  12.3 0.7 dynamic-slice_bitcast_fusion.1
  13.0 3.6 %collective-permute-done.4.refs_2_ = bf16[384,256]{1,0:T(8,128)(2,1)S(1)} collective-permute-done((bf16[384,256]{1,0:T(8,128)(2,1)S(1)}, bf16[384,256]{1,0:T(8,128)(2,1)S(1)}, u32[]{:S(2)}, u32[]{:S(2)}) %collective-permute-start.4) | collective-permute-done | bytes 196640 | tf_op jit(solution)/shard_map/kv_row_1/ppermute | solution.py:211
  16.7 4.4 %collective-permute-start.6 = (bf16[1152,256]{1,0:T(8,128)(2,1)S(1)}, bf16[1152,256]{1,0:T(8,128)(2,1)S(1)}, u32[]{:S(2)}, u32[]{:S(2)}) collective-permute-start(bf16[1152,256]{1,0:T(8,128)(2,1)S(1)} %stack.1.refs_5_.refs_4_.refs_8_), channel_id=1, source_target_pairs={{2,4},{18,20},{34,36},{50,52},{6,8},{22,24},{38,40},{54,56},{10,12... | collective-permute-start | bytes 1769480 | tf_op jit(solution)/shard_map/kv_col_1/ppermute | solution.py:220
  21.0 0.1 collective-permute-start.5
  21.2 0.1 broadcast_add_fusion
  21.2 0.3 select_reduce_fusion
  21.5 0.1 and_select_fusion
  21.6 0.1 copy.12
  21.7 0.1 broadcast_in_dim.63
  21.8 0.1 reshape.147.refs_0_
  21.9 0.0 collective-permute-done.2.refs_4_.refs_3_.refs_6_
  21.9 1.3 %scores.3 = (f32[2,576,768]{2,1,0:T(8,128)S(1)}, f32[8,768]{1,0:T(8,128)S(1)}) custom-call(f32[16,768]{1,0:T(8,128)S(1)} %reshape.147.refs_0_, bf16[384,256]{1,0:T(8,128)(2,1)S(1)} %pad_maximum_fusion.refs_1_.own_qg.refs_0_.refs_3_, bf16[384,256]{1,0:T(8,128)(2,1)S(1)} %collective-permute-done.refs_2_.refs_1_.refs_4_, ...), custom_call_target="tpu_custom_call" | custom-call | tf_op jit(solution)/shard_map/scores/pallas_call | solution.py:174
  23.2 1.3 %scores.4 = (f32[2,576,768]{2,1,0:T(8,128)S(1)}, f32[8,768]{1,0:T(8,128)S(1)}) custom-call(f32[16,768]{1,0:T(8,128)S(1)} %reshape.147.refs_0_, bf16[384,256]{1,0:T(8,128)(2,1)S(1)} %pad_maximum_fusion.refs_1_.own_qg.refs_0_.refs_3_, bf16[384,256]{1,0:T(8,128)(2,1)S(1)} %collective-permute-done.refs_2_.refs_1_.refs_4_, ...), custom_call_target="tpu_custom_call" | custom-call | tf_op jit(solution)/shard_map/scores/pallas_call | solution.py:174
  24.4 9.7 %collective-permute-done.6.refs_5_.refs_4_.refs_8_ = bf16[1152,256]{1,0:T(8,128)(2,1)S(1)} collective-permute-done((bf16[1152,256]{1,0:T(8,128)(2,1)S(1)}, bf16[1152,256]{1,0:T(8,128)(2,1)S(1)}, u32[]{:S(2)}, u32[]{:S(2)}) %collective-permute-start.6) | collective-permute-done | bytes 589856 | tf_op jit(solution)/shard_map/kv_col_1/ppermute | solution.py:220
  34.2 1.3 %scores.5 = (f32[2,576,768]{2,1,0:T(8,128)S(1)}, f32[8,768]{1,0:T(8,128)S(1)}) custom-call(f32[16,768]{1,0:T(8,128)S(1)} %reshape.147.refs_0_, bf16[384,256]{1,0:T(8,128)(2,1)S(1)} %pad_maximum_fusion.refs_1_.own_qg.refs_0_.refs_3_, bf16[384,256]{1,0:T(8,128)(2,1)S(1)} %collective-permute-done.refs_2_.refs_1_.refs_4_, ...), custom_call_target="tpu_custom_call" | custom-call | tf_op jit(solution)/shard_map/scores/pallas_call | solution.py:174
  35.4 0.4 table.1.refs_3_
  35.9 2.5 %collective-permute-start.9 = (f32[8,768]{1,0:T(8,128)S(1)}, f32[8,768]{1,0:T(8,128)S(1)}, u32[]{:S(2)}, u32[]{:S(2)}) collective-permute-start(f32[8,768]{1,0:T(8,128)S(1)} %table.1.refs_3_), channel_id=1, source_target_pairs={{0,192},{64,128},{128,64},{192,0},{1,193},{65,129},{129,65},{193,1... | collective-permute-start | bytes 73736 | tf_op jit(solution)/shard_map/stats_ta/ppermute | solution.py:224
  38.3 0.5 collective-permute-start.8
  38.9 0.3 collective-permute-start.7
  39.1 0.6 product.5.refs_7_
  39.7 0.6 product.3.refs_7_
  40.4 0.6 product.4.refs_7_
  41.0 1.5 %collective-permute-done.8.refs_1_ = f32[8,768]{1,0:T(8,128)S(1)} collective-permute-done((f32[8,768]{1,0:T(8,128)S(1)}, f32[8,768]{1,0:T(8,128)S(1)}, u32[]{:S(2)}, u32[]{:S(2)}) %collective-permute-start.8) | collective-permute-done | bytes 24608 | tf_op jit(solution)/shard_map/stats_ta/ppermute | solution.py:224
  42.5 0.1 merge.1.refs_0_
  42.6 1.8 %grads.3 = (bf16[1152,256]{1,0:T(8,128)(2,1)S(1)}, f32[768,256]{1,0:T(8,128)S(1)}) custom-call(f32[8,768]{1,0:T(8,128)S(1)} %merge.1.refs_0_, f32[8,768]{1,0:T(8,128)S(1)} %get-tuple-element.26.refs_2_.refs_1_, f32[2,576,768]{2,1,0:T(8,128)S(1)} %get-tuple-element.32.refs_2_, bf16[384,256]{1,0:T(8,128)(2,1)S(1)} %pad_maximum_fusion.refs_1_.own_qg.refs_0_.refs_3_, ...), custom_call_target="tpu_custom_call" | custom-call | tf_op jit(solution)/shard_map/grads/pallas_call | solution.py:174
  44.4 5.8 %collective-permute-start.13 = (bf16[1152,256]{1,0:T(8,128)(2,1)S(1)}, bf16[1152,256]{1,0:T(8,128)(2,1)S(1)}, u32[]{:S(2)}, u32[]{:S(2)}) collective-permute-start(bf16[1152,256]{1,0:T(8,128)(2,1)S(1)} %get-tuple-element.37), channel_id=1, source_target_pairs={{2,4},{18,20},{34,36},{50,52},{6,8},{22,24},{38,40},{54,56},{10,12... | collective-permute-start | bytes 1769480 | tf_op jit(solution)/shard_map/d_col_1/ppermute | solution.py:220
  50.3 1.7 %grads.4 = (bf16[1152,256]{1,0:T(8,128)(2,1)S(1)}, f32[768,256]{1,0:T(8,128)S(1)}) custom-call(f32[8,768]{1,0:T(8,128)S(1)} %merge.1.refs_0_, f32[8,768]{1,0:T(8,128)S(1)} %get-tuple-element.25.refs_1_, f32[2,576,768]{2,1,0:T(8,128)S(1)} %get-tuple-element.31.refs_2_, bf16[384,256]{1,0:T(8,128)(2,1)S(1)} %pad_maximum_fusion.refs_1_.own_qg.refs_0_.refs_3_, ...), custom_call_target="tpu_custom_call" | custom-call | tf_op jit(solution)/shard_map/grads/pallas_call | solution.py:174
  52.0 0.1 collective-permute-start.14
  52.1 1.7 %grads.5 = (f32[1152,256]{1,0:T(8,128)S(1)}, f32[768,256]{1,0:T(8,128)S(1)}) custom-call(f32[8,768]{1,0:T(8,128)S(1)} %merge.1.refs_0_, f32[8,768]{1,0:T(8,128)S(1)} %get-tuple-element.24.refs_0_.refs_1_, f32[2,576,768]{2,1,0:T(8,128)S(1)} %get-tuple-element.30.refs_2_, bf16[384,256]{1,0:T(8,128)(2,1)S(1)} %pad_maximum_fusion.refs_1_.own_qg.refs_0_.refs_3_, ...), custom_call_target="tpu_custom_call" | custom-call | tf_op jit(solution)/shard_map/grads/pallas_call | solution.py:174
  53.9 6.0 %collective-permute-done.13.y_ref = bf16[1152,256]{1,0:T(8,128)(2,1)S(1)} collective-permute-done((bf16[1152,256]{1,0:T(8,128)(2,1)S(1)}, bf16[1152,256]{1,0:T(8,128)(2,1)S(1)}, u32[]{:S(2)}, u32[]{:S(2)}) %collective-permute-start.13) | collective-permute-done | bytes 589856 | tf_op jit(solution)/shard_map/d_col_1/ppermute | solution.py:220
  59.9 0.1 add.161.mid_ref
  60.0 0.1 column.1
  60.1 0.4 collective-permute-start.15
  60.5 2.7 %collective-permute-start.16 = (bf16[384,256]{1,0:T(8,128)(2,1)S(1)}, bf16[384,256]{1,0:T(8,128)(2,1)S(1)}, u32[]{:S(2)}, u32[]{:S(2)}) collective-permute-start(bf16[384,256]{1,0:T(8,128)(2,1)S(1)} %get-tuple-element.41), channel_id=1, source_target_pairs={{16,32},{18,34},{20,36},{22,38},{24,40},{26,42},{28,44},{30,46},{3... | collective-permute-start | bytes 589832 | tf_op jit(solution)/shard_map/d_row_1/ppermute | solution.py:211
  63.3 1.2 %collective-permute-start.12 = (bf16[192,256]{1,0:T(8,128)(2,1)S(1)}, bf16[192,256]{1,0:T(8,128)(2,1)S(1)}, u32[]{:S(2)}, u32[]{:S(2)}) collective-permute-start(bf16[192,256]{1,0:T(8,128)(2,1)S(1)} %get-tuple-element.53), channel_id=1, source_target_pairs={{0,192},{64,128},{128,64},{192,0},{1,193},{65,129},{129,65},{193,1... | collective-permute-start | bytes 294920 | tf_op jit(solution)/shard_map/dq_ta/ppermute | solution.py:224
  64.5 0.3 collective-permute-start.11
  64.8 2.4 %collective-permute-start.10 = (bf16[192,256]{1,0:T(8,128)(2,1)S(1)}, bf16[192,256]{1,0:T(8,128)(2,1)S(1)}, u32[]{:S(2)}, u32[]{:S(2)}) collective-permute-start(bf16[192,256]{1,0:T(8,128)(2,1)S(1)} %get-tuple-element.55), channel_id=1, source_target_pairs={{0,128},{64,192},{128,0},{192,64},{1,129},{65,193},{129,1},{193,65... | collective-permute-start | bytes 294920 | tf_op jit(solution)/shard_map/dq_ta/ppermute | solution.py:224
  67.2 0.9 %collective-permute-done.12.c_ref = bf16[192,256]{1,0:T(8,128)(2,1)S(1)} collective-permute-done((bf16[192,256]{1,0:T(8,128)(2,1)S(1)}, bf16[192,256]{1,0:T(8,128)(2,1)S(1)}, u32[]{:S(2)}, u32[]{:S(2)}) %collective-permute-start.12) | collective-permute-done | bytes 98336 | tf_op jit(solution)/shard_map/dq_ta/ppermute | solution.py:224
  68.1 2.1 %collective-permute-done.10.a_ref = bf16[192,256]{1,0:T(8,128)(2,1)S(1)} collective-permute-done((bf16[192,256]{1,0:T(8,128)(2,1)S(1)}, bf16[192,256]{1,0:T(8,128)(2,1)S(1)}, u32[]{:S(2)}, u32[]{:S(2)}) %collective-permute-start.10) | collective-permute-done | bytes 98336 | tf_op jit(solution)/shard_map/dq_ta/ppermute | solution.py:224
  70.3 2.8 %collective-permute-done.16.b_ref = bf16[384,256]{1,0:T(8,128)(2,1)S(1)} collective-permute-done((bf16[384,256]{1,0:T(8,128)(2,1)S(1)}, bf16[384,256]{1,0:T(8,128)(2,1)S(1)}, u32[]{:S(2)}, u32[]{:S(2)}) %collective-permute-start.16) | collective-permute-done | bytes 196640 | tf_op jit(solution)/shard_map/d_row_1/ppermute | solution.py:211
  73.1 0.7 %finish.1 = (bf16[192,256]{1,0:T(8,128)(2,1)}, bf16[192,256]{1,0:T(8,128)(2,1)}, bf16[192,256]{1,0:T(8,128)(2,1)}) custom-call(bf16[192,256]{1,0:T(8,128)(2,1)S(1)} %query.1.dq_ref, f32[384,256]{1,0:T(8,128)S(1)} %get-tuple-element.39.own_ref, bf16[384,256]{1,0:T(8,128)(2,1)S(1)} %collective-permute-done.15.a_ref, ...), custom_call_target="tpu_custom_call" | custom-call | tf_op jit(solution)/shard_map/finish/pallas_call | solution.py:174
  (20 shorter events, 0.3 us)
Async XLA Ops:
  0.6 34.8 %copy-start = (bf16[3,1,8,8,256]{4,3,2,1,0:T(8,128)(2,1)S(1)}, bf16[3,1,8,8,256]{4,3,2,1,0:T(8,128)(2,1)}, u32[]{:S(2)}) copy-start(bf16[3,1,8,8,256]{4,3,2,1,0:T(8,128)(2,1)} %param.9) | copy-start | bytes 294916
  1.6 15.0 %collective-permute-start.4 = (bf16[384,256]{1,0:T(8,128)(2,1)S(1)}, bf16[384,256]{1,0:T(8,128)(2,1)S(1)}, u32[]{:S(2)}, u32[]{:S(2)}) collective-permute-start(bf16[384,256]{1,0:T(8,128)(2,1)S(1)} %pad_maximum_fusion.1.refs_0_), channel_id=1, source_target_pairs={{16,32},{18,34},{20,36},{22,38},{24,40},{26,42},{28,44},{30,46},{3... | collective-permute-start | bytes 589832 | tf_op jit(solution)/shard_map/kv_row_1/ppermute | solution.py:211
  7.8 8.9 %collective-permute-start.3 = (bf16[384,256]{1,0:T(8,128)(2,1)S(1)}, bf16[384,256]{1,0:T(8,128)(2,1)S(1)}, u32[]{:S(2)}, u32[]{:S(2)}) collective-permute-start(bf16[384,256]{1,0:T(8,128)(2,1)S(1)} %pad_maximum_fusion.1.refs_0_), channel_id=1, source_target_pairs={{0,16},{2,18},{4,20},{6,22},{8,24},{10,26},{12,28},{14,30},{32,48}... | collective-permute-start | bytes 589832 | tf_op jit(solution)/shard_map/kv_row_0/ppermute | solution.py:211
  8.8 13.1 %collective-permute-start.2 = (bf16[384,256]{1,0:T(8,128)(2,1)S(1)}, bf16[384,256]{1,0:T(8,128)(2,1)S(1)}, u32[]{:S(2)}, u32[]{:S(2)}) collective-permute-start(bf16[384,256]{1,0:T(8,128)(2,1)S(1)} %pad_maximum_fusion.refs_1_.own_qg.refs_0_.refs_3_), channel_id=1, source_target_pairs={{0,192},{64,128},{128,64},{192,0},{1,193},{65,129},{129,65},{193,1... | collective-permute-start | bytes 589832 | tf_op jit(solution)/shard_map/query_ta/ppermute | solution.py:224
  11.4 10.5 %collective-permute-start.1 = (bf16[384,256]{1,0:T(8,128)(2,1)S(1)}, bf16[384,256]{1,0:T(8,128)(2,1)S(1)}, u32[]{:S(2)}, u32[]{:S(2)}) collective-permute-start(bf16[384,256]{1,0:T(8,128)(2,1)S(1)} %pad_maximum_fusion.refs_1_.own_qg.refs_0_.refs_3_), channel_id=1, source_target_pairs={{0,128},{64,192},{128,0},{192,64},{1,129},{65,193},{129,1},{193,65... | collective-permute-start | bytes 589832 | tf_op jit(solution)/shard_map/query_ta/ppermute | solution.py:224
  11.9 10.0 %collective-permute-start = (bf16[384,256]{1,0:T(8,128)(2,1)S(1)}, bf16[384,256]{1,0:T(8,128)(2,1)S(1)}, u32[]{:S(2)}, u32[]{:S(2)}) collective-permute-start(bf16[384,256]{1,0:T(8,128)(2,1)S(1)} %pad_maximum_fusion.refs_1_.own_qg.refs_0_.refs_3_), channel_id=1, source_target_pairs={{0,64},{64,0},{128,192},{192,128},{1,65},{65,1},{129,193},{193,129... | collective-permute-start | bytes 589832 | tf_op jit(solution)/shard_map/query_ta/ppermute | solution.py:224
  16.7 17.5 %collective-permute-start.6 = (bf16[1152,256]{1,0:T(8,128)(2,1)S(1)}, bf16[1152,256]{1,0:T(8,128)(2,1)S(1)}, u32[]{:S(2)}, u32[]{:S(2)}) collective-permute-start(bf16[1152,256]{1,0:T(8,128)(2,1)S(1)} %stack.1.refs_5_.refs_4_.refs_8_), channel_id=1, source_target_pairs={{2,4},{18,20},{34,36},{50,52},{6,8},{22,24},{38,40},{54,56},{10,12... | collective-permute-start | bytes 1769480 | tf_op jit(solution)/shard_map/kv_col_1/ppermute | solution.py:220
  21.0 2.1 %collective-permute-start.5 = (bf16[1152,256]{1,0:T(8,128)(2,1)S(1)}, bf16[1152,256]{1,0:T(8,128)(2,1)S(1)}, u32[]{:S(2)}, u32[]{:S(2)}) collective-permute-start(bf16[1152,256]{1,0:T(8,128)(2,1)S(1)} %stack.1.refs_5_.refs_4_.refs_8_), channel_id=1, source_target_pairs={{0,2},{16,18},{32,34},{48,50},{4,6},{20,22},{36,38},{52,54},{8,10}... | collective-permute-start | bytes 1769480 | tf_op jit(solution)/shard_map/kv_col_0/ppermute | solution.py:220
  35.9 5.1 %collective-permute-start.9 = (f32[8,768]{1,0:T(8,128)S(1)}, f32[8,768]{1,0:T(8,128)S(1)}, u32[]{:S(2)}, u32[]{:S(2)}) collective-permute-start(f32[8,768]{1,0:T(8,128)S(1)} %table.1.refs_3_), channel_id=1, source_target_pairs={{0,192},{64,128},{128,64},{192,0},{1,193},{65,129},{129,65},{193,1... | collective-permute-start | bytes 73736 | tf_op jit(solution)/shard_map/stats_ta/ppermute | solution.py:224
  38.3 4.2 %collective-permute-start.8 = (f32[8,768]{1,0:T(8,128)S(1)}, f32[8,768]{1,0:T(8,128)S(1)}, u32[]{:S(2)}, u32[]{:S(2)}) collective-permute-start(f32[8,768]{1,0:T(8,128)S(1)} %table.1.refs_3_), channel_id=1, source_target_pairs={{0,128},{64,192},{128,0},{192,64},{1,129},{65,193},{129,1},{193,65... | collective-permute-start | bytes 73736 | tf_op jit(solution)/shard_map/stats_ta/ppermute | solution.py:224
  38.9 3.7 %collective-permute-start.7 = (f32[8,768]{1,0:T(8,128)S(1)}, f32[8,768]{1,0:T(8,128)S(1)}, u32[]{:S(2)}, u32[]{:S(2)}) collective-permute-start(f32[8,768]{1,0:T(8,128)S(1)} %table.1.refs_3_), channel_id=1, source_target_pairs={{0,64},{64,0},{128,192},{192,128},{1,65},{65,1},{129,193},{193,129... | collective-permute-start | bytes 73736 | tf_op jit(solution)/shard_map/stats_ta/ppermute | solution.py:224
  44.4 15.5 %collective-permute-start.13 = (bf16[1152,256]{1,0:T(8,128)(2,1)S(1)}, bf16[1152,256]{1,0:T(8,128)(2,1)S(1)}, u32[]{:S(2)}, u32[]{:S(2)}) collective-permute-start(bf16[1152,256]{1,0:T(8,128)(2,1)S(1)} %get-tuple-element.37), channel_id=1, source_target_pairs={{2,4},{18,20},{34,36},{50,52},{6,8},{22,24},{38,40},{54,56},{10,12... | collective-permute-start | bytes 1769480 | tf_op jit(solution)/shard_map/d_col_1/ppermute | solution.py:220
  52.0 8.0 %collective-permute-start.14 = (bf16[1152,256]{1,0:T(8,128)(2,1)S(1)}, bf16[1152,256]{1,0:T(8,128)(2,1)S(1)}, u32[]{:S(2)}, u32[]{:S(2)}) collective-permute-start(bf16[1152,256]{1,0:T(8,128)(2,1)S(1)} %get-tuple-element.38), channel_id=1, source_target_pairs={{0,2},{16,18},{32,34},{48,50},{4,6},{20,22},{36,38},{52,54},{8,10}... | collective-permute-start | bytes 1769480 | tf_op jit(solution)/shard_map/d_col_0/ppermute | solution.py:220
  60.1 10.2 %collective-permute-start.15 = (bf16[384,256]{1,0:T(8,128)(2,1)S(1)}, bf16[384,256]{1,0:T(8,128)(2,1)S(1)}, u32[]{:S(2)}, u32[]{:S(2)}) collective-permute-start(bf16[384,256]{1,0:T(8,128)(2,1)S(1)} %get-tuple-element.40), channel_id=1, source_target_pairs={{0,16},{2,18},{4,20},{6,22},{8,24},{10,26},{12,28},{14,30},{32,48}... | collective-permute-start | bytes 589832 | tf_op jit(solution)/shard_map/d_row_0/ppermute | solution.py:211
  60.5 12.6 %collective-permute-start.16 = (bf16[384,256]{1,0:T(8,128)(2,1)S(1)}, bf16[384,256]{1,0:T(8,128)(2,1)S(1)}, u32[]{:S(2)}, u32[]{:S(2)}) collective-permute-start(bf16[384,256]{1,0:T(8,128)(2,1)S(1)} %get-tuple-element.41), channel_id=1, source_target_pairs={{16,32},{18,34},{20,36},{22,38},{24,40},{26,42},{28,44},{30,46},{3... | collective-permute-start | bytes 589832 | tf_op jit(solution)/shard_map/d_row_1/ppermute | solution.py:211
  63.3 4.9 %collective-permute-start.12 = (bf16[192,256]{1,0:T(8,128)(2,1)S(1)}, bf16[192,256]{1,0:T(8,128)(2,1)S(1)}, u32[]{:S(2)}, u32[]{:S(2)}) collective-permute-start(bf16[192,256]{1,0:T(8,128)(2,1)S(1)} %get-tuple-element.53), channel_id=1, source_target_pairs={{0,192},{64,128},{128,64},{192,0},{1,193},{65,129},{129,65},{193,1... | collective-permute-start | bytes 294920 | tf_op jit(solution)/shard_map/dq_ta/ppermute | solution.py:224
  64.5 3.7 %collective-permute-start.11 = (bf16[192,256]{1,0:T(8,128)(2,1)S(1)}, bf16[192,256]{1,0:T(8,128)(2,1)S(1)}, u32[]{:S(2)}, u32[]{:S(2)}) collective-permute-start(bf16[192,256]{1,0:T(8,128)(2,1)S(1)} %get-tuple-element.54), channel_id=1, source_target_pairs={{0,64},{64,0},{128,192},{192,128},{1,65},{65,1},{129,193},{193,129... | collective-permute-start | bytes 294920 | tf_op jit(solution)/shard_map/dq_ta/ppermute | solution.py:224
  64.8 5.5 %collective-permute-start.10 = (bf16[192,256]{1,0:T(8,128)(2,1)S(1)}, bf16[192,256]{1,0:T(8,128)(2,1)S(1)}, u32[]{:S(2)}, u32[]{:S(2)}) collective-permute-start(bf16[192,256]{1,0:T(8,128)(2,1)S(1)} %get-tuple-element.55), channel_id=1, source_target_pairs={{0,128},{64,192},{128,0},{192,64},{1,129},{65,193},{129,1},{193,65... | collective-permute-start | bytes 294920 | tf_op jit(solution)/shard_map/dq_ta/ppermute | solution.py:224

commit v3 on v2

--- a/solution.py
+++ b/solution.py
@@ -44,12 +44,20 @@
 def scores_kernel(position, *refs):
     bias_ref, *refs = refs
     *pieces, kv_ref, weights_ref, stats_ref = refs
+    if position == 0:
+        saved_ref, *pieces = pieces
     heads = pieces[0].shape[1] // HEAD_DIM
     rows = pieces[0].shape[0] // 2
     stats_ref[...] = jnp.zeros_like(stats_ref)
     for head in range(heads):
         cols = head_cols(head)
         query = gathered(pieces, 0, head)
+        if position == 0:
+            product = pieces[0][pl.ds(rows, rows), cols].astype(F32)
+            product = product * saved_ref[:, cols].astype(F32)
+            ones = jnp.ones((8, HEAD_DIM), F32)
+            row_dot = dot(ones, product, NT, lax.Precision.HIGHEST)[:1]
+            stats_ref[2 * heads + head : 2 * heads + head + 1, 0:rows] = row_dot
         scores = []
         tops = []
         for row in range(3):
@@ -69,20 +77,13 @@
         stats_ref[heads + head : heads + head + 1, :] = total
 
 
-def table_kernel(heads, own_o, own_qg, *refs):
+def table_kernel(heads, *refs):
     *stats, out_ref = refs
-    rows = own_o.shape[0]
-    out_ref[...] = jnp.zeros_like(out_ref)
+    out_ref[...] = stats[0][...]
     top = functools.reduce(jnp.maximum, [ref[0:heads, :] for ref in stats])
     total = sum(ref[heads : 2 * heads, :] * jnp.exp2(ref[0:heads, :] - top) for ref in stats)
     out_ref[0:heads, :] = top
     out_ref[heads : 2 * heads, :] = total
-    ones = jnp.ones((8, HEAD_DIM), F32)
-    for head in range(heads):
-        cols = head_cols(head)
-        product = own_qg[pl.ds(rows, rows), cols].astype(F32) * own_o[:, cols].astype(F32)
-        row_dot = dot(ones, product, NT, lax.Precision.HIGHEST)[:1]
-        out_ref[2 * heads + head : 2 * heads + head + 1, 0:rows] = row_dot
 
 
 def reordered(table, rows, flip):
@@ -114,12 +115,15 @@
             out_ref[head, pl.ds(row * rows, rows), :] = dot(value, grad, NT)
 
 
-def grads_kernel(first, *refs):
+def grads_kernel(stage, *refs):
     lse_ref, stats_ref, weights_ref, p0, p1, p2, p3, product_ref, kv_ref, *refs = refs
     pieces = (p0, p1, p2, p3)
-    if not first:
-        prior_ref, *refs = refs
-    out_ref, dq_ref = refs
+    if stage == 0:
+        out_ref, kept_ref = refs
+    elif stage == 1:
+        kept_ref, kept_kv_ref, out_ref, dq_ref = refs
+    else:
+        prior_ref, out_ref, dq_ref = refs
     heads = p0.shape[1] // HEAD_DIM
     rows = p0.shape[0] // 2
     for head in range(heads):
@@ -128,7 +132,11 @@
         grad = gathered(pieces, 1, head)
         scale = jnp.exp2(stats_ref[head : head + 1, :] - lse_ref[head : head + 1, :])
         row_dot = lse_ref[heads + head : heads + head + 1, :] * SCALE
-        dq = None if first else prior_ref[:, cols]
+        if stage == 1:
+            whole = pl.ds(0, 3 * rows)
+            dq = dot(kept_ref[head], kept_kv_ref[whole, cols], TN)
+        elif stage == 2:
+            dq = prior_ref[:, cols]
         for row in range(3):
             place = pl.ds(row * rows, rows)
             weights = weights_ref[head, place, :] * scale
@@ -137,9 +145,12 @@
             out_ref[place, cols] = dot(score_grad, query, NN).astype(out_ref.dtype)
             value_part = dot(weights.astype(BF16), grad, NN).astype(out_ref.dtype)
             out_ref[pl.ds((3 + row) * rows, rows), cols] = value_part
-            step = dot(score_grad, kv_ref[place, cols], TN)
-            dq = step if dq is None else dq + step
-        dq_ref[:, cols] = dq
+            if stage == 0:
+                kept_ref[head, place, :] = score_grad
+            else:
+                dq = dq + dot(score_grad, kv_ref[place, cols], TN)
+        if stage:
+            dq_ref[:, cols] = dq
 
 
 def add_kernel(x_ref, y_ref, out_ref):
@@ -267,7 +278,8 @@
 
     def scores(position, kv):
         kernel = functools.partial(scores_kernel, position)
-        return call(kernel, (weight_shape, stat_shape), bias, *pieces, kv)
+        first = (o,) if position == 0 else ()
+        return call(kernel, (weight_shape, stat_shape), bias, *first, *pieces, kv)
 
     def products(kv):
         return call(product_kernel, weight_shape, *pieces, kv)
@@ -275,25 +287,27 @@
     w_mid, s_mid = scores(0, kv_mid)
     w_a, s_a = scores(1, kv_left)
     w_b, s_b = scores(2, kv_right)
-    mine = call(functools.partial(table_kernel, heads), stat_shape, o, qg, s_mid, s_a, s_b)
+    mine = call(functools.partial(table_kernel, heads), stat_shape, s_mid, s_a, s_b)
     swapped = {flip: ta_swap(mine, flip, "stats_ta") for flip in (2, 1, 3)}
     others = tuple(swapped[flip] for flip in (1, 2, 3))
     p_mid, p_a, p_b = products(kv_mid), products(kv_left), products(kv_right)
     others = after(others, p_a, p_b, p_mid)
     lse = call(functools.partial(merge_kernel, heads, rows), stat_shape, *others, mine)
 
-    def grads(stats, weights, product, kv, dtype, *prior):
+    def grads(stage, stats, weights, product, kv, dtype, *prior):
         part = jax.ShapeDtypeStruct((6 * rows, width), dtype)
-        kernel = functools.partial(grads_kernel, not prior)
+        kept = jax.ShapeDtypeStruct(weight_shape.shape, BF16)
         return call(
-            kernel, (part, dq_shape), lse, stats, weights, *pieces, product, kv, *prior
+            functools.partial(grads_kernel, stage),
+            (part, dq_shape if stage else kept),
+            lse, stats, weights, *pieces, product, kv, *prior,
         )
 
-    d_b, dq = grads(s_b, w_b, p_b, kv_right, BF16)
+    d_b, kept = grads(0, s_b, w_b, p_b, kv_right, BF16)
     d_b = col_swap(d_b, 1, "d_col_1")
-    d_a, dq = grads(s_a, w_a, p_a, kv_left, BF16, dq)
+    d_a, dq = grads(1, s_a, w_a, p_a, kv_left, BF16, kept, kv_right)
     d_a = col_swap(d_a, 0, "d_col_0")
-    d_mid, dq = grads(s_mid, w_mid, p_mid, kv_mid, F32, dq)
+    d_mid, dq = grads(2, s_mid, w_mid, p_mid, kv_mid, F32, dq)
     dq = dq.reshape(n_ta, rows, width)
     dq_parts = [ta_swap(dq[flip].astype(BF16), flip, "dq_ta") for flip in (2, 1, 3)]
     d_mid = call(add_kernel, jax.ShapeDtypeStruct(d_mid.shape, F32), d_mid, d_b)

time: 74.6 us -> 73.9 us (level)
  waiting for transfers between devices: 26.7 us -> 25.1 us
  local copies, waits for them, and re-layouts: 1.02 us -> 1.9 us
    ppermute x4, waiting for transfers between devices: 15.7 us -> 13.9 us  [col_swap(): return lax.ppermute(x, 'ha', route)]
    unnamed x2, local copies, waits for them, and re-layouts: 0.01 us -> 0.89 us
  transfers between devices with their start and end apart: 17 -> 17, of which waited for: 7 -> 7; matrix products, arithmetic and copies ran while one was open for 3% -> 3% of each run, Pallas kernels for 11% -> 12%
where the time goes in v3:
time: 73.9 us; the launch traced here: 73.3 us
  starting transfers between devices  30.5 us (41%)
  waiting for transfers between devices  25.1 us (34%)
  Pallas kernels  12.4 us (17%)
  other arithmetic  2.46 us (3%)
  local copies, waits for them, and re-layouts  1.9 us (3%)
  between operations  0.92 us (1%)
    ppermute x4, waiting for transfers between devices, col_swap(): return lax.ppermute(x, 'ha', route)  13.9 us
    pallas_call x16, Pallas kernels, call(): pl.pallas_call(kernel, out_shape=out_shape, in_specs=[vmem] * len(args),...  12.4 us
    ppermute x9, starting transfers between devices, ta_swap(): return lax.ppermute(x, 'ta', [(i, i ^ flip) for i in range(n_ta)])  10.6 us
    ppermute x4, starting transfers between devices, col_swap(): return lax.ppermute(x, 'ha', route)  10.6 us
    ppermute x4, starting transfers between devices, row_swap(): return lax.ppermute(x, 'ha', route)  9.32 us
    ppermute x4, waiting for transfers between devices, row_swap(): return lax.ppermute(x, 'ha', route)  6.62 us
    ppermute x9, waiting for transfers between devices, ta_swap(): return lax.ppermute(x, 'ta', [(i, i ^ flip) for i in range(n_ta)])  4.57 us
  transfers between devices with their start and end apart: 17, of which 7 were waited for; matrix products, arithmetic and copies ran while one was open for 3% of the time, Pallas kernels for 12%

profile of v3, /device:TPU:65, one launch (start us, length us, event | category | flops | bytes accessed | tf_op | source)
XLA Modules:
  0.0 73.3 jit_solution(16882067741925520755)
XLA Ops:
  0.6 1.0 %pad_maximum_fusion.1.refs_0_ = bf16[384,256]{1,0:T(8,128)(2,1)S(1)} fusion(bf16[192,256]{1,0:T(8,128)(2,1)} %bitcast.19, bf16[192,256]{1,0:T(8,128)(2,1)} %bitcast.20), kind=kLoop, calls=%fused_computation.1 | loop fusion | flops 393216 | bytes 393216 | tf_op jit(solution)/shard_map/concatenate | solution.py:240
  1.6 6.1 %collective-permute-start.4 = (bf16[384,256]{1,0:T(8,128)(2,1)S(1)}, bf16[384,256]{1,0:T(8,128)(2,1)S(1)}, u32[]{:S(2)}, u32[]{:S(2)}) collective-permute-start(bf16[384,256]{1,0:T(8,128)(2,1)S(1)} %pad_maximum_fusion.1.refs_0_), channel_id=1, source_target_pairs={{16,32},{18,34},{20,36},{22,38},{24,40},{26,42},{28,44},{30,46},{3... | collective-permute-start | bytes 589832 | tf_op jit(solution)/shard_map/kv_row_1/ppermute | solution.py:222
  7.7 0.1 collective-permute-start.3
  7.8 1.0 %pad_maximum_fusion.refs_2_.refs_1_.refs_0_.refs_3_ = bf16[384,256]{1,0:T(8,128)(2,1)S(1)} fusion(bf16[192,256]{1,0:T(8,128)(2,1)} %bitcast.21, bf16[192,256]{1,0:T(8,128)(2,1)} %bitcast.22), kind=kLoop, calls=%fused_computation | loop fusion | flops 393216 | bytes 393216 | tf_op jit(solution)/shard_map/concatenate | solution.py:243
  8.8 2.6 %collective-permute-start.2 = (bf16[384,256]{1,0:T(8,128)(2,1)S(1)}, bf16[384,256]{1,0:T(8,128)(2,1)S(1)}, u32[]{:S(2)}, u32[]{:S(2)}) collective-permute-start(bf16[384,256]{1,0:T(8,128)(2,1)S(1)} %pad_maximum_fusion.refs_2_.refs_1_.refs_0_.refs_3_), channel_id=1, source_target_pairs={{0,192},{64,128},{128,64},{192,0},{1,193},{65,129},{129,65},{193,1... | collective-permute-start | bytes 589832 | tf_op jit(solution)/shard_map/query_ta/ppermute | solution.py:235
  11.3 0.5 collective-permute-start.1
  11.9 0.3 collective-permute-start
  12.2 0.7 dynamic-slice_bitcast_fusion.1
  12.9 3.6 %collective-permute-done.4.refs_2_ = bf16[384,256]{1,0:T(8,128)(2,1)S(1)} collective-permute-done((bf16[384,256]{1,0:T(8,128)(2,1)S(1)}, bf16[384,256]{1,0:T(8,128)(2,1)S(1)}, u32[]{:S(2)}, u32[]{:S(2)}) %collective-permute-start.4) | collective-permute-done | bytes 196640 | tf_op jit(solution)/shard_map/kv_row_1/ppermute | solution.py:222
  16.6 4.4 %collective-permute-start.6 = (bf16[1152,256]{1,0:T(8,128)(2,1)S(1)}, bf16[1152,256]{1,0:T(8,128)(2,1)S(1)}, u32[]{:S(2)}, u32[]{:S(2)}) collective-permute-start(bf16[1152,256]{1,0:T(8,128)(2,1)S(1)} %stack.1.refs_6_.refs_4_.refs_8_), channel_id=1, source_target_pairs={{2,4},{18,20},{34,36},{50,52},{6,8},{22,24},{38,40},{54,56},{10,12... | collective-permute-start | bytes 1769480 | tf_op jit(solution)/shard_map/kv_col_1/ppermute | solution.py:231
  21.0 0.1 collective-permute-start.5
  21.1 0.1 broadcast_add_fusion
  21.2 0.3 select_reduce_fusion
  21.5 0.1 and_select_fusion
  21.6 0.1 copy.12
  21.7 0.1 broadcast_in_dim.63
  21.7 0.1 reshape.144.refs_0_
  21.9 0.0 copy-start
  21.9 0.9 %copy-done = bf16[3,1,8,8,256]{4,3,2,1,0:T(8,128)(2,1)S(1)} copy-done((bf16[3,1,8,8,256]{4,3,2,1,0:T(8,128)(2,1)S(1)}, bf16[3,1,8,8,256]{4,3,2,1,0:T(8,128)(2,1)}, u32[]{:S(2)}) %copy-start) | copy-done | bytes 98328
  22.8 1.5 %scores.3 = (f32[2,576,768]{2,1,0:T(8,128)S(1)}, f32[8,768]{1,0:T(8,128)S(1)}) custom-call(f32[16,768]{1,0:T(8,128)S(1)} %reshape.144.refs_0_, bf16[192,256]{1,0:T(8,128)(2,1)S(1)} %bitcast.18, bf16[384,256]{1,0:T(8,128)(2,1)S(1)} %pad_maximum_fusion.refs_2_.refs_1_.refs_0_.refs_3_, ...), custom_call_target="tpu_custom_call" | custom-call | tf_op jit(solution)/shard_map/scores/pallas_call | solution.py:185
  24.2 1.3 %scores.4 = (f32[2,576,768]{2,1,0:T(8,128)S(1)}, f32[8,768]{1,0:T(8,128)S(1)}) custom-call(f32[16,768]{1,0:T(8,128)S(1)} %reshape.144.refs_0_, bf16[384,256]{1,0:T(8,128)(2,1)S(1)} %pad_maximum_fusion.refs_2_.refs_1_.refs_0_.refs_3_, bf16[384,256]{1,0:T(8,128)(2,1)S(1)} %collective-permute-done.refs_3_.refs_2_.refs_1_.refs_4_, ...), custom_call_target="tpu_custom_call" | custom-call | tf_op jit(solution)/shard_map/scores/pallas_call | solution.py:185
  25.5 8.6 %collective-permute-done.6.refs_5_.refs_4_.refs_8_.refs_10_ = bf16[1152,256]{1,0:T(8,128)(2,1)S(1)} collective-permute-done((bf16[1152,256]{1,0:T(8,128)(2,1)S(1)}, bf16[1152,256]{1,0:T(8,128)(2,1)S(1)}, u32[]{:S(2)}, u32[]{:S(2)}) %collective-permute-start.6) | collective-permute-done | bytes 589856 | tf_op jit(solution)/shard_map/kv_col_1/ppermute | solution.py:231
  34.1 1.3 %scores.5 = (f32[2,576,768]{2,1,0:T(8,128)S(1)}, f32[8,768]{1,0:T(8,128)S(1)}) custom-call(f32[16,768]{1,0:T(8,128)S(1)} %reshape.144.refs_0_, bf16[384,256]{1,0:T(8,128)(2,1)S(1)} %pad_maximum_fusion.refs_2_.refs_1_.refs_0_.refs_3_, bf16[384,256]{1,0:T(8,128)(2,1)S(1)} %collective-permute-done.refs_3_.refs_2_.refs_1_.refs_4_, ...), custom_call_target="tpu_custom_call" | custom-call | tf_op jit(solution)/shard_map/scores/pallas_call | solution.py:185
  35.4 2.6 %collective-permute-start.9 = (f32[8,768]{1,0:T(8,128)S(1)}, f32[8,768]{1,0:T(8,128)S(1)}, u32[]{:S(2)}, u32[]{:S(2)}) collective-permute-start(f32[8,768]{1,0:T(8,128)S(1)} %table.1.refs_3_), channel_id=1, source_target_pairs={{0,192},{64,128},{128,64},{192,0},{1,193},{65,129},{129,65},{193,1... | collective-permute-start | bytes 73736 | tf_op jit(solution)/shard_map/stats_ta/ppermute | solution.py:235
  38.0 0.5 collective-permute-start.8
  38.5 0.3 collective-permute-start.7
  38.8 0.6 product.5.refs_7_
  39.4 0.6 product.3.refs_7_
  40.0 0.6 product.4.refs_7_
  40.6 1.5 %collective-permute-done.8.refs_1_ = f32[8,768]{1,0:T(8,128)S(1)} collective-permute-done((f32[8,768]{1,0:T(8,128)S(1)}, f32[8,768]{1,0:T(8,128)S(1)}, u32[]{:S(2)}, u32[]{:S(2)}) %collective-permute-start.8) | collective-permute-done | bytes 24608 | tf_op jit(solution)/shard_map/stats_ta/ppermute | solution.py:235
  42.2 0.1 merge.1.refs_0_
  42.3 1.4 %grads.3 = (bf16[1152,256]{1,0:T(8,128)(2,1)S(1)}, bf16[2,576,768]{2,1,0:T(8,128)(2,1)S(1)}) custom-call(f32[8,768]{1,0:T(8,128)S(1)} %merge.1.refs_0_, f32[8,768]{1,0:T(8,128)S(1)} %get-tuple-element.26.refs_2_.refs_1_, f32[2,576,768]{2,1,0:T(8,128)S(1)} %get-tuple-element.32.refs_2_, bf16[384,256]{1,0:T(8,128)(2,1)S(1)} %pad_maximum_fusion.refs_2_.refs_1_.refs_0_.refs_3_, ...), custom_call_target="tpu_custom_call" | custom-call | tf_op jit(solution)/shard_map/grads/pallas_call | solution.py:185
  43.7 6.0 %collective-permute-start.13 = (bf16[1152,256]{1,0:T(8,128)(2,1)S(1)}, bf16[1152,256]{1,0:T(8,128)(2,1)S(1)}, u32[]{:S(2)}, u32[]{:S(2)}) collective-permute-start(bf16[1152,256]{1,0:T(8,128)(2,1)S(1)} %get-tuple-element.37), channel_id=1, source_target_pairs={{2,4},{18,20},{34,36},{50,52},{6,8},{22,24},{38,40},{54,56},{10,12... | collective-permute-start | bytes 1769480 | tf_op jit(solution)/shard_map/d_col_1/ppermute | solution.py:231
  49.7 2.3 %grads.4 = (bf16[1152,256]{1,0:T(8,128)(2,1)S(1)}, f32[768,256]{1,0:T(8,128)S(1)}) custom-call(f32[8,768]{1,0:T(8,128)S(1)} %merge.1.refs_0_, f32[8,768]{1,0:T(8,128)S(1)} %get-tuple-element.25.refs_1_, f32[2,576,768]{2,1,0:T(8,128)S(1)} %get-tuple-element.31.refs_2_, bf16[384,256]{1,0:T(8,128)(2,1)S(1)} %pad_maximum_fusion.refs_2_.refs_1_.refs_0_.refs_3_, ...), custom_call_target="tpu_custom_call" | custom-call | tf_op jit(solution)/shard_map/grads/pallas_call | solution.py:185
  52.0 0.1 collective-permute-start.14
  52.1 1.7 %grads.5 = (f32[1152,256]{1,0:T(8,128)S(1)}, f32[768,256]{1,0:T(8,128)S(1)}) custom-call(f32[8,768]{1,0:T(8,128)S(1)} %merge.1.refs_0_, f32[8,768]{1,0:T(8,128)S(1)} %get-tuple-element.24.refs_0_.refs_1_, f32[2,576,768]{2,1,0:T(8,128)S(1)} %get-tuple-element.30.refs_2_, bf16[384,256]{1,0:T(8,128)(2,1)S(1)} %pad_maximum_fusion.refs_2_.refs_1_.refs_0_.refs_3_, ...), custom_call_target="tpu_custom_call" | custom-call | tf_op jit(solution)/shard_map/grads/pallas_call | solution.py:185
  53.9 5.3 %collective-permute-done.13.y_ref = bf16[1152,256]{1,0:T(8,128)(2,1)S(1)} collective-permute-done((bf16[1152,256]{1,0:T(8,128)(2,1)S(1)}, bf16[1152,256]{1,0:T(8,128)(2,1)S(1)}, u32[]{:S(2)}, u32[]{:S(2)}) %collective-permute-start.13) | collective-permute-done | bytes 589856 | tf_op jit(solution)/shard_map/d_col_1/ppermute | solution.py:231
  59.1 0.1 add.161.mid_ref
  59.3 0.1 column.1
  59.4 0.4 collective-permute-start.15
  59.7 2.7 %collective-permute-start.16 = (bf16[384,256]{1,0:T(8,128)(2,1)S(1)}, bf16[384,256]{1,0:T(8,128)(2,1)S(1)}, u32[]{:S(2)}, u32[]{:S(2)}) collective-permute-start(bf16[384,256]{1,0:T(8,128)(2,1)S(1)} %get-tuple-element.41), channel_id=1, source_target_pairs={{16,32},{18,34},{20,36},{22,38},{24,40},{26,42},{28,44},{30,46},{3... | collective-permute-start | bytes 589832 | tf_op jit(solution)/shard_map/d_row_1/ppermute | solution.py:222
  62.5 1.2 %collective-permute-start.12 = (bf16[192,256]{1,0:T(8,128)(2,1)S(1)}, bf16[192,256]{1,0:T(8,128)(2,1)S(1)}, u32[]{:S(2)}, u32[]{:S(2)}) collective-permute-start(bf16[192,256]{1,0:T(8,128)(2,1)S(1)} %get-tuple-element.53), channel_id=1, source_target_pairs={{0,192},{64,128},{128,64},{192,0},{1,193},{65,129},{129,65},{193,1... | collective-permute-start | bytes 294920 | tf_op jit(solution)/shard_map/dq_ta/ppermute | solution.py:235
  63.7 0.3 collective-permute-start.11
  64.0 2.4 %collective-permute-start.10 = (bf16[192,256]{1,0:T(8,128)(2,1)S(1)}, bf16[192,256]{1,0:T(8,128)(2,1)S(1)}, u32[]{:S(2)}, u32[]{:S(2)}) collective-permute-start(bf16[192,256]{1,0:T(8,128)(2,1)S(1)} %get-tuple-element.55), channel_id=1, source_target_pairs={{0,128},{64,192},{128,0},{192,64},{1,129},{65,193},{129,1},{193,65... | collective-permute-start | bytes 294920 | tf_op jit(solution)/shard_map/dq_ta/ppermute | solution.py:235
  66.5 1.6 %collective-permute-done.12.c_ref = bf16[192,256]{1,0:T(8,128)(2,1)S(1)} collective-permute-done((bf16[192,256]{1,0:T(8,128)(2,1)S(1)}, bf16[192,256]{1,0:T(8,128)(2,1)S(1)}, u32[]{:S(2)}, u32[]{:S(2)}) %collective-permute-start.12) | collective-permute-done | bytes 98336 | tf_op jit(solution)/shard_map/dq_ta/ppermute | solution.py:235
  68.1 1.4 %collective-permute-done.10.a_ref = bf16[192,256]{1,0:T(8,128)(2,1)S(1)} collective-permute-done((bf16[192,256]{1,0:T(8,128)(2,1)S(1)}, bf16[192,256]{1,0:T(8,128)(2,1)S(1)}, u32[]{:S(2)}, u32[]{:S(2)}) %collective-permute-start.10) | collective-permute-done | bytes 98336 | tf_op jit(solution)/shard_map/dq_ta/ppermute | solution.py:235
  69.6 3.0 %collective-permute-done.16.b_ref = bf16[384,256]{1,0:T(8,128)(2,1)S(1)} collective-permute-done((bf16[384,256]{1,0:T(8,128)(2,1)S(1)}, bf16[384,256]{1,0:T(8,128)(2,1)S(1)}, u32[]{:S(2)}, u32[]{:S(2)}) %collective-permute-start.16) | collective-permute-done | bytes 196640 | tf_op jit(solution)/shard_map/d_row_1/ppermute | solution.py:222
  72.6 0.7 %finish.1 = (bf16[192,256]{1,0:T(8,128)(2,1)}, bf16[192,256]{1,0:T(8,128)(2,1)}, bf16[192,256]{1,0:T(8,128)(2,1)}) custom-call(bf16[192,256]{1,0:T(8,128)(2,1)S(1)} %query.1.dq_ref, f32[384,256]{1,0:T(8,128)S(1)} %get-tuple-element.39.own_ref, bf16[384,256]{1,0:T(8,128)(2,1)S(1)} %collective-permute-done.15.a_ref, ...), custom_call_target="tpu_custom_call" | custom-call | tf_op jit(solution)/shard_map/finish/pallas_call | solution.py:185
  (20 shorter events, 0.3 us)
Async XLA Ops:
  1.6 15.0 %collective-permute-start.4 = (bf16[384,256]{1,0:T(8,128)(2,1)S(1)}, bf16[384,256]{1,0:T(8,128)(2,1)S(1)}, u32[]{:S(2)}, u32[]{:S(2)}) collective-permute-start(bf16[384,256]{1,0:T(8,128)(2,1)S(1)} %pad_maximum_fusion.1.refs_0_), channel_id=1, source_target_pairs={{16,32},{18,34},{20,36},{22,38},{24,40},{26,42},{28,44},{30,46},{3... | collective-permute-start | bytes 589832 | tf_op jit(solution)/shard_map/kv_row_1/ppermute | solution.py:222
  7.7 8.9 %collective-permute-start.3 = (bf16[384,256]{1,0:T(8,128)(2,1)S(1)}, bf16[384,256]{1,0:T(8,128)(2,1)S(1)}, u32[]{:S(2)}, u32[]{:S(2)}) collective-permute-start(bf16[384,256]{1,0:T(8,128)(2,1)S(1)} %pad_maximum_fusion.1.refs_0_), channel_id=1, source_target_pairs={{0,16},{2,18},{4,20},{6,22},{8,24},{10,26},{12,28},{14,30},{32,48}... | collective-permute-start | bytes 589832 | tf_op jit(solution)/shard_map/kv_row_0/ppermute | solution.py:222
  8.8 13.1 %collective-permute-start.2 = (bf16[384,256]{1,0:T(8,128)(2,1)S(1)}, bf16[384,256]{1,0:T(8,128)(2,1)S(1)}, u32[]{:S(2)}, u32[]{:S(2)}) collective-permute-start(bf16[384,256]{1,0:T(8,128)(2,1)S(1)} %pad_maximum_fusion.refs_2_.refs_1_.refs_0_.refs_3_), channel_id=1, source_target_pairs={{0,192},{64,128},{128,64},{192,0},{1,193},{65,129},{129,65},{193,1... | collective-permute-start | bytes 589832 | tf_op jit(solution)/shard_map/query_ta/ppermute | solution.py:235
  11.3 10.5 %collective-permute-start.1 = (bf16[384,256]{1,0:T(8,128)(2,1)S(1)}, bf16[384,256]{1,0:T(8,128)(2,1)S(1)}, u32[]{:S(2)}, u32[]{:S(2)}) collective-permute-start(bf16[384,256]{1,0:T(8,128)(2,1)S(1)} %pad_maximum_fusion.refs_2_.refs_1_.refs_0_.refs_3_), channel_id=1, source_target_pairs={{0,128},{64,192},{128,0},{192,64},{1,129},{65,193},{129,1},{193,65... | collective-permute-start | bytes 589832 | tf_op jit(solution)/shard_map/query_ta/ppermute | solution.py:235
  11.9 10.0 %collective-permute-start = (bf16[384,256]{1,0:T(8,128)(2,1)S(1)}, bf16[384,256]{1,0:T(8,128)(2,1)S(1)}, u32[]{:S(2)}, u32[]{:S(2)}) collective-permute-start(bf16[384,256]{1,0:T(8,128)(2,1)S(1)} %pad_maximum_fusion.refs_2_.refs_1_.refs_0_.refs_3_), channel_id=1, source_target_pairs={{0,64},{64,0},{128,192},{192,128},{1,65},{65,1},{129,193},{193,129... | collective-permute-start | bytes 589832 | tf_op jit(solution)/shard_map/query_ta/ppermute | solution.py:235
  16.6 17.5 %collective-permute-start.6 = (bf16[1152,256]{1,0:T(8,128)(2,1)S(1)}, bf16[1152,256]{1,0:T(8,128)(2,1)S(1)}, u32[]{:S(2)}, u32[]{:S(2)}) collective-permute-start(bf16[1152,256]{1,0:T(8,128)(2,1)S(1)} %stack.1.refs_6_.refs_4_.refs_8_), channel_id=1, source_target_pairs={{2,4},{18,20},{34,36},{50,52},{6,8},{22,24},{38,40},{54,56},{10,12... | collective-permute-start | bytes 1769480 | tf_op jit(solution)/shard_map/kv_col_1/ppermute | solution.py:231
  21.0 3.2 %collective-permute-start.5 = (bf16[1152,256]{1,0:T(8,128)(2,1)S(1)}, bf16[1152,256]{1,0:T(8,128)(2,1)S(1)}, u32[]{:S(2)}, u32[]{:S(2)}) collective-permute-start(bf16[1152,256]{1,0:T(8,128)(2,1)S(1)} %stack.1.refs_6_.refs_4_.refs_8_), channel_id=1, source_target_pairs={{0,2},{16,18},{32,34},{48,50},{4,6},{20,22},{36,38},{52,54},{8,10}... | collective-permute-start | bytes 1769480 | tf_op jit(solution)/shard_map/kv_col_0/ppermute | solution.py:231
  21.9 0.9 %copy-start = (bf16[3,1,8,8,256]{4,3,2,1,0:T(8,128)(2,1)S(1)}, bf16[3,1,8,8,256]{4,3,2,1,0:T(8,128)(2,1)}, u32[]{:S(2)}) copy-start(bf16[3,1,8,8,256]{4,3,2,1,0:T(8,128)(2,1)} %param.9) | copy-start | bytes 294916
  35.4 5.2 %collective-permute-start.9 = (f32[8,768]{1,0:T(8,128)S(1)}, f32[8,768]{1,0:T(8,128)S(1)}, u32[]{:S(2)}, u32[]{:S(2)}) collective-permute-start(f32[8,768]{1,0:T(8,128)S(1)} %table.1.refs_3_), channel_id=1, source_target_pairs={{0,192},{64,128},{128,64},{192,0},{1,193},{65,129},{129,65},{193,1... | collective-permute-start | bytes 73736 | tf_op jit(solution)/shard_map/stats_ta/ppermute | solution.py:235
  38.0 4.2 %collective-permute-start.8 = (f32[8,768]{1,0:T(8,128)S(1)}, f32[8,768]{1,0:T(8,128)S(1)}, u32[]{:S(2)}, u32[]{:S(2)}) collective-permute-start(f32[8,768]{1,0:T(8,128)S(1)} %table.1.refs_3_), channel_id=1, source_target_pairs={{0,128},{64,192},{128,0},{192,64},{1,129},{65,193},{129,1},{193,65... | collective-permute-start | bytes 73736 | tf_op jit(solution)/shard_map/stats_ta/ppermute | solution.py:235
  38.5 3.7 %collective-permute-start.7 = (f32[8,768]{1,0:T(8,128)S(1)}, f32[8,768]{1,0:T(8,128)S(1)}, u32[]{:S(2)}, u32[]{:S(2)}) collective-permute-start(f32[8,768]{1,0:T(8,128)S(1)} %table.1.refs_3_), channel_id=1, source_target_pairs={{0,64},{64,0},{128,192},{192,128},{1,65},{65,1},{129,193},{193,129... | collective-permute-start | bytes 73736 | tf_op jit(solution)/shard_map/stats_ta/ppermute | solution.py:235
  43.7 15.5 %collective-permute-start.13 = (bf16[1152,256]{1,0:T(8,128)(2,1)S(1)}, bf16[1152,256]{1,0:T(8,128)(2,1)S(1)}, u32[]{:S(2)}, u32[]{:S(2)}) collective-permute-start(bf16[1152,256]{1,0:T(8,128)(2,1)S(1)} %get-tuple-element.37), channel_id=1, source_target_pairs={{2,4},{18,20},{34,36},{50,52},{6,8},{22,24},{38,40},{54,56},{10,12... | collective-permute-start | bytes 1769480 | tf_op jit(solution)/shard_map/d_col_1/ppermute | solution.py:231
  52.0 7.3 %collective-permute-start.14 = (bf16[1152,256]{1,0:T(8,128)(2,1)S(1)}, bf16[1152,256]{1,0:T(8,128)(2,1)S(1)}, u32[]{:S(2)}, u32[]{:S(2)}) collective-permute-start(bf16[1152,256]{1,0:T(8,128)(2,1)S(1)} %get-tuple-element.38), channel_id=1, source_target_pairs={{0,2},{16,18},{32,34},{48,50},{4,6},{20,22},{36,38},{52,54},{8,10}... | collective-permute-start | bytes 1769480 | tf_op jit(solution)/shard_map/d_col_0/ppermute | solution.py:231
  59.4 10.2 %collective-permute-start.15 = (bf16[384,256]{1,0:T(8,128)(2,1)S(1)}, bf16[384,256]{1,0:T(8,128)(2,1)S(1)}, u32[]{:S(2)}, u32[]{:S(2)}) collective-permute-start(bf16[384,256]{1,0:T(8,128)(2,1)S(1)} %get-tuple-element.40), channel_id=1, source_target_pairs={{0,16},{2,18},{4,20},{6,22},{8,24},{10,26},{12,28},{14,30},{32,48}... | collective-permute-start | bytes 589832 | tf_op jit(solution)/shard_map/d_row_0/ppermute | solution.py:222
  59.7 12.8 %collective-permute-start.16 = (bf16[384,256]{1,0:T(8,128)(2,1)S(1)}, bf16[384,256]{1,0:T(8,128)(2,1)S(1)}, u32[]{:S(2)}, u32[]{:S(2)}) collective-permute-start(bf16[384,256]{1,0:T(8,128)(2,1)S(1)} %get-tuple-element.41), channel_id=1, source_target_pairs={{16,32},{18,34},{20,36},{22,38},{24,40},{26,42},{28,44},{30,46},{3... | collective-permute-start | bytes 589832 | tf_op jit(solution)/shard_map/d_row_1/ppermute | solution.py:222
  62.5 5.6 %collective-permute-start.12 = (bf16[192,256]{1,0:T(8,128)(2,1)S(1)}, bf16[192,256]{1,0:T(8,128)(2,1)S(1)}, u32[]{:S(2)}, u32[]{:S(2)}) collective-permute-start(bf16[192,256]{1,0:T(8,128)(2,1)S(1)} %get-tuple-element.53), channel_id=1, source_target_pairs={{0,192},{64,128},{128,64},{192,0},{1,193},{65,129},{129,65},{193,1... | collective-permute-start | bytes 294920 | tf_op jit(solution)/shard_map/dq_ta/ppermute | solution.py:235
  63.7 4.4 %collective-permute-start.11 = (bf16[192,256]{1,0:T(8,128)(2,1)S(1)}, bf16[192,256]{1,0:T(8,128)(2,1)S(1)}, u32[]{:S(2)}, u32[]{:S(2)}) collective-permute-start(bf16[192,256]{1,0:T(8,128)(2,1)S(1)} %get-tuple-element.54), channel_id=1, source_target_pairs={{0,64},{64,0},{128,192},{192,128},{1,65},{65,1},{129,193},{193,129... | collective-permute-start | bytes 294920 | tf_op jit(solution)/shard_map/dq_ta/ppermute | solution.py:235
  64.0 5.5 %collective-permute-start.10 = (bf16[192,256]{1,0:T(8,128)(2,1)S(1)}, bf16[192,256]{1,0:T(8,128)(2,1)S(1)}, u32[]{:S(2)}, u32[]{:S(2)}) collective-permute-start(bf16[192,256]{1,0:T(8,128)(2,1)S(1)} %get-tuple-element.55), channel_id=1, source_target_pairs={{0,128},{64,192},{128,0},{192,64},{1,129},{65,193},{129,1},{193,65... | collective-permute-start | bytes 294920 | tf_op jit(solution)/shard_map/dq_ta/ppermute | solution.py:235

commit v4 on v3

--- a/solution.py
+++ b/solution.py
@@ -96,7 +96,7 @@
 
 def merge_kernel(heads, rows, *refs):
     *tables, out_ref = refs
-    tables = [reordered(ref[...], rows, flip) for flip, ref in zip((1, 2, 3, 0), tables)]
+    tables = [reordered(ref[...], rows, flip) for flip, ref in zip((1, 3, 2, 0), tables)]
     out_ref[...] = jnp.zeros_like(out_ref)
     top = functools.reduce(jnp.maximum, [t[0:heads] for t in tables])
     total = sum(t[heads : 2 * heads] * jnp.exp2(t[0:heads] - top) for t in tables)
@@ -289,7 +289,7 @@
     w_b, s_b = scores(2, kv_right)
     mine = call(functools.partial(table_kernel, heads), stat_shape, s_mid, s_a, s_b)
     swapped = {flip: ta_swap(mine, flip, "stats_ta") for flip in (2, 1, 3)}
-    others = tuple(swapped[flip] for flip in (1, 2, 3))
+    others = tuple(swapped[flip] for flip in (1, 3, 2))
     p_mid, p_a, p_b = products(kv_mid), products(kv_left), products(kv_right)
     others = after(others, p_a, p_b, p_mid)
     lse = call(functools.partial(merge_kernel, heads, rows), stat_shape, *others, mine)
@@ -309,7 +309,7 @@
     d_a = col_swap(d_a, 0, "d_col_0")
     d_mid, dq = grads(2, s_mid, w_mid, p_mid, kv_mid, F32, dq)
     dq = dq.reshape(n_ta, rows, width)
-    dq_parts = [ta_swap(dq[flip].astype(BF16), flip, "dq_ta") for flip in (2, 1, 3)]
+    dq_parts = [ta_swap(dq[flip].astype(BF16), flip, "dq_ta") for flip in (1, 3, 2)]
     d_mid = call(add_kernel, jax.ShapeDtypeStruct(d_mid.shape, F32), d_mid, d_b)
     own = jax.ShapeDtypeStruct((2 * rows, width), F32)
     sent = jax.ShapeDtypeStruct((2 * rows, width), BF16)

time: 73.9 us -> 73.6 us (level)
  starting transfers between devices: 30.5 us -> 29.7 us
  waiting for transfers between devices: 25.1 us -> 25.9 us
    ppermute x9, starting transfers between devices: 10.6 us -> 9.77 us  [ta_swap(): return lax.ppermute(x, 'ta', [(i, i ^ flip) for i in range(n_ta)])]
where the time goes in v4:
time: 73.6 us; the launch traced here: 73.3 us
  starting transfers between devices  29.7 us (40%)
  waiting for transfers between devices  25.9 us (35%)
  Pallas kernels  12.4 us (17%)
  other arithmetic  2.46 us (3%)
  local copies, waits for them, and re-layouts  1.9 us (3%)
  between operations  0.93 us (1%)
    ppermute x4, waiting for transfers between devices, col_swap(): return lax.ppermute(x, 'ha', route)  13.9 us
    pallas_call x16, Pallas kernels, call(): pl.pallas_call(kernel, out_shape=out_shape, in_specs=[vmem] * len(args),...  12.4 us
    ppermute x4, starting transfers between devices, col_swap(): return lax.ppermute(x, 'ha', route)  10.6 us
    ppermute x9, starting transfers between devices, ta_swap(): return lax.ppermute(x, 'ta', [(i, i ^ flip) for i in range(n_ta)])  9.77 us
    ppermute x4, starting transfers between devices, row_swap(): return lax.ppermute(x, 'ha', route)  9.32 us
    ppermute x4, waiting for transfers between devices, row_swap(): return lax.ppermute(x, 'ha', route)  7.01 us
    ppermute x9, waiting for transfers between devices, ta_swap(): return lax.ppermute(x, 'ta', [(i, i ^ flip) for i in range(n_ta)])  5.01 us
  transfers between devices with their start and end apart: 17, of which 7 were waited for; matrix products, arithmetic and copies ran while one was open for 3% of the time, Pallas kernels for 12%

profile of v4, /device:TPU:65, one launch (start us, length us, event | category | flops | bytes accessed | tf_op | source)
XLA Modules:
  0.0 73.3 jit_solution(11660236523294879677)
XLA Ops:
  0.6 1.0 %pad_maximum_fusion.1.refs_0_ = bf16[384,256]{1,0:T(8,128)(2,1)S(1)} fusion(bf16[192,256]{1,0:T(8,128)(2,1)} %bitcast.19, bf16[192,256]{1,0:T(8,128)(2,1)} %bitcast.20), kind=kLoop, calls=%fused_computation.1 | loop fusion | flops 393216 | bytes 393216 | tf_op jit(solution)/shard_map/concatenate | solution.py:240
  1.6 6.1 %collective-permute-start.4 = (bf16[384,256]{1,0:T(8,128)(2,1)S(1)}, bf16[384,256]{1,0:T(8,128)(2,1)S(1)}, u32[]{:S(2)}, u32[]{:S(2)}) collective-permute-start(bf16[384,256]{1,0:T(8,128)(2,1)S(1)} %pad_maximum_fusion.1.refs_0_), channel_id=1, source_target_pairs={{16,32},{18,34},{20,36},{22,38},{24,40},{26,42},{28,44},{30,46},{3... | collective-permute-start | bytes 589832 | tf_op jit(solution)/shard_map/kv_row_1/ppermute | solution.py:222
  7.7 0.1 collective-permute-start.3
  7.8 1.0 %pad_maximum_fusion.refs_2_.refs_1_.refs_0_.refs_3_ = bf16[384,256]{1,0:T(8,128)(2,1)S(1)} fusion(bf16[192,256]{1,0:T(8,128)(2,1)} %bitcast.21, bf16[192,256]{1,0:T(8,128)(2,1)} %bitcast.22), kind=kLoop, calls=%fused_computation | loop fusion | flops 393216 | bytes 393216 | tf_op jit(solution)/shard_map/concatenate | solution.py:243
  8.8 2.6 %collective-permute-start.2 = (bf16[384,256]{1,0:T(8,128)(2,1)S(1)}, bf16[384,256]{1,0:T(8,128)(2,1)S(1)}, u32[]{:S(2)}, u32[]{:S(2)}) collective-permute-start(bf16[384,256]{1,0:T(8,128)(2,1)S(1)} %pad_maximum_fusion.refs_2_.refs_1_.refs_0_.refs_3_), channel_id=1, source_target_pairs={{0,192},{64,128},{128,64},{192,0},{1,193},{65,129},{129,65},{193,1... | collective-permute-start | bytes 589832 | tf_op jit(solution)/shard_map/query_ta/ppermute | solution.py:235
  11.3 0.5 collective-permute-start.1
  11.9 0.3 collective-permute-start
  12.2 0.7 dynamic-slice_bitcast_fusion.1
  12.9 3.6 %collective-permute-done.4.refs_2_ = bf16[384,256]{1,0:T(8,128)(2,1)S(1)} collective-permute-done((bf16[384,256]{1,0:T(8,128)(2,1)S(1)}, bf16[384,256]{1,0:T(8,128)(2,1)S(1)}, u32[]{:S(2)}, u32[]{:S(2)}) %collective-permute-start.4) | collective-permute-done | bytes 196640 | tf_op jit(solution)/shard_map/kv_row_1/ppermute | solution.py:222
  16.6 4.4 %collective-permute-start.6 = (bf16[1152,256]{1,0:T(8,128)(2,1)S(1)}, bf16[1152,256]{1,0:T(8,128)(2,1)S(1)}, u32[]{:S(2)}, u32[]{:S(2)}) collective-permute-start(bf16[1152,256]{1,0:T(8,128)(2,1)S(1)} %stack.1.refs_6_.refs_4_.refs_8_), channel_id=1, source_target_pairs={{2,4},{18,20},{34,36},{50,52},{6,8},{22,24},{38,40},{54,56},{10,12... | collective-permute-start | bytes 1769480 | tf_op jit(solution)/shard_map/kv_col_1/ppermute | solution.py:231
  21.0 0.1 collective-permute-start.5
  21.1 0.1 broadcast_add_fusion
  21.2 0.3 select_reduce_fusion
  21.5 0.1 and_select_fusion
  21.6 0.1 copy.12
  21.7 0.1 broadcast_in_dim.63
  21.7 0.1 reshape.144.refs_0_
  21.9 0.0 collective-permute-done.refs_3_.refs_2_.refs_1_.refs_4_
  21.9 0.0 copy-start
  21.9 0.9 %copy-done = bf16[3,1,8,8,256]{4,3,2,1,0:T(8,128)(2,1)S(1)} copy-done((bf16[3,1,8,8,256]{4,3,2,1,0:T(8,128)(2,1)S(1)}, bf16[3,1,8,8,256]{4,3,2,1,0:T(8,128)(2,1)}, u32[]{:S(2)}) %copy-start) | copy-done | bytes 98328
  22.8 1.5 %scores.3 = (f32[2,576,768]{2,1,0:T(8,128)S(1)}, f32[8,768]{1,0:T(8,128)S(1)}) custom-call(f32[16,768]{1,0:T(8,128)S(1)} %reshape.144.refs_0_, bf16[192,256]{1,0:T(8,128)(2,1)S(1)} %bitcast.18, bf16[384,256]{1,0:T(8,128)(2,1)S(1)} %pad_maximum_fusion.refs_2_.refs_1_.refs_0_.refs_3_, ...), custom_call_target="tpu_custom_call" | custom-call | tf_op jit(solution)/shard_map/scores/pallas_call | solution.py:185
  24.2 1.3 %scores.4 = (f32[2,576,768]{2,1,0:T(8,128)S(1)}, f32[8,768]{1,0:T(8,128)S(1)}) custom-call(f32[16,768]{1,0:T(8,128)S(1)} %reshape.144.refs_0_, bf16[384,256]{1,0:T(8,128)(2,1)S(1)} %pad_maximum_fusion.refs_2_.refs_1_.refs_0_.refs_3_, bf16[384,256]{1,0:T(8,128)(2,1)S(1)} %collective-permute-done.refs_3_.refs_2_.refs_1_.refs_4_, ...), custom_call_target="tpu_custom_call" | custom-call | tf_op jit(solution)/shard_map/scores/pallas_call | solution.py:185
  25.5 8.6 %collective-permute-done.6.refs_5_.refs_4_.refs_8_.refs_10_ = bf16[1152,256]{1,0:T(8,128)(2,1)S(1)} collective-permute-done((bf16[1152,256]{1,0:T(8,128)(2,1)S(1)}, bf16[1152,256]{1,0:T(8,128)(2,1)S(1)}, u32[]{:S(2)}, u32[]{:S(2)}) %collective-permute-start.6) | collective-permute-done | bytes 589856 | tf_op jit(solution)/shard_map/kv_col_1/ppermute | solution.py:231
  34.1 1.3 %scores.5 = (f32[2,576,768]{2,1,0:T(8,128)S(1)}, f32[8,768]{1,0:T(8,128)S(1)}) custom-call(f32[16,768]{1,0:T(8,128)S(1)} %reshape.144.refs_0_, bf16[384,256]{1,0:T(8,128)(2,1)S(1)} %pad_maximum_fusion.refs_2_.refs_1_.refs_0_.refs_3_, bf16[384,256]{1,0:T(8,128)(2,1)S(1)} %collective-permute-done.refs_3_.refs_2_.refs_1_.refs_4_, ...), custom_call_target="tpu_custom_call" | custom-call | tf_op jit(solution)/shard_map/scores/pallas_call | solution.py:185
  35.4 2.8 %collective-permute-start.9 = (f32[8,768]{1,0:T(8,128)S(1)}, f32[8,768]{1,0:T(8,128)S(1)}, u32[]{:S(2)}, u32[]{:S(2)}) collective-permute-start(f32[8,768]{1,0:T(8,128)S(1)} %table.1.refs_3_), channel_id=1, source_target_pairs={{0,128},{64,192},{128,0},{192,64},{1,129},{65,193},{129,1},{193,65... | collective-permute-start | bytes 73736 | tf_op jit(solution)/shard_map/stats_ta/ppermute | solution.py:235
  38.3 0.9 %collective-permute-start.8 = (f32[8,768]{1,0:T(8,128)S(1)}, f32[8,768]{1,0:T(8,128)S(1)}, u32[]{:S(2)}, u32[]{:S(2)}) collective-permute-start(f32[8,768]{1,0:T(8,128)S(1)} %table.1.refs_3_), channel_id=1, source_target_pairs={{0,192},{64,128},{128,64},{192,0},{1,193},{65,129},{129,65},{193,1... | collective-permute-start | bytes 73736 | tf_op jit(solution)/shard_map/stats_ta/ppermute | solution.py:235
  39.1 0.6 product.5.refs_7_
  39.7 0.6 product.3.refs_7_
  40.4 0.6 product.4.refs_7_
  41.0 1.1 %collective-permute-done.8.refs_1_ = f32[8,768]{1,0:T(8,128)S(1)} collective-permute-done((f32[8,768]{1,0:T(8,128)S(1)}, f32[8,768]{1,0:T(8,128)S(1)}, u32[]{:S(2)}, u32[]{:S(2)}) %collective-permute-start.8) | collective-permute-done | bytes 24608 | tf_op jit(solution)/shard_map/stats_ta/ppermute | solution.py:235
  42.1 0.1 merge.1.refs_0_
  42.3 1.4 %grads.3 = (bf16[1152,256]{1,0:T(8,128)(2,1)S(1)}, bf16[2,576,768]{2,1,0:T(8,128)(2,1)S(1)}) custom-call(f32[8,768]{1,0:T(8,128)S(1)} %merge.1.refs_0_, f32[8,768]{1,0:T(8,128)S(1)} %get-tuple-element.26.refs_2_.refs_1_, f32[2,576,768]{2,1,0:T(8,128)S(1)} %get-tuple-element.32.refs_2_, bf16[384,256]{1,0:T(8,128)(2,1)S(1)} %pad_maximum_fusion.refs_2_.refs_1_.refs_0_.refs_3_, ...), custom_call_target="tpu_custom_call" | custom-call | tf_op jit(solution)/shard_map/grads/pallas_call | solution.py:185
  43.7 6.0 %collective-permute-start.13 = (bf16[1152,256]{1,0:T(8,128)(2,1)S(1)}, bf16[1152,256]{1,0:T(8,128)(2,1)S(1)}, u32[]{:S(2)}, u32[]{:S(2)}) collective-permute-start(bf16[1152,256]{1,0:T(8,128)(2,1)S(1)} %get-tuple-element.37), channel_id=1, source_target_pairs={{2,4},{18,20},{34,36},{50,52},{6,8},{22,24},{38,40},{54,56},{10,12... | collective-permute-start | bytes 1769480 | tf_op jit(solution)/shard_map/d_col_1/ppermute | solution.py:231
  49.7 2.3 %grads.4 = (bf16[1152,256]{1,0:T(8,128)(2,1)S(1)}, f32[768,256]{1,0:T(8,128)S(1)}) custom-call(f32[8,768]{1,0:T(8,128)S(1)} %merge.1.refs_0_, f32[8,768]{1,0:T(8,128)S(1)} %get-tuple-element.25.refs_1_, f32[2,576,768]{2,1,0:T(8,128)S(1)} %get-tuple-element.31.refs_2_, bf16[384,256]{1,0:T(8,128)(2,1)S(1)} %pad_maximum_fusion.refs_2_.refs_1_.refs_0_.refs_3_, ...), custom_call_target="tpu_custom_call" | custom-call | tf_op jit(solution)/shard_map/grads/pallas_call | solution.py:185
  51.9 0.1 collective-permute-start.14
  52.0 1.7 %grads.5 = (f32[1152,256]{1,0:T(8,128)S(1)}, f32[768,256]{1,0:T(8,128)S(1)}) custom-call(f32[8,768]{1,0:T(8,128)S(1)} %merge.1.refs_0_, f32[8,768]{1,0:T(8,128)S(1)} %get-tuple-element.24.refs_0_.refs_1_, f32[2,576,768]{2,1,0:T(8,128)S(1)} %get-tuple-element.30.refs_2_, bf16[384,256]{1,0:T(8,128)(2,1)S(1)} %pad_maximum_fusion.refs_2_.refs_1_.refs_0_.refs_3_, ...), custom_call_target="tpu_custom_call" | custom-call | tf_op jit(solution)/shard_map/grads/pallas_call | solution.py:185
  53.8 5.3 %collective-permute-done.13.y_ref = bf16[1152,256]{1,0:T(8,128)(2,1)S(1)} collective-permute-done((bf16[1152,256]{1,0:T(8,128)(2,1)S(1)}, bf16[1152,256]{1,0:T(8,128)(2,1)S(1)}, u32[]{:S(2)}, u32[]{:S(2)}) %collective-permute-start.13) | collective-permute-done | bytes 589856 | tf_op jit(solution)/shard_map/d_col_1/ppermute | solution.py:231
  59.1 0.1 add.161.mid_ref
  59.2 0.1 column.1
  59.3 0.4 collective-permute-start.15
  59.7 2.7 %collective-permute-start.16 = (bf16[384,256]{1,0:T(8,128)(2,1)S(1)}, bf16[384,256]{1,0:T(8,128)(2,1)S(1)}, u32[]{:S(2)}, u32[]{:S(2)}) collective-permute-start(bf16[384,256]{1,0:T(8,128)(2,1)S(1)} %get-tuple-element.41), channel_id=1, source_target_pairs={{16,32},{18,34},{20,36},{22,38},{24,40},{26,42},{28,44},{30,46},{3... | collective-permute-start | bytes 589832 | tf_op jit(solution)/shard_map/d_row_1/ppermute | solution.py:222
  62.5 1.4 %collective-permute-start.12 = (bf16[192,256]{1,0:T(8,128)(2,1)S(1)}, bf16[192,256]{1,0:T(8,128)(2,1)S(1)}, u32[]{:S(2)}, u32[]{:S(2)}) collective-permute-start(bf16[192,256]{1,0:T(8,128)(2,1)S(1)} %get-tuple-element.53), channel_id=1, source_target_pairs={{0,128},{64,192},{128,0},{192,64},{1,129},{65,193},{129,1},{193,65... | collective-permute-start | bytes 294920 | tf_op jit(solution)/shard_map/dq_ta/ppermute | solution.py:235
  63.9 0.9 %collective-permute-start.11 = (bf16[192,256]{1,0:T(8,128)(2,1)S(1)}, bf16[192,256]{1,0:T(8,128)(2,1)S(1)}, u32[]{:S(2)}, u32[]{:S(2)}) collective-permute-start(bf16[192,256]{1,0:T(8,128)(2,1)S(1)} %get-tuple-element.54), channel_id=1, source_target_pairs={{0,192},{64,128},{128,64},{192,0},{1,193},{65,129},{129,65},{193,1... | collective-permute-start | bytes 294920 | tf_op jit(solution)/shard_map/dq_ta/ppermute | solution.py:235
  64.7 0.5 collective-permute-start.10
  65.2 3.4 %collective-permute-done.12.c_ref = bf16[192,256]{1,0:T(8,128)(2,1)S(1)} collective-permute-done((bf16[192,256]{1,0:T(8,128)(2,1)S(1)}, bf16[192,256]{1,0:T(8,128)(2,1)S(1)}, u32[]{:S(2)}, u32[]{:S(2)}) %collective-permute-start.12) | collective-permute-done | bytes 98336 | tf_op jit(solution)/shard_map/dq_ta/ppermute | solution.py:235
  68.7 0.4 collective-permute-done.11.b_ref
  69.2 3.4 %collective-permute-done.16.b_ref = bf16[384,256]{1,0:T(8,128)(2,1)S(1)} collective-permute-done((bf16[384,256]{1,0:T(8,128)(2,1)S(1)}, bf16[384,256]{1,0:T(8,128)(2,1)S(1)}, u32[]{:S(2)}, u32[]{:S(2)}) %collective-permute-start.16) | collective-permute-done | bytes 196640 | tf_op jit(solution)/shard_map/d_row_1/ppermute | solution.py:222
  72.5 0.7 %finish.1 = (bf16[192,256]{1,0:T(8,128)(2,1)}, bf16[192,256]{1,0:T(8,128)(2,1)}, bf16[192,256]{1,0:T(8,128)(2,1)}) custom-call(bf16[192,256]{1,0:T(8,128)(2,1)S(1)} %query.1.dq_ref, f32[384,256]{1,0:T(8,128)S(1)} %get-tuple-element.39.own_ref, bf16[384,256]{1,0:T(8,128)(2,1)S(1)} %collective-permute-done.15.a_ref, ...), custom_call_target="tpu_custom_call" | custom-call | tf_op jit(solution)/shard_map/finish/pallas_call | solution.py:185
  (20 shorter events, 0.3 us)
Async XLA Ops:
  1.6 15.0 %collective-permute-start.4 = (bf16[384,256]{1,0:T(8,128)(2,1)S(1)}, bf16[384,256]{1,0:T(8,128)(2,1)S(1)}, u32[]{:S(2)}, u32[]{:S(2)}) collective-permute-start(bf16[384,256]{1,0:T(8,128)(2,1)S(1)} %pad_maximum_fusion.1.refs_0_), channel_id=1, source_target_pairs={{16,32},{18,34},{20,36},{22,38},{24,40},{26,42},{28,44},{30,46},{3... | collective-permute-start | bytes 589832 | tf_op jit(solution)/shard_map/kv_row_1/ppermute | solution.py:222
  7.7 8.9 %collective-permute-start.3 = (bf16[384,256]{1,0:T(8,128)(2,1)S(1)}, bf16[384,256]{1,0:T(8,128)(2,1)S(1)}, u32[]{:S(2)}, u32[]{:S(2)}) collective-permute-start(bf16[384,256]{1,0:T(8,128)(2,1)S(1)} %pad_maximum_fusion.1.refs_0_), channel_id=1, source_target_pairs={{0,16},{2,18},{4,20},{6,22},{8,24},{10,26},{12,28},{14,30},{32,48}... | collective-permute-start | bytes 589832 | tf_op jit(solution)/shard_map/kv_row_0/ppermute | solution.py:222
  8.8 13.1 %collective-permute-start.2 = (bf16[384,256]{1,0:T(8,128)(2,1)S(1)}, bf16[384,256]{1,0:T(8,128)(2,1)S(1)}, u32[]{:S(2)}, u32[]{:S(2)}) collective-permute-start(bf16[384,256]{1,0:T(8,128)(2,1)S(1)} %pad_maximum_fusion.refs_2_.refs_1_.refs_0_.refs_3_), channel_id=1, source_target_pairs={{0,192},{64,128},{128,64},{192,0},{1,193},{65,129},{129,65},{193,1... | collective-permute-start | bytes 589832 | tf_op jit(solution)/shard_map/query_ta/ppermute | solution.py:235
  11.3 10.5 %collective-permute-start.1 = (bf16[384,256]{1,0:T(8,128)(2,1)S(1)}, bf16[384,256]{1,0:T(8,128)(2,1)S(1)}, u32[]{:S(2)}, u32[]{:S(2)}) collective-permute-start(bf16[384,256]{1,0:T(8,128)(2,1)S(1)} %pad_maximum_fusion.refs_2_.refs_1_.refs_0_.refs_3_), channel_id=1, source_target_pairs={{0,128},{64,192},{128,0},{192,64},{1,129},{65,193},{129,1},{193,65... | collective-permute-start | bytes 589832 | tf_op jit(solution)/shard_map/query_ta/ppermute | solution.py:235
  11.9 10.0 %collective-permute-start = (bf16[384,256]{1,0:T(8,128)(2,1)S(1)}, bf16[384,256]{1,0:T(8,128)(2,1)S(1)}, u32[]{:S(2)}, u32[]{:S(2)}) collective-permute-start(bf16[384,256]{1,0:T(8,128)(2,1)S(1)} %pad_maximum_fusion.refs_2_.refs_1_.refs_0_.refs_3_), channel_id=1, source_target_pairs={{0,64},{64,0},{128,192},{192,128},{1,65},{65,1},{129,193},{193,129... | collective-permute-start | bytes 589832 | tf_op jit(solution)/shard_map/query_ta/ppermute | solution.py:235
  16.6 17.5 %collective-permute-start.6 = (bf16[1152,256]{1,0:T(8,128)(2,1)S(1)}, bf16[1152,256]{1,0:T(8,128)(2,1)S(1)}, u32[]{:S(2)}, u32[]{:S(2)}) collective-permute-start(bf16[1152,256]{1,0:T(8,128)(2,1)S(1)} %stack.1.refs_6_.refs_4_.refs_8_), channel_id=1, source_target_pairs={{2,4},{18,20},{34,36},{50,52},{6,8},{22,24},{38,40},{54,56},{10,12... | collective-permute-start | bytes 1769480 | tf_op jit(solution)/shard_map/kv_col_1/ppermute | solution.py:231
  21.0 3.2 %collective-permute-start.5 = (bf16[1152,256]{1,0:T(8,128)(2,1)S(1)}, bf16[1152,256]{1,0:T(8,128)(2,1)S(1)}, u32[]{:S(2)}, u32[]{:S(2)}) collective-permute-start(bf16[1152,256]{1,0:T(8,128)(2,1)S(1)} %stack.1.refs_6_.refs_4_.refs_8_), channel_id=1, source_target_pairs={{0,2},{16,18},{32,34},{48,50},{4,6},{20,22},{36,38},{52,54},{8,10}... | collective-permute-start | bytes 1769480 | tf_op jit(solution)/shard_map/kv_col_0/ppermute | solution.py:231
  21.9 0.9 %copy-start = (bf16[3,1,8,8,256]{4,3,2,1,0:T(8,128)(2,1)S(1)}, bf16[3,1,8,8,256]{4,3,2,1,0:T(8,128)(2,1)}, u32[]{:S(2)}) copy-start(bf16[3,1,8,8,256]{4,3,2,1,0:T(8,128)(2,1)} %param.9) | copy-start | bytes 294916
  35.4 5.6 %collective-permute-start.9 = (f32[8,768]{1,0:T(8,128)S(1)}, f32[8,768]{1,0:T(8,128)S(1)}, u32[]{:S(2)}, u32[]{:S(2)}) collective-permute-start(f32[8,768]{1,0:T(8,128)S(1)} %table.1.refs_3_), channel_id=1, source_target_pairs={{0,128},{64,192},{128,0},{192,64},{1,129},{65,193},{129,1},{193,65... | collective-permute-start | bytes 73736 | tf_op jit(solution)/shard_map/stats_ta/ppermute | solution.py:235
  38.3 3.9 %collective-permute-start.8 = (f32[8,768]{1,0:T(8,128)S(1)}, f32[8,768]{1,0:T(8,128)S(1)}, u32[]{:S(2)}, u32[]{:S(2)}) collective-permute-start(f32[8,768]{1,0:T(8,128)S(1)} %table.1.refs_3_), channel_id=1, source_target_pairs={{0,192},{64,128},{128,64},{192,0},{1,193},{65,129},{129,65},{193,1... | collective-permute-start | bytes 73736 | tf_op jit(solution)/shard_map/stats_ta/ppermute | solution.py:235
  39.1 3.0 %collective-permute-start.7 = (f32[8,768]{1,0:T(8,128)S(1)}, f32[8,768]{1,0:T(8,128)S(1)}, u32[]{:S(2)}, u32[]{:S(2)}) collective-permute-start(f32[8,768]{1,0:T(8,128)S(1)} %table.1.refs_3_), channel_id=1, source_target_pairs={{0,64},{64,0},{128,192},{192,128},{1,65},{65,1},{129,193},{193,129... | collective-permute-start | bytes 73736 | tf_op jit(solution)/shard_map/stats_ta/ppermute | solution.py:235
  43.7 15.5 %collective-permute-start.13 = (bf16[1152,256]{1,0:T(8,128)(2,1)S(1)}, bf16[1152,256]{1,0:T(8,128)(2,1)S(1)}, u32[]{:S(2)}, u32[]{:S(2)}) collective-permute-start(bf16[1152,256]{1,0:T(8,128)(2,1)S(1)} %get-tuple-element.37), channel_id=1, source_target_pairs={{2,4},{18,20},{34,36},{50,52},{6,8},{22,24},{38,40},{54,56},{10,12... | collective-permute-start | bytes 1769480 | tf_op jit(solution)/shard_map/d_col_1/ppermute | solution.py:231
  51.9 7.3 %collective-permute-start.14 = (bf16[1152,256]{1,0:T(8,128)(2,1)S(1)}, bf16[1152,256]{1,0:T(8,128)(2,1)S(1)}, u32[]{:S(2)}, u32[]{:S(2)}) collective-permute-start(bf16[1152,256]{1,0:T(8,128)(2,1)S(1)} %get-tuple-element.38), channel_id=1, source_target_pairs={{0,2},{16,18},{32,34},{48,50},{4,6},{20,22},{36,38},{52,54},{8,10}... | collective-permute-start | bytes 1769480 | tf_op jit(solution)/shard_map/d_col_0/ppermute | solution.py:231
  59.3 9.8 %collective-permute-start.15 = (bf16[384,256]{1,0:T(8,128)(2,1)S(1)}, bf16[384,256]{1,0:T(8,128)(2,1)S(1)}, u32[]{:S(2)}, u32[]{:S(2)}) collective-permute-start(bf16[384,256]{1,0:T(8,128)(2,1)S(1)} %get-tuple-element.40), channel_id=1, source_target_pairs={{0,16},{2,18},{4,20},{6,22},{8,24},{10,26},{12,28},{14,30},{32,48}... | collective-permute-start | bytes 589832 | tf_op jit(solution)/shard_map/d_row_0/ppermute | solution.py:222
  59.7 12.8 %collective-permute-start.16 = (bf16[384,256]{1,0:T(8,128)(2,1)S(1)}, bf16[384,256]{1,0:T(8,128)(2,1)S(1)}, u32[]{:S(2)}, u32[]{:S(2)}) collective-permute-start(bf16[384,256]{1,0:T(8,128)(2,1)S(1)} %get-tuple-element.41), channel_id=1, source_target_pairs={{16,32},{18,34},{20,36},{22,38},{24,40},{26,42},{28,44},{30,46},{3... | collective-permute-start | bytes 589832 | tf_op jit(solution)/shard_map/d_row_1/ppermute | solution.py:222
  62.5 6.2 %collective-permute-start.12 = (bf16[192,256]{1,0:T(8,128)(2,1)S(1)}, bf16[192,256]{1,0:T(8,128)(2,1)S(1)}, u32[]{:S(2)}, u32[]{:S(2)}) collective-permute-start(bf16[192,256]{1,0:T(8,128)(2,1)S(1)} %get-tuple-element.53), channel_id=1, source_target_pairs={{0,128},{64,192},{128,0},{192,64},{1,129},{65,193},{129,1},{193,65... | collective-permute-start | bytes 294920 | tf_op jit(solution)/shard_map/dq_ta/ppermute | solution.py:235
  63.9 5.2 %collective-permute-start.11 = (bf16[192,256]{1,0:T(8,128)(2,1)S(1)}, bf16[192,256]{1,0:T(8,128)(2,1)S(1)}, u32[]{:S(2)}, u32[]{:S(2)}) collective-permute-start(bf16[192,256]{1,0:T(8,128)(2,1)S(1)} %get-tuple-element.54), channel_id=1, source_target_pairs={{0,192},{64,128},{128,64},{192,0},{1,193},{65,129},{129,65},{193,1... | collective-permute-start | bytes 294920 | tf_op jit(solution)/shard_map/dq_ta/ppermute | solution.py:235
  64.7 4.4 %collective-permute-start.10 = (bf16[192,256]{1,0:T(8,128)(2,1)S(1)}, bf16[192,256]{1,0:T(8,128)(2,1)S(1)}, u32[]{:S(2)}, u32[]{:S(2)}) collective-permute-start(bf16[192,256]{1,0:T(8,128)(2,1)S(1)} %get-tuple-element.55), channel_id=1, source_target_pairs={{0,64},{64,0},{128,192},{192,128},{1,65},{65,1},{129,193},{193,129... | collective-permute-start | bytes 294920 | tf_op jit(solution)/shard_map/dq_ta/ppermute | solution.py:235

commit v5 on v4

--- a/solution.py
+++ b/solution.py
@@ -34,11 +34,25 @@
     )
 
 
-def stack_kernel(rows, *refs):
-    *parts, out_ref = refs
+def both_kernel(x_ref, y_ref, out_ref):
+    rows = x_ref.shape[0]
+    out_ref[pl.ds(0, rows), :] = x_ref[...]
+    out_ref[pl.ds(rows, rows), :] = y_ref[...]
+
+
+def stack_kernel(rows, own, near_a, near_b, far_a, far_b, other, mid_ref, right_ref):
     for half in range(2):
-        for i, ref in enumerate(parts):
-            out_ref[pl.ds((3 * half + i) * rows, rows), :] = ref[pl.ds(half * rows, rows), :]
+        place = pl.ds(half * rows, rows)
+        beside = pl.ds((2 + half) * rows, rows)
+        blocks = (own[place, :], near_a[place, :] + far_a[place, :], near_b[place, :] + far_b[place, :])
+        others = (other[place, :], far_a[beside, :], far_b[beside, :])
+        for i in range(3):
+            mid_ref[pl.ds((3 * half + i) * rows, rows), :] = blocks[i]
+            right_ref[pl.ds((3 * half + i) * rows, rows), :] = others[i]
+
+
+def join_kernel(x_ref, y_ref, out_ref):
+    out_ref[...] = x_ref[...] + y_ref[...]
 
 
 def scores_kernel(position, *refs):
@@ -212,23 +226,27 @@
         ends = [(i, i + 1) for i in range(first, count - 1, 2)]
         return ends + [(d, s) for s, d in ends]
 
-    def row_swap(x, first, name):
+    far = (col_tiles // 2 - 1, col_tiles // 2)
+    near = [c for c in range(col_tiles) if c not in far]
+
+    def row_swap(x, first, columns, name):
         route = [
             (s * col_tiles + c, d * col_tiles + c)
             for s, d in pairs(row_tiles, first)
-            for c in range(col_tiles)
+            for c in columns
         ]
         with jax.named_scope(name):
             return lax.ppermute(x, "ha", route)
 
-    def col_swap(x, first, name):
-        route = [
-            (r * col_tiles + s, r * col_tiles + d)
-            for s, d in pairs(col_tiles, first)
-            for r in range(row_tiles)
-        ]
+    def col_swap(x, ends, name):
+        route = [(r * col_tiles + s, r * col_tiles + d) for s, d in ends for r in range(row_tiles)]
         with jax.named_scope(name):
             return lax.ppermute(x, "ha", route)
+
+    inner = pairs(col_tiles, 0)
+    outer = pairs(col_tiles, 1)
+    middle = [pair for pair in outer if pair[0] in far]
+    outside = [pair for pair in outer if pair[0] not in far]
 
     def ta_swap(x, flip, name):
         with jax.named_scope(name):
@@ -238,15 +256,24 @@
         x.reshape(rows, width) for x in (query_in, key_in, value_in, saved_out, out_grad)
     )
     kv = jnp.concatenate([k, v], axis=0)
-    kv_b = row_swap(kv, 1, "kv_row_1")
-    kv_a = row_swap(kv, 0, "kv_row_0")
+    kv_far = col_swap(kv, middle, "kv_far")
+    kv_b = row_swap(kv, 1, near, "kv_row_1")
+    kv_a = row_swap(kv, 0, near, "kv_row_0")
     qg = jnp.concatenate([q, g], axis=0)
     swapped = {flip: ta_swap(qg, flip, "query_ta") for flip in (2, 1, 3)}
     pieces = [qg] + [swapped[flip] for flip in (1, 2, 3)]
+    two_shape = jax.ShapeDtypeStruct((4 * rows, width), BF16)
     stack_shape = jax.ShapeDtypeStruct((6 * rows, width), BF16)
-    kv_mid = call(functools.partial(stack_kernel, rows), stack_shape, kv, kv_a, kv_b)
-    kv_right = col_swap(kv_mid, 1, "kv_col_1")
-    kv_left = col_swap(kv_mid, 0, "kv_col_0")
+    both = call(both_kernel, two_shape, kv, kv_far)
+    both_b = row_swap(both, 1, far, "far_row_1")
+    both_a = row_swap(both, 0, far, "far_row_0")
+    kv_mid, kv_right = call(
+        functools.partial(stack_kernel, rows), (stack_shape, stack_shape),
+        kv, kv_a, kv_b, both_a, both_b, kv_far,
+    )
+    kv_out = col_swap(kv_mid, outside, "kv_col_1")
+    kv_left = col_swap(kv_mid, inner, "kv_col_0")
+    kv_right = call(join_kernel, stack_shape, kv_right, kv_out)
 
     place = jnp.arange(16, dtype=jnp.int32)
     row_step = jnp.where(place < 9, place % 3, 0)
@@ -304,20 +331,20 @@
         )
 
     d_b, kept = grads(0, s_b, w_b, p_b, kv_right, BF16)
-    d_b = col_swap(d_b, 1, "d_col_1")
+    d_b = col_swap(d_b, outer, "d_col_1")
     d_a, dq = grads(1, s_a, w_a, p_a, kv_left, BF16, kept, kv_right)
-    d_a = col_swap(d_a, 0, "d_col_0")
+    d_a = col_swap(d_a, inner, "d_col_0")
     d_mid, dq = grads(2, s_mid, w_mid, p_mid, kv_mid, F32, dq)
     dq = dq.reshape(n_ta, rows, width)
-    dq_parts = [ta_swap(dq[flip].astype(BF16), flip, "dq_ta") for flip in (1, 3, 2)]
+    dq_parts = [ta_swap(dq[flip], flip, "dq_ta") for flip in (1, 3, 2)]
     d_mid = call(add_kernel, jax.ShapeDtypeStruct(d_mid.shape, F32), d_mid, d_b)
     own = jax.ShapeDtypeStruct((2 * rows, width), F32)
     sent = jax.ShapeDtypeStruct((2 * rows, width), BF16)
     own, to_a, to_b = call(
         functools.partial(column_kernel, rows), (own, sent, sent), d_mid, d_a
     )
-    d_b = row_swap(to_b, 1, "d_row_1")
-    d_a = row_swap(to_a, 0, "d_row_0")
+    d_b = row_swap(to_b, 1, range(col_tiles), "d_row_1")
+    d_a = row_swap(to_a, 0, range(col_tiles), "d_row_0")
     one = jax.ShapeDtypeStruct((rows, width), BF16)
     dq = call(query_kernel, one, dq[0], *dq_parts)
     outs = call(finish_kernel, (one, one, one), dq, own, d_a, d_b)

time: 73.6 us -> 73.9 us (level)
  starting transfers between devices: 29.7 us -> 36.4 us
  waiting for transfers between devices: 25.9 us -> 20.2 us
  local copies, waits for them, and re-layouts: 1.9 us -> 1.04 us
    ppermute x4 -> x5, waiting for transfers between devices: 13.9 us -> 8.68 us  [col_swap(): return lax.ppermute(x, 'ha', route)]
    ppermute x4 -> x6, starting transfers between devices: 9.32 us -> 13 us  [row_swap(): return lax.ppermute(x, 'ha', route)]
    ppermute x9, waiting for transfers between devices: 5.01 us -> 2.16 us  [ta_swap(): return lax.ppermute(x, 'ta', [(i, i ^ flip) for i in range(n_ta)])]
    ppermute x4 -> x6, waiting for transfers between devices: 7.01 us -> 9.37 us  [row_swap(): return lax.ppermute(x, 'ha', route)]
    ppermute x4 -> x5, starting transfers between devices: 10.6 us -> 12.4 us  [col_swap(): return lax.ppermute(x, 'ha', route)]
    ppermute x9, starting transfers between devices: 9.77 us -> 11.1 us  [ta_swap(): return lax.ppermute(x, 'ta', [(i, i ^ flip) for i in range(n_ta)])]
    unnamed x2, local copies, waits for them, and re-layouts: 0.89 us -> 0.01 us
    pallas_call x16 -> x18, Pallas kernels: 12.4 us -> 12.5 us  [call(): pl.pallas_call(kernel, out_shape=out_shape, in_specs=[vmem] * len(args),...]
  transfers between devices with their start and end apart: 17 -> 20, of which waited for: 7 -> 7; matrix products, arithmetic and copies ran while one was open for 3% -> 3% of each run, Pallas kernels for 12% -> 12%
where the time goes in v5:
time: 73.9 us; the launch traced here: 73.6 us
  starting transfers between devices  36.4 us (49%)
  waiting for transfers between devices  20.2 us (27%)
  Pallas kernels  12.5 us (17%)
  other arithmetic  2.45 us (3%)
  local copies, waits for them, and re-layouts  1.04 us (1%)
  between operations  0.89 us (1%)
    ppermute x6, starting transfers between devices, row_swap(): return lax.ppermute(x, 'ha', route)  13 us
    pallas_call x18, Pallas kernels, call(): pl.pallas_call(kernel, out_shape=out_shape, in_specs=[vmem] * len(args),...  12.5 us
    ppermute x5, starting transfers between devices, col_swap(): return lax.ppermute(x, 'ha', route)  12.4 us
    ppermute x9, starting transfers between devices, ta_swap(): return lax.ppermute(x, 'ta', [(i, i ^ flip) for i in range(n_ta)])  11.1 us
    ppermute x6, waiting for transfers between devices, row_swap(): return lax.ppermute(x, 'ha', route)  9.37 us
    ppermute x5, waiting for transfers between devices, col_swap(): return lax.ppermute(x, 'ha', route)  8.68 us
    ppermute x9, waiting for transfers between devices, ta_swap(): return lax.ppermute(x, 'ta', [(i, i ^ flip) for i in range(n_ta)])  2.16 us
  transfers between devices with their start and end apart: 20, of which 7 were waited for; matrix products, arithmetic and copies ran while one was open for 3% of the time, Pallas kernels for 12%

profile of v5, /device:TPU:65, one launch (start us, length us, event | category | flops | bytes accessed | tf_op | source)
XLA Modules:
  0.0 73.6 jit_solution(18172989373202103290)
XLA Ops:
  0.6 1.0 %pad_maximum_fusion.1.x_ref.own = bf16[384,256]{1,0:T(8,128)(2,1)S(1)} fusion(bf16[192,256]{1,0:T(8,128)(2,1)} %bitcast.19, bf16[192,256]{1,0:T(8,128)(2,1)} %bitcast.20), kind=kLoop, calls=%fused_computation.1 | loop fusion | flops 393216 | bytes 393216 | tf_op jit(solution)/shard_map/concatenate | solution.py:258
  1.6 0.7 collective-permute-start.5
  2.3 6.1 %collective-permute-start.4 = (bf16[384,256]{1,0:T(8,128)(2,1)S(1)}, bf16[384,256]{1,0:T(8,128)(2,1)S(1)}, u32[]{:S(2)}, u32[]{:S(2)}) collective-permute-start(bf16[384,256]{1,0:T(8,128)(2,1)S(1)} %pad_maximum_fusion.1.x_ref.own), channel_id=1, source_target_pairs={{16,32},{18,34},{20,36},{26,42},{28,44},{30,46},{32,16},{34,18},{3... | collective-permute-start | bytes 589832 | tf_op jit(solution)/shard_map/kv_row_1/ppermute | solution.py:239
  8.4 1.9 %collective-permute-start.3 = (bf16[384,256]{1,0:T(8,128)(2,1)S(1)}, bf16[384,256]{1,0:T(8,128)(2,1)S(1)}, u32[]{:S(2)}, u32[]{:S(2)}) collective-permute-start(bf16[384,256]{1,0:T(8,128)(2,1)S(1)} %pad_maximum_fusion.1.x_ref.own), channel_id=1, source_target_pairs={{0,16},{2,18},{4,20},{10,26},{12,28},{14,30},{32,48},{34,50},{36,5... | collective-permute-start | bytes 589832 | tf_op jit(solution)/shard_map/kv_row_0/ppermute | solution.py:239
  10.4 1.0 %pad_maximum_fusion.refs_2_.refs_1_.refs_0_.refs_3_ = bf16[384,256]{1,0:T(8,128)(2,1)S(1)} fusion(bf16[192,256]{1,0:T(8,128)(2,1)} %bitcast.21, bf16[192,256]{1,0:T(8,128)(2,1)} %bitcast.22), kind=kLoop, calls=%fused_computation | loop fusion | flops 393216 | bytes 393216 | tf_op jit(solution)/shard_map/concatenate | solution.py:262
  11.3 2.6 %collective-permute-start.2 = (bf16[384,256]{1,0:T(8,128)(2,1)S(1)}, bf16[384,256]{1,0:T(8,128)(2,1)S(1)}, u32[]{:S(2)}, u32[]{:S(2)}) collective-permute-start(bf16[384,256]{1,0:T(8,128)(2,1)S(1)} %pad_maximum_fusion.refs_2_.refs_1_.refs_0_.refs_3_), channel_id=1, source_target_pairs={{0,192},{64,128},{128,64},{192,0},{1,193},{65,129},{129,65},{193,1... | collective-permute-start | bytes 589832 | tf_op jit(solution)/shard_map/query_ta/ppermute | solution.py:253
  13.9 0.7 collective-permute-start.7
  14.6 0.7 collective-permute-start.6
  15.4 0.7 dynamic-slice_bitcast_fusion.1
  16.1 1.8 %collective-permute-start.1 = (bf16[384,256]{1,0:T(8,128)(2,1)S(1)}, bf16[384,256]{1,0:T(8,128)(2,1)S(1)}, u32[]{:S(2)}, u32[]{:S(2)}) collective-permute-start(bf16[384,256]{1,0:T(8,128)(2,1)S(1)} %pad_maximum_fusion.refs_2_.refs_1_.refs_0_.refs_3_), channel_id=1, source_target_pairs={{0,128},{64,192},{128,0},{192,64},{1,129},{65,193},{129,1},{193,65... | collective-permute-start | bytes 589832 | tf_op jit(solution)/shard_map/query_ta/ppermute | solution.py:253
  17.9 0.3 collective-permute-start
  18.3 0.1 stack.1
  18.4 5.7 %collective-permute-start.9 = (bf16[1152,256]{1,0:T(8,128)(2,1)S(1)}, bf16[1152,256]{1,0:T(8,128)(2,1)S(1)}, u32[]{:S(2)}, u32[]{:S(2)}) collective-permute-start(bf16[1152,256]{1,0:T(8,128)(2,1)S(1)} %get-tuple-element.26.refs_6_.refs_4_.refs_8_), channel_id=1, source_target_pairs={{2,4},{18,20},{34,36},{50,52},{10,12},{26,28},{42,44},{58,60},{4,2... | collective-permute-start | bytes 1769480 | tf_op jit(solution)/shard_map/kv_col_1/ppermute | solution.py:244
  24.0 0.1 collective-permute-start.8
  24.2 0.3 select_reduce_fusion
  24.5 0.1 and_select_fusion
  24.6 0.1 copy.12
  24.7 0.1 broadcast_in_dim.63
  24.8 0.1 reshape.144.refs_0_
  24.9 1.3 %collective-permute-done.refs_3_.refs_2_.refs_1_.refs_4_ = bf16[384,256]{1,0:T(8,128)(2,1)S(1)} collective-permute-done((bf16[384,256]{1,0:T(8,128)(2,1)S(1)}, bf16[384,256]{1,0:T(8,128)(2,1)S(1)}, u32[]{:S(2)}, u32[]{:S(2)}) %collective-permute-start) | collective-permute-done | bytes 196640 | tf_op jit(solution)/shard_map/query_ta/ppermute | solution.py:253
  26.2 1.5 %scores.3 = (f32[2,576,768]{2,1,0:T(8,128)S(1)}, f32[8,768]{1,0:T(8,128)S(1)}) custom-call(f32[16,768]{1,0:T(8,128)S(1)} %reshape.144.refs_0_, bf16[192,256]{1,0:T(8,128)(2,1)S(1)} %bitcast.18, bf16[384,256]{1,0:T(8,128)(2,1)S(1)} %pad_maximum_fusion.refs_2_.refs_1_.refs_0_.refs_3_, ...), custom_call_target="tpu_custom_call" | custom-call | tf_op jit(solution)/shard_map/scores/pallas_call | solution.py:199
  27.7 1.3 %scores.4 = (f32[2,576,768]{2,1,0:T(8,128)S(1)}, f32[8,768]{1,0:T(8,128)S(1)}) custom-call(f32[16,768]{1,0:T(8,128)S(1)} %reshape.144.refs_0_, bf16[384,256]{1,0:T(8,128)(2,1)S(1)} %pad_maximum_fusion.refs_2_.refs_1_.refs_0_.refs_3_, bf16[384,256]{1,0:T(8,128)(2,1)S(1)} %collective-permute-done.refs_3_.refs_2_.refs_1_.refs_4_, ...), custom_call_target="tpu_custom_call" | custom-call | tf_op jit(solution)/shard_map/scores/pallas_call | solution.py:199
  28.9 2.6 %collective-permute-done.9.y_ref = bf16[1152,256]{1,0:T(8,128)(2,1)S(1)} collective-permute-done((bf16[1152,256]{1,0:T(8,128)(2,1)S(1)}, bf16[1152,256]{1,0:T(8,128)(2,1)S(1)}, u32[]{:S(2)}, u32[]{:S(2)}) %collective-permute-start.9) | collective-permute-done | bytes 589856 | tf_op jit(solution)/shard_map/kv_col_1/ppermute | solution.py:244
  31.6 1.3 %scores.5 = (f32[2,576,768]{2,1,0:T(8,128)S(1)}, f32[8,768]{1,0:T(8,128)S(1)}) custom-call(f32[16,768]{1,0:T(8,128)S(1)} %reshape.144.refs_0_, bf16[384,256]{1,0:T(8,128)(2,1)S(1)} %pad_maximum_fusion.refs_2_.refs_1_.refs_0_.refs_3_, bf16[384,256]{1,0:T(8,128)(2,1)S(1)} %collective-permute-done.refs_3_.refs_2_.refs_1_.refs_4_, ...), custom_call_target="tpu_custom_call" | custom-call | tf_op jit(solution)/shard_map/scores/pallas_call | solution.py:199
  32.9 1.8 %collective-permute-start.12 = (f32[8,768]{1,0:T(8,128)S(1)}, f32[8,768]{1,0:T(8,128)S(1)}, u32[]{:S(2)}, u32[]{:S(2)}) collective-permute-start(f32[8,768]{1,0:T(8,128)S(1)} %table.1.refs_3_), channel_id=1, source_target_pairs={{0,128},{64,192},{128,0},{192,64},{1,129},{65,193},{129,1},{193,65... | collective-permute-start | bytes 73736 | tf_op jit(solution)/shard_map/stats_ta/ppermute | solution.py:253
  34.7 1.8 %collective-permute-start.11 = (f32[8,768]{1,0:T(8,128)S(1)}, f32[8,768]{1,0:T(8,128)S(1)}, u32[]{:S(2)}, u32[]{:S(2)}) collective-permute-start(f32[8,768]{1,0:T(8,128)S(1)} %table.1.refs_3_), channel_id=1, source_target_pairs={{0,192},{64,128},{128,64},{192,0},{1,193},{65,129},{129,65},{193,1... | collective-permute-start | bytes 73736 | tf_op jit(solution)/shard_map/stats_ta/ppermute | solution.py:253
  36.6 0.6 product.5.refs_7_
  37.2 0.6 product.3.refs_7_
  37.8 0.6 product.4.refs_7_
  38.4 0.5 collective-permute-done.11.refs_1_
  39.0 0.3 collective-permute-done.10.refs_0_
  39.2 0.1 merge.1.refs_0_
  39.3 1.4 %grads.3 = (bf16[1152,256]{1,0:T(8,128)(2,1)S(1)}, bf16[2,576,768]{2,1,0:T(8,128)(2,1)S(1)}) custom-call(f32[8,768]{1,0:T(8,128)S(1)} %merge.1.refs_0_, f32[8,768]{1,0:T(8,128)S(1)} %get-tuple-element.30.refs_2_.refs_1_, f32[2,576,768]{2,1,0:T(8,128)S(1)} %get-tuple-element.36.refs_2_, bf16[384,256]{1,0:T(8,128)(2,1)S(1)} %pad_maximum_fusion.refs_2_.refs_1_.refs_0_.refs_3_, ...), custom_call_target="tpu_custom_call" | custom-call | tf_op jit(solution)/shard_map/grads/pallas_call | solution.py:199
  40.7 5.8 %collective-permute-start.16 = (bf16[1152,256]{1,0:T(8,128)(2,1)S(1)}, bf16[1152,256]{1,0:T(8,128)(2,1)S(1)}, u32[]{:S(2)}, u32[]{:S(2)}) collective-permute-start(bf16[1152,256]{1,0:T(8,128)(2,1)S(1)} %get-tuple-element.41), channel_id=1, source_target_pairs={{2,4},{18,20},{34,36},{50,52},{6,8},{22,24},{38,40},{54,56},{10,12... | collective-permute-start | bytes 1769480 | tf_op jit(solution)/shard_map/d_col_1/ppermute | solution.py:244
  46.6 2.3 %grads.4 = (bf16[1152,256]{1,0:T(8,128)(2,1)S(1)}, f32[768,256]{1,0:T(8,128)S(1)}) custom-call(f32[8,768]{1,0:T(8,128)S(1)} %merge.1.refs_0_, f32[8,768]{1,0:T(8,128)S(1)} %get-tuple-element.28.refs_1_, f32[2,576,768]{2,1,0:T(8,128)S(1)} %get-tuple-element.35.refs_2_, bf16[384,256]{1,0:T(8,128)(2,1)S(1)} %pad_maximum_fusion.refs_2_.refs_1_.refs_0_.refs_3_, ...), custom_call_target="tpu_custom_call" | custom-call | tf_op jit(solution)/shard_map/grads/pallas_call | solution.py:199
  48.9 0.1 collective-permute-start.17
  49.0 1.7 %grads.5 = (f32[1152,256]{1,0:T(8,128)S(1)}, f32[768,256]{1,0:T(8,128)S(1)}) custom-call(f32[8,768]{1,0:T(8,128)S(1)} %merge.1.refs_0_, f32[8,768]{1,0:T(8,128)S(1)} %get-tuple-element.27.refs_0_.refs_1_, f32[2,576,768]{2,1,0:T(8,128)S(1)} %get-tuple-element.34.refs_2_, bf16[384,256]{1,0:T(8,128)(2,1)S(1)} %pad_maximum_fusion.refs_2_.refs_1_.refs_0_.refs_3_, ...), custom_call_target="tpu_custom_call" | custom-call | tf_op jit(solution)/shard_map/grads/pallas_call | solution.py:199
  50.8 1.4 %collective-permute-start.15 = (f32[192,256]{1,0:T(8,128)S(1)}, f32[192,256]{1,0:T(8,128)S(1)}, u32[]{:S(2)}, u32[]{:S(2)}) collective-permute-start(f32[192,256]{1,0:T(8,128)S(1)} %get-tuple-element.57), channel_id=1, source_target_pairs={{0,128},{64,192},{128,0},{192,64},{1,129},{65,193},{129,1},{193,65... | collective-permute-start | bytes 589832 | tf_op jit(solution)/shard_map/dq_ta/ppermute | solution.py:253
  52.1 1.0 %collective-permute-start.14 = (f32[192,256]{1,0:T(8,128)S(1)}, f32[192,256]{1,0:T(8,128)S(1)}, u32[]{:S(2)}, u32[]{:S(2)}) collective-permute-start(f32[192,256]{1,0:T(8,128)S(1)} %get-tuple-element.58), channel_id=1, source_target_pairs={{0,192},{64,128},{128,64},{192,0},{1,193},{65,129},{129,65},{193,1... | collective-permute-start | bytes 589832 | tf_op jit(solution)/shard_map/dq_ta/ppermute | solution.py:253
  53.1 0.4 collective-permute-start.13
  53.5 6.0 %collective-permute-done.16.y_ref = bf16[1152,256]{1,0:T(8,128)(2,1)S(1)} collective-permute-done((bf16[1152,256]{1,0:T(8,128)(2,1)S(1)}, bf16[1152,256]{1,0:T(8,128)(2,1)S(1)}, u32[]{:S(2)}, u32[]{:S(2)}) %collective-permute-start.16) | collective-permute-done | bytes 589856 | tf_op jit(solution)/shard_map/d_col_1/ppermute | solution.py:244
  59.5 0.1 add.161.mid_ref
  59.7 0.1 column.1
  59.8 0.4 collective-permute-start.18
  60.2 3.2 %collective-permute-start.19 = (bf16[384,256]{1,0:T(8,128)(2,1)S(1)}, bf16[384,256]{1,0:T(8,128)(2,1)S(1)}, u32[]{:S(2)}, u32[]{:S(2)}) collective-permute-start(bf16[384,256]{1,0:T(8,128)(2,1)S(1)} %get-tuple-element.45), channel_id=1, source_target_pairs={{16,32},{18,34},{20,36},{22,38},{24,40},{26,42},{28,44},{30,46},{3... | collective-permute-start | bytes 589832 | tf_op jit(solution)/shard_map/d_row_1/ppermute | solution.py:239
  63.4 1.9 %collective-permute-done.18.a_ref = bf16[384,256]{1,0:T(8,128)(2,1)S(1)} collective-permute-done((bf16[384,256]{1,0:T(8,128)(2,1)S(1)}, bf16[384,256]{1,0:T(8,128)(2,1)S(1)}, u32[]{:S(2)}, u32[]{:S(2)}) %collective-permute-start.18) | collective-permute-done | bytes 196640 | tf_op jit(solution)/shard_map/d_row_0/ppermute | solution.py:239
  65.4 7.5 %collective-permute-done.19.b_ref = bf16[384,256]{1,0:T(8,128)(2,1)S(1)} collective-permute-done((bf16[384,256]{1,0:T(8,128)(2,1)S(1)}, bf16[384,256]{1,0:T(8,128)(2,1)S(1)}, u32[]{:S(2)}, u32[]{:S(2)}) %collective-permute-start.19) | collective-permute-done | bytes 196640 | tf_op jit(solution)/shard_map/d_row_1/ppermute | solution.py:239
  72.8 0.7 %finish.1 = (bf16[192,256]{1,0:T(8,128)(2,1)}, bf16[192,256]{1,0:T(8,128)(2,1)}, bf16[192,256]{1,0:T(8,128)(2,1)}) custom-call(bf16[192,256]{1,0:T(8,128)(2,1)S(1)} %query.1.dq_ref, f32[384,256]{1,0:T(8,128)S(1)} %get-tuple-element.43.own_ref, bf16[384,256]{1,0:T(8,128)(2,1)S(1)} %collective-permute-done.18.a_ref, ...), custom_call_target="tpu_custom_call" | custom-call | tf_op jit(solution)/shard_map/finish/pallas_call | solution.py:199
  (26 shorter events, 0.4 us)
Async XLA Ops:
  0.6 25.6 %copy-start = (bf16[3,1,8,8,256]{4,3,2,1,0:T(8,128)(2,1)S(1)}, bf16[3,1,8,8,256]{4,3,2,1,0:T(8,128)(2,1)}, u32[]{:S(2)}) copy-start(bf16[3,1,8,8,256]{4,3,2,1,0:T(8,128)(2,1)} %param.9) | copy-start | bytes 294916
  1.6 12.3 %collective-permute-start.5 = (bf16[384,256]{1,0:T(8,128)(2,1)S(1)}, bf16[384,256]{1,0:T(8,128)(2,1)S(1)}, u32[]{:S(2)}, u32[]{:S(2)}) collective-permute-start(bf16[384,256]{1,0:T(8,128)(2,1)S(1)} %pad_maximum_fusion.1.x_ref.own), channel_id=1, source_target_pairs={{6,8},{22,24},{38,40},{54,56},{8,6},{24,22},{40,38},{56,54},{7,9},... | collective-permute-start | bytes 589832 | tf_op jit(solution)/shard_map/kv_far/ppermute | solution.py:244
  2.3 13.8 %collective-permute-start.4 = (bf16[384,256]{1,0:T(8,128)(2,1)S(1)}, bf16[384,256]{1,0:T(8,128)(2,1)S(1)}, u32[]{:S(2)}, u32[]{:S(2)}) collective-permute-start(bf16[384,256]{1,0:T(8,128)(2,1)S(1)} %pad_maximum_fusion.1.x_ref.own), channel_id=1, source_target_pairs={{16,32},{18,34},{20,36},{26,42},{28,44},{30,46},{32,16},{34,18},{3... | collective-permute-start | bytes 589832 | tf_op jit(solution)/shard_map/kv_row_1/ppermute | solution.py:239
  8.4 9.5 %collective-permute-start.3 = (bf16[384,256]{1,0:T(8,128)(2,1)S(1)}, bf16[384,256]{1,0:T(8,128)(2,1)S(1)}, u32[]{:S(2)}, u32[]{:S(2)}) collective-permute-start(bf16[384,256]{1,0:T(8,128)(2,1)S(1)} %pad_maximum_fusion.1.x_ref.own), channel_id=1, source_target_pairs={{0,16},{2,18},{4,20},{10,26},{12,28},{14,30},{32,48},{34,50},{36,5... | collective-permute-start | bytes 589832 | tf_op jit(solution)/shard_map/kv_row_0/ppermute | solution.py:239
  11.3 13.5 %collective-permute-start.2 = (bf16[384,256]{1,0:T(8,128)(2,1)S(1)}, bf16[384,256]{1,0:T(8,128)(2,1)S(1)}, u32[]{:S(2)}, u32[]{:S(2)}) collective-permute-start(bf16[384,256]{1,0:T(8,128)(2,1)S(1)} %pad_maximum_fusion.refs_2_.refs_1_.refs_0_.refs_3_), channel_id=1, source_target_pairs={{0,192},{64,128},{128,64},{192,0},{1,193},{65,129},{129,65},{193,1... | collective-permute-start | bytes 589832 | tf_op jit(solution)/shard_map/query_ta/ppermute | solution.py:253
  13.9 4.3 %collective-permute-start.7 = (bf16[768,256]{1,0:T(8,128)(2,1)S(1)}, bf16[768,256]{1,0:T(8,128)(2,1)S(1)}, u32[]{:S(2)}, u32[]{:S(2)}) collective-permute-start(bf16[768,256]{1,0:T(8,128)(2,1)S(1)} %both.1), channel_id=1, source_target_pairs={{22,38},{24,40},{38,22},{40,24},{23,39},{25,41},{39,23},{41,25},{8... | collective-permute-start | bytes 1179656 | tf_op jit(solution)/shard_map/far_row_1/ppermute | solution.py:239
  14.6 3.6 %collective-permute-start.6 = (bf16[768,256]{1,0:T(8,128)(2,1)S(1)}, bf16[768,256]{1,0:T(8,128)(2,1)S(1)}, u32[]{:S(2)}, u32[]{:S(2)}) collective-permute-start(bf16[768,256]{1,0:T(8,128)(2,1)S(1)} %both.1), channel_id=1, source_target_pairs={{6,22},{8,24},{38,54},{40,56},{22,6},{24,8},{54,38},{56,40},{7,23}... | collective-permute-start | bytes 1179656 | tf_op jit(solution)/shard_map/far_row_0/ppermute | solution.py:239
  16.1 8.8 %collective-permute-start.1 = (bf16[384,256]{1,0:T(8,128)(2,1)S(1)}, bf16[384,256]{1,0:T(8,128)(2,1)S(1)}, u32[]{:S(2)}, u32[]{:S(2)}) collective-permute-start(bf16[384,256]{1,0:T(8,128)(2,1)S(1)} %pad_maximum_fusion.refs_2_.refs_1_.refs_0_.refs_3_), channel_id=1, source_target_pairs={{0,128},{64,192},{128,0},{192,64},{1,129},{65,193},{129,1},{193,65... | collective-permute-start | bytes 589832 | tf_op jit(solution)/shard_map/query_ta/ppermute | solution.py:253
  17.9 8.3 %collective-permute-start = (bf16[384,256]{1,0:T(8,128)(2,1)S(1)}, bf16[384,256]{1,0:T(8,128)(2,1)S(1)}, u32[]{:S(2)}, u32[]{:S(2)}) collective-permute-start(bf16[384,256]{1,0:T(8,128)(2,1)S(1)} %pad_maximum_fusion.refs_2_.refs_1_.refs_0_.refs_3_), channel_id=1, source_target_pairs={{0,64},{64,0},{128,192},{192,128},{1,65},{65,1},{129,193},{193,129... | collective-permute-start | bytes 589832 | tf_op jit(solution)/shard_map/query_ta/ppermute | solution.py:253
  18.4 13.2 %collective-permute-start.9 = (bf16[1152,256]{1,0:T(8,128)(2,1)S(1)}, bf16[1152,256]{1,0:T(8,128)(2,1)S(1)}, u32[]{:S(2)}, u32[]{:S(2)}) collective-permute-start(bf16[1152,256]{1,0:T(8,128)(2,1)S(1)} %get-tuple-element.26.refs_6_.refs_4_.refs_8_), channel_id=1, source_target_pairs={{2,4},{18,20},{34,36},{50,52},{10,12},{26,28},{42,44},{58,60},{4,2... | collective-permute-start | bytes 1769480 | tf_op jit(solution)/shard_map/kv_col_1/ppermute | solution.py:244
  24.0 3.6 %collective-permute-start.8 = (bf16[1152,256]{1,0:T(8,128)(2,1)S(1)}, bf16[1152,256]{1,0:T(8,128)(2,1)S(1)}, u32[]{:S(2)}, u32[]{:S(2)}) collective-permute-start(bf16[1152,256]{1,0:T(8,128)(2,1)S(1)} %get-tuple-element.26.refs_6_.refs_4_.refs_8_), channel_id=1, source_target_pairs={{0,2},{16,18},{32,34},{48,50},{4,6},{20,22},{36,38},{52,54},{8,10}... | collective-permute-start | bytes 1769480 | tf_op jit(solution)/shard_map/kv_col_0/ppermute | solution.py:244
  32.9 5.5 %collective-permute-start.12 = (f32[8,768]{1,0:T(8,128)S(1)}, f32[8,768]{1,0:T(8,128)S(1)}, u32[]{:S(2)}, u32[]{:S(2)}) collective-permute-start(f32[8,768]{1,0:T(8,128)S(1)} %table.1.refs_3_), channel_id=1, source_target_pairs={{0,128},{64,192},{128,0},{192,64},{1,129},{65,193},{129,1},{193,65... | collective-permute-start | bytes 73736 | tf_op jit(solution)/shard_map/stats_ta/ppermute | solution.py:253
  34.7 4.2 %collective-permute-start.11 = (f32[8,768]{1,0:T(8,128)S(1)}, f32[8,768]{1,0:T(8,128)S(1)}, u32[]{:S(2)}, u32[]{:S(2)}) collective-permute-start(f32[8,768]{1,0:T(8,128)S(1)} %table.1.refs_3_), channel_id=1, source_target_pairs={{0,192},{64,128},{128,64},{192,0},{1,193},{65,129},{129,65},{193,1... | collective-permute-start | bytes 73736 | tf_op jit(solution)/shard_map/stats_ta/ppermute | solution.py:253
  36.6 2.7 %collective-permute-start.10 = (f32[8,768]{1,0:T(8,128)S(1)}, f32[8,768]{1,0:T(8,128)S(1)}, u32[]{:S(2)}, u32[]{:S(2)}) collective-permute-start(f32[8,768]{1,0:T(8,128)S(1)} %table.1.refs_3_), channel_id=1, source_target_pairs={{0,64},{64,0},{128,192},{192,128},{1,65},{65,1},{129,193},{193,129... | collective-permute-start | bytes 73736 | tf_op jit(solution)/shard_map/stats_ta/ppermute | solution.py:253
  40.7 18.8 %collective-permute-start.16 = (bf16[1152,256]{1,0:T(8,128)(2,1)S(1)}, bf16[1152,256]{1,0:T(8,128)(2,1)S(1)}, u32[]{:S(2)}, u32[]{:S(2)}) collective-permute-start(bf16[1152,256]{1,0:T(8,128)(2,1)S(1)} %get-tuple-element.41), channel_id=1, source_target_pairs={{2,4},{18,20},{34,36},{50,52},{6,8},{22,24},{38,40},{54,56},{10,12... | collective-permute-start | bytes 1769480 | tf_op jit(solution)/shard_map/d_col_1/ppermute | solution.py:244
  48.9 10.8 %collective-permute-start.17 = (bf16[1152,256]{1,0:T(8,128)(2,1)S(1)}, bf16[1152,256]{1,0:T(8,128)(2,1)S(1)}, u32[]{:S(2)}, u32[]{:S(2)}) collective-permute-start(bf16[1152,256]{1,0:T(8,128)(2,1)S(1)} %get-tuple-element.42), channel_id=1, source_target_pairs={{0,2},{16,18},{32,34},{48,50},{4,6},{20,22},{36,38},{52,54},{8,10}... | collective-permute-start | bytes 1769480 | tf_op jit(solution)/shard_map/d_col_0/ppermute | solution.py:244
  50.8 12.6 %collective-permute-start.15 = (f32[192,256]{1,0:T(8,128)S(1)}, f32[192,256]{1,0:T(8,128)S(1)}, u32[]{:S(2)}, u32[]{:S(2)}) collective-permute-start(f32[192,256]{1,0:T(8,128)S(1)} %get-tuple-element.57), channel_id=1, source_target_pairs={{0,128},{64,192},{128,0},{192,64},{1,129},{65,193},{129,1},{193,65... | collective-permute-start | bytes 589832 | tf_op jit(solution)/shard_map/dq_ta/ppermute | solution.py:253
  52.1 11.3 %collective-permute-start.14 = (f32[192,256]{1,0:T(8,128)S(1)}, f32[192,256]{1,0:T(8,128)S(1)}, u32[]{:S(2)}, u32[]{:S(2)}) collective-permute-start(f32[192,256]{1,0:T(8,128)S(1)} %get-tuple-element.58), channel_id=1, source_target_pairs={{0,192},{64,128},{128,64},{192,0},{1,193},{65,129},{129,65},{193,1... | collective-permute-start | bytes 589832 | tf_op jit(solution)/shard_map/dq_ta/ppermute | solution.py:253
  53.1 10.3 %collective-permute-start.13 = (f32[192,256]{1,0:T(8,128)S(1)}, f32[192,256]{1,0:T(8,128)S(1)}, u32[]{:S(2)}, u32[]{:S(2)}) collective-permute-start(f32[192,256]{1,0:T(8,128)S(1)} %get-tuple-element.59), channel_id=1, source_target_pairs={{0,64},{64,0},{128,192},{192,128},{1,65},{65,1},{129,193},{193,129... | collective-permute-start | bytes 589832 | tf_op jit(solution)/shard_map/dq_ta/ppermute | solution.py:253
  59.8 5.6 %collective-permute-start.18 = (bf16[384,256]{1,0:T(8,128)(2,1)S(1)}, bf16[384,256]{1,0:T(8,128)(2,1)S(1)}, u32[]{:S(2)}, u32[]{:S(2)}) collective-permute-start(bf16[384,256]{1,0:T(8,128)(2,1)S(1)} %get-tuple-element.44), channel_id=1, source_target_pairs={{0,16},{2,18},{4,20},{6,22},{8,24},{10,26},{12,28},{14,30},{32,48}... | collective-permute-start | bytes 589832 | tf_op jit(solution)/shard_map/d_row_0/ppermute | solution.py:239
  60.2 12.6 %collective-permute-start.19 = (bf16[384,256]{1,0:T(8,128)(2,1)S(1)}, bf16[384,256]{1,0:T(8,128)(2,1)S(1)}, u32[]{:S(2)}, u32[]{:S(2)}) collective-permute-start(bf16[384,256]{1,0:T(8,128)(2,1)S(1)} %get-tuple-element.45), channel_id=1, source_target_pairs={{16,32},{18,34},{20,36},{22,38},{24,40},{26,42},{28,44},{30,46},{3... | collective-permute-start | bytes 589832 | tf_op jit(solution)/shard_map/d_row_1/ppermute | solution.py:239
